TPU v7x, 32 devices: a whole 2x2x4 slice. The times are simulated.
32 devices in a mesh: dp: 8 (over y, x, core), ctx: 4 (over z).
Axes of the slice: x: 2, y: 2, z: 4, core: 2. Of those that a mesh axis runs over, the one named last changes fastest.
Arguments:
- layer_input: bfloat16 [16384, 1152], P(('dp', 'ctx')), may hold values from -6 to 6
- cotangent: bfloat16 [16384, 1152], P(('dp', 'ctx')), may hold values from -6 to 6
- lengths: int32 [8], P('dp'), may hold values from 1537 to 2048, as said below
- weights: float32 [1152, 23296], P(('dp', 'ctx'))
- norm_gains: float32 [1152, 4], P(('dp', 'ctx')), may hold values from -0.4 to 0.4
- head_gains: float32 [256, 2], P(('dp', 'ctx')), may hold values from -0.2 to 0.2
- moment_weights: float32 [1152, 23296], P(('dp', 'ctx')), may hold values from -38.4 to 38.4
- moment_gains: float32 [1152, 4], P(('dp', 'ctx')), may hold values from -38.4 to 38.4
- moment_head: float32 [256, 2], P(('dp', 'ctx')), may hold values from -38.4 to 38.4
- square_weights: float32 [1152, 23296], P(('dp', 'ctx')), may hold values from 425.984 to 1638.4
- square_gains: float32 [1152, 4], P(('dp', 'ctx')), may hold values from 425.984 to 1638.4
- square_head: float32 [256, 2], P(('dp', 'ctx')), may hold values from 13107.2 to 52428.8
Outputs:
- output: bfloat16 [16384, 1152], P(('dp', 'ctx'))
- grad_input: bfloat16 [16384, 1152], P(('dp', 'ctx'))
- new_weights: float32 [1152, 23296], P(('dp', 'ctx'))
- new_gains: float32 [1152, 4], P(('dp', 'ctx'))
- new_head_gains: float32 [256, 2], P(('dp', 'ctx'))
- first_weights: float32 [1152, 23296], P(('dp', 'ctx'))
- first_gains: float32 [1152, 4], P(('dp', 'ctx'))
- first_head: float32 [256, 2], P(('dp', 'ctx'))
- second_weights: float32 [1152, 23296], P(('dp', 'ctx'))
- second_gains: float32 [1152, 4], P(('dp', 'ctx'))
- second_head: float32 [256, 2], P(('dp', 'ctx'))
- weights_bf16: bfloat16 [1152, 23296], P(('dp', 'ctx'))
Inputs may be any that keep to these rules, and one draw needn't show every extreme that they name: `lengths`: each sequence has at least 1537 valid tokens; in every draw some sequence is full.
All inputs are finite; a program needn't handle non-finite values.
Results may differ from a plain program's by a relative error of at most 0.019.
Values may be sent and summed in bfloat16 or wider, within the bound.
No kernel may reach another device: no remote copies, remote signals or barrier semaphores. Data moves between devices by JAX's collectives and lax.ppermute only.
A program may use at most 448 MiB of HBM per device.

v0:
```python
import jax
import jax.numpy as jnp
from jax import lax
from jax.sharding import PartitionSpec as P

H = 4
HD = 256
FF = 6912
STEP = 10


NORM_EPS = 1e-06
ROPE_BASE = 1000000.0
QUERY_SCALE = 0.0625
BETA_ONE = 0.9
BETA_TWO = 0.95
ADAM_EPS = 1e-08
RATE_WEIGHTS = 0.03
RATE_GAINS = 0.1
WEIGHT_DECAY = 0.1
NEG_LARGE = -1e30


def block_positions(slots, rows, count):
    half_rows = rows // 2
    device = slots // rows
    within = slots % rows
    block = jnp.where(within < half_rows, device, 2 * count - 1 - device)
    return block * half_rows + within % half_rows


def rms_gain(values, gain):
    return values * lax.rsqrt(jnp.mean(values * values, axis=-1, keepdims=True) + NORM_EPS) * gain


def rotate(values, positions):
    half_dim = values.shape[-1] // 2
    freqs = jnp.power(ROPE_BASE, -2.0 * jnp.arange(half_dim).astype(jnp.float32) / values.shape[-1])
    angles = positions.astype(jnp.float32)[:, None] * freqs[None, :]
    cosine = jnp.cos(angles)[:, None, :]
    sine = jnp.sin(angles)[:, None, :]
    first = values[..., :half_dim]
    second = values[..., half_dim:]
    return jnp.concatenate(
        [first * cosine - second * sine, second * cosine + first * sine], axis=-1
    )


def geglu(gate_up):
    return jax.nn.gelu(gate_up[:, :FF], approximate=True) * gate_up[:, FF:]


def offsets():
    q_cols = H * HD
    start_gate = q_cols + 2 * HD
    start_out = start_gate + 2 * FF
    start_down = start_out + q_cols
    return (q_cols, start_gate, start_out, start_down)


def adamw(weight, grad, first, second, rate, decay):
    first_new = BETA_ONE * first + (1.0 - BETA_ONE) * grad
    second_new = BETA_TWO * second + (1.0 - BETA_TWO) * grad * grad
    update = (
        first_new
        / (1.0 - BETA_ONE**STEP)
        / (jnp.sqrt(second_new / (1.0 - BETA_TWO**STEP)) + ADAM_EPS)
    )
    return (weight - rate * (update + decay * weight), first_new, second_new)


def body(
    layer_input,
    cotangent,
    lengths,
    weights,
    norm_gains,
    head_gains,
    moment_weights,
    moment_gains,
    moment_head,
    square_weights,
    square_gains,
    square_head,
):
    q_cols, start_gate, start_out, start_down = offsets()
    full_w, full_g, full_h = (
        lax.all_gather(weights.astype(jnp.bfloat16), ("dp", "ctx"), axis=0, tiled=True),
        lax.all_gather(norm_gains.astype(jnp.bfloat16), ("dp", "ctx"), axis=0, tiled=True),
        lax.all_gather(head_gains.astype(jnp.bfloat16), ("dp", "ctx"), axis=0, tiled=True),
    )
    gain_f = 1.0 + full_g.astype(jnp.float32)
    head_f = 1.0 + full_h.astype(jnp.float32)
    tok_rows = layer_input.shape[0]
    ctx_count = lax.axis_size("ctx")
    local_slots = lax.axis_index("ctx") * tok_rows + jnp.arange(tok_rows, dtype=jnp.int32)
    positions = block_positions(local_slots, tok_rows, ctx_count)
    seq_length = lengths[0]
    row_valid = positions < seq_length
    inputs = layer_input.astype(jnp.float32)
    normed_in, pull_in = jax.vjp(rms_gain, inputs, gain_f[:, 0])
    normed_low = normed_in.astype(jnp.bfloat16)
    w_qkv = full_w[:, :start_gate]
    projected = jnp.dot(normed_low, w_qkv, preferred_element_type=jnp.float32)

    def query_key(query_raw, key_raw, head_arg):
        query_out = (
            rotate(rms_gain(query_raw.reshape(tok_rows, H, HD), head_arg[:, 0]), positions)
            * QUERY_SCALE
        )
        key_out = rotate(rms_gain(key_raw[:, None, :], head_arg[:, 1]), positions)[:, 0]
        return (query_out, key_out)

    (queries, keys), pull_qk = jax.vjp(
        query_key, projected[:, :q_cols], projected[:, q_cols : q_cols + HD], head_f
    )
    query_low = queries.astype(jnp.bfloat16)
    key_low = keys.astype(jnp.bfloat16)
    value_low = projected[:, q_cols + HD :].astype(jnp.bfloat16)
    all_keys, all_values = (
        lax.all_gather(key_low, "ctx", axis=0, tiled=True),
        lax.all_gather(value_low, "ctx", axis=0, tiled=True),
    )
    key_pos = block_positions(jnp.arange(all_keys.shape[0], dtype=jnp.int32), tok_rows, ctx_count)
    allowed = (key_pos[None, :] <= positions[:, None]) & (key_pos < seq_length)[None, :]
    scores = jnp.einsum("thd,sd->hts", query_low, all_keys, preferred_element_type=jnp.float32)
    scores = jnp.where(allowed[None], scores, NEG_LARGE)
    row_max = jnp.max(scores, axis=-1, keepdims=True)
    expon = jnp.exp(scores - row_max)
    row_total = jnp.sum(expon, axis=-1, keepdims=True)
    probs_low = (expon / row_total).astype(jnp.bfloat16)
    log_total = (row_max + jnp.log(row_total))[..., 0]
    mixed = jnp.einsum("hts,sd->thd", probs_low, all_values, preferred_element_type=jnp.float32)
    mixed_low = mixed.reshape(tok_rows, q_cols).astype(jnp.bfloat16)
    w_out = full_w[:, start_out:start_down]
    attn_proj = jnp.einsum("tc,dc->td", mixed_low, w_out, preferred_element_type=jnp.float32)
    post_attn, pull_attn = jax.vjp(rms_gain, attn_proj, gain_f[:, 1])
    residual_mid = inputs + post_attn
    normed_mid, pull_mid = jax.vjp(rms_gain, residual_mid, gain_f[:, 2])
    mid_low = normed_mid.astype(jnp.bfloat16)
    w_gate_up = full_w[:, start_gate:start_out]
    gate_up = jnp.dot(mid_low, w_gate_up, preferred_element_type=jnp.float32)
    hidden, pull_hidden = jax.vjp(geglu, gate_up)
    hidden_low = hidden.astype(jnp.bfloat16)
    w_down = full_w[:, start_down:]
    mlp_proj = jnp.einsum("tf,df->td", hidden_low, w_down, preferred_element_type=jnp.float32)
    post_mlp, pull_mlp = jax.vjp(rms_gain, mlp_proj, gain_f[:, 3])
    output = (residual_mid + post_mlp).astype(jnp.bfloat16)
    out_grad = cotangent.astype(jnp.float32) * row_valid[:, None].astype(jnp.float32)
    mlp_grad, grad_three = pull_mlp(out_grad)
    mlp_grad_low = mlp_grad.astype(jnp.bfloat16)
    grad_down = jnp.einsum(
        "td,tf->df", mlp_grad_low, hidden_low, preferred_element_type=jnp.float32
    )
    hidden_grad = jnp.dot(mlp_grad_low, w_down, preferred_element_type=jnp.float32)
    (gate_up_grad,) = pull_hidden(hidden_grad)
    gate_up_low = gate_up_grad.astype(jnp.bfloat16)
    grad_gate_up = jnp.einsum("td,tc->dc", mid_low, gate_up_low, preferred_element_type=jnp.float32)
    mid_grad = jnp.einsum("tc,dc->td", gate_up_low, w_gate_up, preferred_element_type=jnp.float32)
    resid_part, grad_two = pull_mid(mid_grad)
    residual_grad = out_grad + resid_part
    attn_grad, grad_one = pull_attn(residual_grad)
    attn_low = attn_grad.astype(jnp.bfloat16)
    grad_out = jnp.einsum("td,tc->dc", attn_low, mixed_low, preferred_element_type=jnp.float32)
    mixed_grad = jnp.dot(attn_low, w_out, preferred_element_type=jnp.float32).astype(jnp.bfloat16)
    query_heads = query_low.transpose(1, 0, 2)
    grad_heads = mixed_grad.reshape(tok_rows, H, HD).transpose(1, 0, 2)

    def head_back(head_in):
        query_one, grad_one_head, total_one = head_in
        head_scores = jnp.einsum(
            "td,sd->ts", query_one, all_keys, preferred_element_type=jnp.float32
        )
        head_scores = jnp.where(allowed, head_scores, NEG_LARGE)
        head_probs = jnp.exp(head_scores - total_one[:, None])
        prob_grad = jnp.einsum(
            "td,sd->ts", grad_one_head, all_values, preferred_element_type=jnp.float32
        )
        delta_row = jnp.sum(head_probs * prob_grad, axis=-1, keepdims=True)
        score_low = (head_probs * (prob_grad - delta_row)).astype(jnp.bfloat16)
        query_grad = jnp.dot(score_low, all_keys, preferred_element_type=jnp.float32)
        key_part = jnp.einsum("ts,td->sd", score_low, query_one, preferred_element_type=jnp.float32)
        value_part = jnp.einsum(
            "ts,td->sd",
            head_probs.astype(jnp.bfloat16),
            grad_one_head,
            preferred_element_type=jnp.float32,
        )
        return (query_grad, key_part, value_part)

    query_grads, key_parts, value_parts = lax.map(head_back, (query_heads, grad_heads, log_total))
    key_grad, value_grad = (
        lax.psum_scatter(
            jnp.sum(key_parts, axis=0).astype(jnp.bfloat16), "ctx", scatter_dimension=0, tiled=True
        ).astype(jnp.float32),
        lax.psum_scatter(
            jnp.sum(value_parts, axis=0).astype(jnp.bfloat16),
            "ctx",
            scatter_dimension=0,
            tiled=True,
        ).astype(jnp.float32),
    )
    raw_query, raw_key, grad_head = pull_qk((query_grads.transpose(1, 0, 2), key_grad))
    proj_low = jnp.concatenate([raw_query, raw_key, value_grad], axis=1).astype(jnp.bfloat16)
    grad_qkv = jnp.einsum("td,tc->dc", normed_low, proj_low, preferred_element_type=jnp.float32)
    in_part = jnp.einsum("tc,dc->td", proj_low, w_qkv, preferred_element_type=jnp.float32)
    input_part, grad_zero = pull_in(in_part)
    grad_input = (residual_grad + input_part).astype(jnp.bfloat16)
    sum_qkv, sum_gate_up, sum_out, sum_down, sum_gains, sum_head = (
        lax.psum_scatter(grad_qkv, ("dp", "ctx"), scatter_dimension=0, tiled=True),
        lax.psum_scatter(grad_gate_up, ("dp", "ctx"), scatter_dimension=0, tiled=True),
        lax.psum_scatter(grad_out, ("dp", "ctx"), scatter_dimension=0, tiled=True),
        lax.psum_scatter(grad_down, ("dp", "ctx"), scatter_dimension=0, tiled=True),
        lax.psum_scatter(
            jnp.stack([grad_zero, grad_one, grad_two, grad_three], axis=1),
            ("dp", "ctx"),
            scatter_dimension=0,
            tiled=True,
        ),
        lax.psum_scatter(grad_head, ("dp", "ctx"), scatter_dimension=0, tiled=True),
    )
    sum_weights = jnp.concatenate([sum_qkv, sum_gate_up, sum_out, sum_down], axis=1)
    new_w, first_w, second_w = adamw(
        weights, sum_weights, moment_weights, square_weights, RATE_WEIGHTS, WEIGHT_DECAY
    )
    new_g, first_g, second_g = adamw(
        norm_gains, sum_gains, moment_gains, square_gains, RATE_GAINS, 0.0
    )
    new_h, first_h, second_h = adamw(
        head_gains, sum_head, moment_head, square_head, RATE_GAINS, 0.0
    )
    return (
        output,
        grad_input,
        new_w,
        new_g,
        new_h,
        first_w,
        first_g,
        first_h,
        second_w,
        second_g,
        second_h,
        new_w.astype(jnp.bfloat16),
    )


def solution(mesh):
    in_specs = (
        P(("dp", "ctx"), None),
        P(("dp", "ctx"), None),
        P("dp"),
        P(("dp", "ctx"), None),
        P(("dp", "ctx"), None),
        P(("dp", "ctx"), None),
        P(("dp", "ctx"), None),
        P(("dp", "ctx"), None),
        P(("dp", "ctx"), None),
        P(("dp", "ctx"), None),
        P(("dp", "ctx"), None),
        P(("dp", "ctx"), None),
    )
    out_specs = (
        P(("dp", "ctx"), None),
        P(("dp", "ctx"), None),
        P(("dp", "ctx"), None),
        P(("dp", "ctx"), None),
        P(("dp", "ctx"), None),
        P(("dp", "ctx"), None),
        P(("dp", "ctx"), None),
        P(("dp", "ctx"), None),
        P(("dp", "ctx"), None),
        P(("dp", "ctx"), None),
        P(("dp", "ctx"), None),
        P(("dp", "ctx"), None),
    )
    return jax.shard_map(body, mesh=mesh, in_specs=in_specs, out_specs=out_specs, check_vma=False)
```

profile of v0, /device:TPU:0, one launch (start us, length us, event | category | flops | bytes accessed | tf_op | source)
XLA Modules:
  0.0 4195.0 jit_solution(12638009151412296921)
XLA Ops:
  7.2 3.5 convert_bitcast_fusion
  10.9 71.1 %all-gather.1 = bf16[32,36,4]{1,2,0:T(4,128)(2,1)S(1)} all-gather(bf16[1,36,4]{1,2,0:T(4,128)(2,1)S(1)} %convert_bitcast_fusion.1), channel_id=1, replica_groups=mesh['dp'=8,'ctx'=4] {'dp','ctx'}, dimensions={0}, use_global_device_ids=true | all-gather | bytes 9504 | tf_op jit(solution)/shard_map/all_gather | solution.py:89
  82.1 64.1 %all-gather.3 = bf16[32,8,2]{1,2,0:T(2,128)(2,1)S(1)} all-gather(bf16[1,8,2]{1,2,0:T(2,128)(2,1)S(1)} %convert_bitcast_fusion.2), channel_id=1, replica_groups=mesh['dp'=8,'ctx'=4] {'dp','ctx'}, dimensions={0}, use_global_device_ids=true | all-gather | bytes 1056 | tf_op jit(solution)/shard_map/all_gather | solution.py:90
  148.8 186.2 %all-gather.12.cloned.1.call-done = bf16[32,36,23296]{2,1,0:T(8,128)(2,1)} async-done(((bf16[1,36,23296]{2,1,0:T(8,128)(2,1)}), bf16[32,36,23296]{2,1,0:T(8,128)(2,1)}) %all-gather.12.cloned.1.call-update) | async-done | bytes 53674000 | tf_op jit(solution)/shard_map/all_gather | solution.py:88
  335.0 42.9 %reshape.437 = bf16[1152,23296]{1,0:T(8,128)(2,1)} reshape(bf16[32,36,23296]{2,1,0:T(8,128)(2,1)} %all-gather.12.cloned.1.call-done) | data formatting | bytes 107347968
  377.9 4.3 fusion.44
  387.9 2.5 compare_and_fusion
  392.2 2.2 slice.151
  396.3 2.9 multiply_reduce_fusion.11
  406.1 6.1 all-gather.10.cloned.1.call-done
  412.2 10.1 fusion.27
  422.2 8.8 fusion.38
  431.6 9.6 all-gather.8.cloned.1.call-done
  441.2 9.0 fusion.67
  450.3 3.8 multiply_reduce_fusion.9
  456.0 28.3 fusion.25
  484.3 10.8 multiply_convert_fusion.1
  495.1 18.3 multiply_reduce_fusion.7
  513.5 2.5 multiply_reduce_fusion.1
  516.6 34.5 fusion.40
  551.1 28.9 multiply_reduce_fusion.2
  580.0 33.6 fusion.65
  613.6 1797.0 %fusion.3 = f32[48,13824]{1,0:T(8,128)} fusion(f32[1152,13824]{1,0:T(8,128)} %fusion.65), kind=kCustom, calls=%all-reduce-scatter.1 | all-reduce-scatter fusion | flops 21233664 | bytes 66355200
  2410.6 3.3 slice.97
  2413.9 2.8 collective-permute-start.10
  2416.7 3.1 collective-permute-start.4
  2419.9 3.6 multiply_reduce_fusion.3
  2424.9 3.7 fusion.68
  2428.7 37.5 while.15
  2432.4 2.1 fusion.175
  2434.5 2.1 fusion.176
  2453.2 2.1 fusion.176
  2469.7 5.3 reduce_sum.217
  2475.1 5.4 reduce_sum.220
  2480.5 18.1 fusion.129
  2498.7 2.9 multiply_reduce_fusion.10
  2505.3 5.2 fusion.139
  2510.5 33.1 reduce-scatter.13.cloned.1.call-done
  2551.5 22.7 reduce-scatter.15.cloned.1.call-done
  2576.0 6.5 fusion.74
  2582.5 1031.7 %fusion.132 = (f32[40,6912]{1,0:T(8,128)}, f32[40,1024]{1,0:T(8,128)}, f32[40,1536]{1,0:T(8,128)}) fusion(f32[1152,6912]{1,0:T(8,128)} %fusion.129, f32[1152,1024]{1,0:T(8,128)} %fusion.139, f32[1152,1536]{1,0:T(8,128)} %fusion.74), kind=kCustom, calls=%all-reduce-scatter.4 | all-reduce-scatter fusion | flops 12124161 | bytes 45162496
  3618.4 4.0 collective-permute-start.12
  3622.4 2.1 collective-permute-start.13
  3624.6 4.0 collective-permute-start.14
  3628.5 3.2 collective-permute-start
  3631.7 5.1 collective-permute-start.1
  3636.8 7.6 collective-permute-start.2
  3644.5 13.6 collective-permute-start.5
  3658.1 91.6 %collective-permute-start.6 = (f32[48,13824]{1,0:T(8,128)}, f32[48,13824]{1,0:T(8,128)}, u32[]{:S(2)}, u32[]{:S(2)}) collective-permute-start(f32[48,13824]{1,0:T(8,128)} %fusion.3), channel_id=1, source_target_pairs={{0,3},{1,4},{2,5},{3,6},{4,7},{5,8},{6,9},{7,10},{8,11},{9,12},{10... | collective-permute-start | bytes 7962632
  3749.7 2.8 collective-permute-start.7
  3752.5 2.8 collective-permute-start.8
  3755.4 2.8 collective-permute-start.9
  3758.1 7.1 fusion.49
  3767.4 252.7 %all-reduce.18 = (f32[1152,4]{0,1:T(4,128)}, f32[256,2]{0,1:T(2,128)}) all-reduce(f32[1152,4]{0,1:T(4,128)} %pad_maximum_fusion.5, f32[256,2]{0,1:T(2,128)S(1)} %pad_add_fusion.2), channel_id=9, replica_groups=mesh['dp'=8,'ctx'=4] {'dp','ctx'}, use_global_device_ids=true, to_apply=%region_29.30.clone | all-reduce | flops 5120 | bytes 40960
  4023.6 3.3 fusion.54
  4026.9 8.0 concatenate.20
  4035.9 8.2 concatenate.18
  4045.9 2.8 collective-permute-start.16
  4048.6 5.0 collective-permute-start.17
  4053.6 2.3 collective-permute-start.18
  4055.9 3.6 collective-permute-start.19
  4059.6 93.5 %concatenate.19 = f32[420,13824]{1,0:T(8,128)} concatenate(f32[36,13824]{1,0:T(8,128)S(1)} %copy-done.26, f32[48,13824]{1,0:T(8,128)} %collective-permute-done.10, f32[48,13824]{1,0:T(8,128)} %collective-permute-done.9, f32[48,13824]{1,0:T(8,128)} %collective-permute-done.8, f32[48,13824]{1,0:T(8,128)} %collective-permute-done.7, f32[48,13824]{1,0:T(8,128)} %collective-permute-done.6, ...), dimensions={0} | concatenate | bytes 46448640
  4155.0 23.1 concatenate.21
  4179.6 8.6 fusion.133
  (294 shorter events, 86.7 us)
Async XLA Ops:
  7.2 74.9 %copy-start.77 = (f32[8,2]{0,1:T(2,128)S(1)}, f32[8,2]{0,1:T(2,128)}, u32[]{:S(2)}) copy-start(f32[8,2]{0,1:T(2,128)} %param.19) | copy-start | bytes 196
  7.2 327.8 %all-gather.12.cloned.1.call-start = ((), (), s32[]{:S(2)}) async-start(), calls=%async_computation.6 | async-start | bytes 61501440 | tf_op jit(solution)/shard_map/all_gather | solution.py:88
  10.7 137.1 %copy-start.11 = (bf16[512,1152]{1,0:T(8,128)(2,1)S(1)}, bf16[512,1152]{1,0:T(8,128)(2,1)}, u32[]{:S(2)}) copy-start(bf16[512,1152]{1,0:T(8,128)(2,1)} %param.14) | copy-start | bytes 3538948
  10.8 401.4 %all-gather.10.cloned.1.call-start = ((), (), s32[]{:S(2)}) async-start(), calls=%async_computation.5 | async-start | bytes 1310720 | tf_op jit(solution)/shard_map/all_gather | solution.py:121
  147.2 238.9 %copy-start.72 = (f32[128]{0:T(128)}, f32[128]{0:T(128)S(1)}, u32[]{:S(2)}) copy-start(f32[128]{0:T(128)S(1)} %multiply_power_fusion) | copy-start | bytes 1540
  147.2 238.9 %copy-start.46 = (f32[512]{0:T(512)}, f32[512]{0:T(512)S(1)}, u32[]{:S(2)}) copy-start(f32[512]{0:T(512)S(1)} %fusion.121) | copy-start | bytes 6148
  147.9 230.0 %copy-start.51 = (f32[1152]{0:T(1024)}, f32[1152]{0:T(1024)S(1)}, u32[]{:S(2)}) copy-start(f32[1152]{0:T(1024)S(1)} %get-tuple-element.113) | copy-start | bytes 13828
  148.2 229.7 %copy-start.57 = (f32[512]{0:T(512)}, f32[512]{0:T(512)S(1)}, u32[]{:S(2)}) copy-start(f32[512]{0:T(512)S(1)} %fusion.55) | copy-start | bytes 6148
  148.2 229.7 %copy-start.70 = (f32[512]{0:T(512)}, f32[512]{0:T(512)S(1)}, u32[]{:S(2)}) copy-start(f32[512]{0:T(512)S(1)} %fusion.115) | copy-start | bytes 6148
  148.8 233.6 %copy-start.62 = (f32[256,1]{0,1:T(1,128)}, f32[256,1]{0,1:T(1,128)S(1)}, u32[]{:S(2)}) copy-start(f32[256,1]{0,1:T(1,128)S(1)} %get-tuple-element.175) | copy-start | bytes 3076
  385.9 55.3 %all-gather.8.cloned.1.call-start = ((), (), s32[]{:S(2)}) async-start(), calls=%async_computation.2 | async-start | bytes 1310720 | tf_op jit(solution)/shard_map/all_gather | solution.py:122
  387.9 15.8 copy-start.21
  392.2 10.4 copy-start
  402.2 2141.4 %reduce-scatter.13.cloned.1.call-start = ((), (), s32[]{:S(2)}) async-start(), calls=%async_computation.3 | async-start | bytes 1310720 | tf_op jit(solution)/shard_map/reduce_scatter | solution.py:193
  495.1 18.4 copy-start.2
  495.1 18.4 copy-start.9
  495.1 18.4 copy-start.31
  2410.6 9.2 copy-start.6
  2410.6 9.3 copy-start.38
  2410.6 9.3 copy-start.45
  2413.9 1338.7 %collective-permute-start.10 = (f32[48,13824]{1,0:T(8,128)}, f32[48,13824]{1,0:T(8,128)}, u32[]{:S(2)}, u32[]{:S(2)}) collective-permute-start(f32[48,13824]{1,0:T(8,128)} %fusion.3), channel_id=1, source_target_pairs={{0,7},{1,8},{2,9},{3,10},{4,11},{5,12},{6,13},{7,14},{8,15},{9,16}... | collective-permute-start | bytes 7962632
  2416.7 1338.7 %collective-permute-start.4 = (f32[48,13824]{1,0:T(8,128)}, f32[48,13824]{1,0:T(8,128)}, u32[]{:S(2)}, u32[]{:S(2)}) collective-permute-start(f32[48,13824]{1,0:T(8,128)} %fusion.3), channel_id=1, source_target_pairs={{0,1},{1,2},{2,3},{3,4},{4,5},{5,6},{6,7},{7,8},{8,9},{9,10},{10,1... | collective-permute-start | bytes 7962632
  2475.0 99.2 %reduce-scatter.15.cloned.1.call-start = ((), (), s32[]{:S(2)}) async-start(), calls=%async_computation.4 | async-start | bytes 1310720 | tf_op jit(solution)/shard_map/reduce_scatter | solution.py:196
  2480.5 18.2 copy-start.1
  2480.5 18.2 copy-start.36
  2480.5 18.2 copy-start.65
  2503.7 40.9 copy-start.47
  2503.7 40.9 copy-start.73
  2503.7 42.1 %copy-start.49 = (f32[512]{0:T(512)S(1)}, f32[512]{0:T(512)}, u32[]{:S(2)}) copy-start(f32[512]{0:T(512)} %copy-done.48) | copy-start | bytes 6148
  2503.7 42.1 %copy-start.63 = (f32[256,1]{0,1:T(1,128)S(1)}, f32[256,1]{0,1:T(1,128)}, u32[]{:S(2)}) copy-start(f32[256,1]{0,1:T(1,128)} %copy-done.62) | copy-start | bytes 3076
  2503.7 1114.6 %collective-permute-start.11 = (f32[36,13824]{1,0:T(8,128)}, f32[36,13824]{1,0:T(8,128)S(1)}, u32[]{:S(2)}, u32[]{:S(2)}) collective-permute-start(f32[36,13824]{1,0:T(8,128)} %slice.97), channel_id=1, source_target_pairs={{0,8},{1,9},{2,10},{3,11},{4,12},{5,13},{6,14},{7,15},{8,16},{9,17... | collective-permute-start | bytes 5971976
  2510.5 37.2 copy-start.60
  2544.6 31.4 copy-start.12
  2544.6 31.4 copy-start.52
  2544.7 31.4 copy-start.71
  2582.5 1061.9 %copy-start.53 = (f32[1152]{0:T(1024)S(1)}, f32[1152]{0:T(1024)}, u32[]{:S(2)}) copy-start(f32[1152]{0:T(1024)} %get-tuple-element.98) | copy-start | bytes 13828
  2582.5 1061.9 %copy-start.68 = (f32[1152]{0:T(1024)S(1)}, f32[1152]{0:T(1024)}, u32[]{:S(2)}) copy-start(f32[1152]{0:T(1024)} %get-tuple-element.100) | copy-start | bytes 13828
  2582.5 1061.9 %copy-start.50 = (f32[1152]{0:T(1024)S(1)}, f32[1152]{0:T(1024)}, u32[]{:S(2)}) copy-start(f32[1152]{0:T(1024)} %get-tuple-element.106) | copy-start | bytes 13828
  3615.0 9.5 collective-permute-start.3
  3617.1 5.3 collective-permute-start.15
  3618.4 26.1 copy-start.25
  3618.4 10.2 collective-permute-start.12
  3622.4 22.0 copy-start.61
  3622.4 9.3 collective-permute-start.13
  3624.5 19.9 copy-start.54
  3624.6 12.3 collective-permute-start.14
  3628.5 16.0 collective-permute-start
  3631.7 26.4 collective-permute-start.1
  3636.8 112.9 %collective-permute-start.2 = (f32[40,1536]{1,0:T(8,128)}, f32[40,1536]{1,0:T(8,128)}, u32[]{:S(2)}, u32[]{:S(2)}) collective-permute-start(f32[40,1536]{1,0:T(8,128)} %get-tuple-element.145), channel_id=1, source_target_pairs={{0,3},{1,4},{2,5},{3,6},{4,7},{5,8},{6,9},{7,10},{8,11},{9,12},{10... | collective-permute-start | bytes 737288
  3644.5 122.3 %copy-start.74 = (f32[256]{0:T(256)S(1)}, f32[256]{0:T(256)}, u32[]{:S(2)}) copy-start(f32[256]{0:T(256)} %get-tuple-element.104) | copy-start | bytes 3076
  3644.5 122.3 %copy-start.75 = (f32[256]{0:T(256)S(1)}, f32[256]{0:T(256)}, u32[]{:S(2)}) copy-start(f32[256]{0:T(256)} %get-tuple-element.102) | copy-start | bytes 3076
  3644.5 375.6 %copy-start.58 = (f32[512]{0:T(512)S(1)}, f32[512]{0:T(512)}, u32[]{:S(2)}) copy-start(f32[512]{0:T(512)} %copy-done.57) | copy-start | bytes 6148
  3644.5 379.1 %copy-start.8 = (f32[512,1152]{1,0:T(8,128)S(1)}, f32[512,1152]{1,0:T(8,128)}, u32[]{:S(2)}) copy-start(f32[512,1152]{1,0:T(8,128)} %copy-done.7) | copy-start | bytes 7077892
  3644.5 401.3 %collective-permute-start.5 = (f32[48,13824]{1,0:T(8,128)}, f32[48,13824]{1,0:T(8,128)}, u32[]{:S(2)}, u32[]{:S(2)}) collective-permute-start(f32[48,13824]{1,0:T(8,128)} %fusion.3), channel_id=1, source_target_pairs={{0,2},{1,3},{2,4},{3,5},{4,6},{5,7},{6,8},{7,9},{8,10},{9,11},{10,... | collective-permute-start | bytes 7962632
  3658.1 390.5 %collective-permute-start.6 = (f32[48,13824]{1,0:T(8,128)}, f32[48,13824]{1,0:T(8,128)}, u32[]{:S(2)}, u32[]{:S(2)}) collective-permute-start(f32[48,13824]{1,0:T(8,128)} %fusion.3), channel_id=1, source_target_pairs={{0,3},{1,4},{2,5},{3,6},{4,7},{5,8},{6,9},{7,10},{8,11},{9,12},{10... | collective-permute-start | bytes 7962632
  3749.7 303.9 %collective-permute-start.7 = (f32[48,13824]{1,0:T(8,128)}, f32[48,13824]{1,0:T(8,128)}, u32[]{:S(2)}, u32[]{:S(2)}) collective-permute-start(f32[48,13824]{1,0:T(8,128)} %fusion.3), channel_id=1, source_target_pairs={{0,4},{1,5},{2,6},{3,7},{4,8},{5,9},{6,10},{7,11},{8,12},{9,13},{1... | collective-permute-start | bytes 7962632
  3752.5 303.4 %collective-permute-start.8 = (f32[48,13824]{1,0:T(8,128)}, f32[48,13824]{1,0:T(8,128)}, u32[]{:S(2)}, u32[]{:S(2)}) collective-permute-start(f32[48,13824]{1,0:T(8,128)} %fusion.3), channel_id=1, source_target_pairs={{0,5},{1,6},{2,7},{3,8},{4,9},{5,10},{6,11},{7,12},{8,13},{9,14},{... | collective-permute-start | bytes 7962632
  3755.4 304.2 %collective-permute-start.9 = (f32[48,13824]{1,0:T(8,128)}, f32[48,13824]{1,0:T(8,128)}, u32[]{:S(2)}, u32[]{:S(2)}) collective-permute-start(f32[48,13824]{1,0:T(8,128)} %fusion.3), channel_id=1, source_target_pairs={{0,6},{1,7},{2,8},{3,9},{4,10},{5,11},{6,12},{7,13},{8,14},{9,15},... | collective-permute-start | bytes 7962632
  4026.9 18.9 copy-start.18
  4026.9 32.6 copy-start.26
  4045.9 109.1 %collective-permute-start.16 = (f32[40,6912]{1,0:T(8,128)S(1)}, f32[40,6912]{1,0:T(8,128)}, u32[]{:S(2)}, u32[]{:S(2)}) collective-permute-start(f32[40,6912]{1,0:T(8,128)S(1)} %copy-done.18), channel_id=1, source_target_pairs={{0,1},{1,2},{2,3},{3,4},{4,5},{5,6},{6,7},{7,8},{8,9},{9,10},{10,1... | collective-permute-start | bytes 3317768
  4048.6 106.4 %collective-permute-start.17 = (f32[40,6912]{1,0:T(8,128)S(1)}, f32[40,6912]{1,0:T(8,128)}, u32[]{:S(2)}, u32[]{:S(2)}) collective-permute-start(f32[40,6912]{1,0:T(8,128)S(1)} %copy-done.18), channel_id=1, source_target_pairs={{0,2},{1,3},{2,4},{3,5},{4,6},{5,7},{6,8},{7,9},{8,10},{9,11},{10,... | collective-permute-start | bytes 3317768
  4053.6 101.4 %collective-permute-start.18 = (f32[40,6912]{1,0:T(8,128)S(1)}, f32[40,6912]{1,0:T(8,128)}, u32[]{:S(2)}, u32[]{:S(2)}) collective-permute-start(f32[40,6912]{1,0:T(8,128)S(1)} %copy-done.18), channel_id=1, source_target_pairs={{0,3},{1,4},{2,5},{3,6},{4,7},{5,8},{6,9},{7,10},{8,11},{9,12},{10... | collective-permute-start | bytes 3317768
  4055.9 99.0 %collective-permute-start.19 = (f32[4,6912]{1,0:T(4,128)}, f32[4,6912]{1,0:T(4,128)}, u32[]{:S(2)}, u32[]{:S(2)}) collective-permute-start(f32[4,6912]{1,0:T(4,128)} %slice.99), channel_id=1, source_target_pairs={{0,4},{1,5},{2,6},{3,7},{4,8},{5,9},{6,10},{7,11},{8,12},{9,13},{1... | collective-permute-start | bytes 331784
  (43 other events, 148.0 us)
Sparse Core Ops, SparseCore 0:
  11.5 323.4 all-gather.11
  386.0 26.0 all-gather.9
  413.8 27.4 all-gather.7
  2475.1 68.4 reduce-scatter.12
  2546.4 27.7 reduce-scatter.14
where the time goes:
time: 4210 us; the launch traced here: 4190 us
  blocking collectives  3220 us (76%)
  waiting for transfers between devices  258 us (6%)
  matrix products  244 us (6%)
  local copies, waits for them, and re-layouts  210 us (5%)
  starting transfers between devices  164 us (4%)
  other arithmetic  86.7 us (2%)
    unnamed x3, blocking collectives  3080 us
    unnamed x169, local copies, waits for them, and re-layouts  193 us
    all_gather x1, waiting for transfers between devices, body(): lax.all_gather(weights.astype(jnp.bfloat16), ('dp', 'ctx'), axis=0, tiled...  186 us
    unnamed x20, starting transfers between devices  163 us
  transfers between devices with their start and end apart: 25, of which 5 were waited for; matrix products, arithmetic and copies ran while one was open for 31% of the time, Pallas kernels for 0%

commit v1 on v0

v1 whole, which is shorter than its diff:
```python
import numpy as np
import jax
import jax.numpy as jnp
from jax import lax
from jax.sharding import Mesh, PartitionSpec as P

H = 4
HD = 256
FF = 6912
STEP = 10


NORM_EPS = 1e-06
ROPE_BASE = 1000000.0
QUERY_SCALE = 0.0625
BETA_ONE = 0.9
BETA_TWO = 0.95
ADAM_EPS = 1e-08
RATE_WEIGHTS = 0.03
RATE_GAINS = 0.1
WEIGHT_DECAY = 0.1
NEG_LARGE = -1e30

LANES = 128
GROUP = 4
QUARTER = -(-FF // (GROUP * LANES)) * LANES
Q_COLS = H * HD
START_GATE = Q_COLS + 2 * HD
START_OUT = START_GATE + 2 * FF
START_DOWN = START_OUT + Q_COLS
BF = jnp.bfloat16
F32 = jnp.float32


def block_positions(slots, rows, count):
    half_rows = rows // 2
    device = slots // rows
    within = slots % rows
    block = jnp.where(within < half_rows, device, 2 * count - 1 - device)
    return block * half_rows + within % half_rows


def rms_gain(values, gain):
    return values * lax.rsqrt(jnp.mean(values * values, axis=-1, keepdims=True) + NORM_EPS) * gain


def rotate(values, positions):
    half_dim = values.shape[-1] // 2
    freqs = jnp.power(ROPE_BASE, -2.0 * jnp.arange(half_dim).astype(jnp.float32) / values.shape[-1])
    angles = positions.astype(jnp.float32)[:, None] * freqs[None, :]
    cosine = jnp.cos(angles)[:, None, :]
    sine = jnp.sin(angles)[:, None, :]
    first = values[..., :half_dim]
    second = values[..., half_dim:]
    return jnp.concatenate(
        [first * cosine - second * sine, second * cosine + first * sine], axis=-1
    )


def adamw(weight, grad, first, second, rate, decay):
    first_new = BETA_ONE * first + (1.0 - BETA_ONE) * grad
    second_new = BETA_TWO * second + (1.0 - BETA_TWO) * grad * grad
    update = (
        first_new
        / (1.0 - BETA_ONE**STEP)
        / (jnp.sqrt(second_new / (1.0 - BETA_TWO**STEP)) + ADAM_EPS)
    )
    return (weight - rate * (update + decay * weight), first_new, second_new)


def swap(values, axis, distance=1):
    count = lax.axis_size(axis)
    return lax.ppermute(values, axis, [((i + distance) % count, i) for i in range(count)])


def gather_direct(values, axis):
    count, me = lax.axis_size(axis), lax.axis_index(axis)
    out = jnp.zeros((count,) + values.shape, values.dtype)
    out = lax.dynamic_update_index_in_dim(out, values, me, 0)
    for distance in range(1, count):
        got = swap(values, axis, distance)
        out = lax.dynamic_update_index_in_dim(out, got, (me + distance) % count, 0)
    return out


def line_steps(values, axis):
    count = lax.axis_size(axis)
    below, above = [], []
    up, down = values, values
    for step in range(1, count):
        up = lax.ppermute(up, axis, [(i, i + 1) for i in range(step - 1, count - 1)])
        down = lax.ppermute(down, axis, [(i, i - 1) for i in range(1, count - step + 1)])
        below.append(up)
        above.append(down)
    return below, above


def gather_line(values, axis):
    count, me = lax.axis_size(axis), lax.axis_index(axis)
    below, above = line_steps(values, axis)
    out = jnp.zeros((count,) + values.shape, values.dtype)
    out = lax.dynamic_update_index_in_dim(out, values, me, 0)
    for offset in range(1, count):
        got = jnp.where(me + offset < count, above[offset - 1], below[count - offset - 1])
        out = lax.dynamic_update_index_in_dim(out, got, (me + offset) % count, 0)
    return out


def scatter_direct(parts, axis, dim=0):
    count, me = lax.axis_size(axis), lax.axis_index(axis)
    total = lax.dynamic_index_in_dim(parts, me, dim, keepdims=False).astype(F32)
    for distance in range(1, count):
        mine = lax.dynamic_index_in_dim(parts, (me - distance) % count, dim, keepdims=False)
        total = total + swap(mine.astype(BF), axis, distance).astype(F32)
    return total


def scatter_line(parts, axis, dim=0):
    count, me = lax.axis_size(axis), lax.axis_index(axis)

    def own(index):
        return lax.dynamic_index_in_dim(parts, jnp.clip(index, 0, count - 1), dim, keepdims=False)

    up = down = None
    for step in range(1, count):
        far = count - step
        up_out = own(me + far).astype(F32)
        down_out = own(me - far).astype(F32)
        if step > 1:
            up_out, down_out = up_out + up.astype(F32), down_out + down.astype(F32)
        up = lax.ppermute(up_out.astype(BF), axis, [(i, i + 1) for i in range(step)])
        down = lax.ppermute(
            down_out.astype(BF), axis, [(i, i - 1) for i in range(count - step, count)]
        )
    return own(me).astype(F32) + up.astype(F32) + down.astype(F32)


def gather_rows(shard):
    half = shard.shape[1] // 2 // LANES * LANES
    first = gather_direct(shard[:, :half], "x")
    first = gather_direct(gather_line(first, "z"), "r")
    first = gather_direct(first, "c")
    second = gather_direct(shard[:, half:], "r")
    second = gather_direct(gather_line(second, "z"), "x")
    second = gather_direct(second, "c")
    first = first.transpose(1, 2, 3, 0, 4, 5)
    second = second.transpose(3, 2, 1, 0, 4, 5)
    return jnp.concatenate([first, second], axis=-1)


def scatter_rows(parts):
    half = parts.shape[-1] // 2 // LANES * LANES
    first = scatter_direct(parts[..., :half], "c", 3).astype(BF)
    first = scatter_direct(first, "r", 0).astype(BF)
    first = scatter_line(first, "z", 0).astype(BF)
    first = scatter_direct(first, "x", 0)
    second = scatter_direct(parts[..., half:], "c", 3).astype(BF)
    second = scatter_direct(second, "x", 2).astype(BF)
    second = scatter_line(second, "z", 1).astype(BF)
    second = scatter_direct(second, "r", 0)
    return jnp.concatenate([first, second], axis=-1)


def group_permute(values, mask):
    return lax.ppermute(values, ("x", "c"), [(i ^ mask, i) for i in range(GROUP)])


def group_spread(shard):
    rows = shard.shape[0]
    me = 2 * lax.axis_index("x") + lax.axis_index("c")
    out = jnp.zeros((GROUP, rows, QUARTER), shard.dtype)
    for mask in range(GROUP):
        mine = lax.dynamic_slice_in_dim(shard, (me ^ mask) * QUARTER, QUARTER, 1)
        got = group_permute(mine, mask) if mask else mine
        out = lax.dynamic_update_index_in_dim(out, got, me ^ mask, 0)
    return out.reshape(GROUP * rows, QUARTER)


def group_collect(block):
    rows = block.shape[0] // GROUP
    me = 2 * lax.axis_index("x") + lax.axis_index("c")
    parts = block.reshape(GROUP, rows, QUARTER)
    out = jnp.zeros((rows, GROUP * QUARTER), block.dtype)
    for mask in range(GROUP):
        mine = lax.dynamic_index_in_dim(parts, me ^ mask, 0, keepdims=False)
        got = group_permute(mine, mask) if mask else mine
        out = lax.dynamic_update_slice_in_dim(out, got, (me ^ mask) * QUARTER, 1)
    return out


def gather_blocks(block):
    full = gather_direct(gather_line(block, "z"), "r")
    return full.reshape(-1, block.shape[1])


def scatter_blocks(parts):
    r_count, z_count = lax.axis_size("r"), lax.axis_size("z")
    parts = parts.reshape(r_count, z_count, -1, parts.shape[1])
    return scatter_line(scatter_direct(parts, "r", 0).astype(BF), "z", 0)


def exchange(values):
    other = swap(values, "c")
    across = swap(values, "x")
    across_other = swap(across, "c")
    return jnp.concatenate([values, other, across, across_other], axis=0)


def exchange_back(parts):
    rows = parts.shape[0] // GROUP
    own, other, across, across_other = (parts[i * rows : (i + 1) * rows] for i in range(GROUP))
    far = across + swap(across_other.astype(BF), "c").astype(F32)
    near = own + swap(other.astype(BF), "c").astype(F32)
    return near + swap(far.astype(BF), "x").astype(F32)


def pad_cols(values, cols):
    return jnp.pad(values, ((0, 0), (0, cols - values.shape[1])))


def body(
    layer_input,
    cotangent,
    lengths,
    weights,
    norm_gains,
    head_gains,
    moment_weights,
    moment_gains,
    moment_head,
    square_weights,
    square_gains,
    square_head,
):
    rows = weights.shape[0]
    head_rows = head_gains.shape[0]
    width = layer_input.shape[1]
    r_count, z_count = lax.axis_size("r"), lax.axis_size("z")

    weights_low = weights.astype(BF)
    gain_cols = jnp.zeros((max(rows, head_rows), LANES), BF)
    gain_cols = gain_cols.at[:rows, :4].set(norm_gains.astype(BF))
    gain_cols = gain_cols.at[:head_rows, 4:6].set(head_gains.astype(BF))[:rows]
    first_shard = jnp.concatenate([weights_low[:, :START_GATE], gain_cols], axis=1)
    first_full = gather_rows(first_shard)
    w_qkv = first_full[..., :START_GATE].reshape(width, START_GATE)
    gain_part = first_full[..., START_GATE:]
    gain_f = 1.0 + gain_part[..., :4].reshape(width, 4).astype(F32)
    head_f = (
        gain_part[..., :head_rows, 4:6].transpose(0, 2, 3, 1, 4, 5).reshape(HD, 2).astype(F32)
    ) + 1.0
    w_out = gather_rows(weights_low[:, START_OUT:START_DOWN]).reshape(width, Q_COLS)
    padded = GROUP * QUARTER
    w_gate = gather_blocks(group_spread(pad_cols(weights_low[:, START_GATE : START_GATE + FF], padded)))
    w_up = gather_blocks(group_spread(pad_cols(weights_low[:, START_GATE + FF : START_OUT], padded)))
    w_down = gather_blocks(group_spread(pad_cols(weights_low[:, START_DOWN:], padded)))

    order = (
        np.arange(width)
        .reshape(r_count, 2, 2, z_count, rows)
        .transpose(0, 3, 1, 2, 4)
        .reshape(width)
    )
    place = (jnp.arange(width)[:, None] == jnp.asarray(order)[None, :]).astype(BF)

    tok_rows = layer_input.shape[0]
    ctx_count = z_count
    local_slots = lax.axis_index("z") * tok_rows + jnp.arange(tok_rows, dtype=jnp.int32)
    positions = block_positions(local_slots, tok_rows, ctx_count)
    seq_length = lengths[0]
    row_valid = positions < seq_length
    inputs = jnp.dot(layer_input, place, preferred_element_type=F32)
    cot = jnp.dot(cotangent, place, preferred_element_type=F32)
    normed_in, pull_in = jax.vjp(rms_gain, inputs, gain_f[:, 0])
    normed_low = normed_in.astype(BF)
    projected = jnp.dot(normed_low, w_qkv, preferred_element_type=F32)

    def query_key(query_raw, key_raw, head_arg):
        query_out = (
            rotate(rms_gain(query_raw.reshape(tok_rows, H, HD), head_arg[:, 0]), positions)
            * QUERY_SCALE
        )
        key_out = rotate(rms_gain(key_raw[:, None, :], head_arg[:, 1]), positions)[:, 0]
        return (query_out, key_out)

    (queries, keys), pull_qk = jax.vjp(
        query_key, projected[:, :Q_COLS], projected[:, Q_COLS : Q_COLS + HD], head_f
    )
    query_low = queries.astype(BF)
    key_low = keys.astype(BF)
    value_low = projected[:, Q_COLS + HD :].astype(BF)
    key_value = gather_line(jnp.concatenate([key_low, value_low], axis=1), "z")
    key_value = key_value.reshape(z_count * tok_rows, 2 * HD)
    all_keys, all_values = key_value[:, :HD], key_value[:, HD:]
    key_pos = block_positions(jnp.arange(all_keys.shape[0], dtype=jnp.int32), tok_rows, ctx_count)
    allowed = (key_pos[None, :] <= positions[:, None]) & (key_pos < seq_length)[None, :]
    scores = jnp.einsum("thd,sd->hts", query_low, all_keys, preferred_element_type=F32)
    scores = jnp.where(allowed[None], scores, NEG_LARGE)
    row_max = jnp.max(scores, axis=-1, keepdims=True)
    expon = jnp.exp(scores - row_max)
    row_total = jnp.sum(expon, axis=-1, keepdims=True)
    probs_low = (expon / row_total).astype(BF)
    log_total = (row_max + jnp.log(row_total))[..., 0]
    mixed = jnp.einsum("hts,sd->thd", probs_low, all_values, preferred_element_type=F32)
    mixed_low = mixed.reshape(tok_rows, Q_COLS).astype(BF)
    attn_proj = jnp.einsum("tc,dc->td", mixed_low, w_out, preferred_element_type=F32)
    post_attn, pull_attn = jax.vjp(rms_gain, attn_proj, gain_f[:, 1])
    residual_mid = inputs + post_attn
    normed_mid, pull_mid = jax.vjp(rms_gain, residual_mid, gain_f[:, 2])

    mid_low = exchange(normed_mid.astype(BF))
    gate = jnp.dot(mid_low, w_gate, preferred_element_type=F32)
    up = jnp.dot(mid_low, w_up, preferred_element_type=F32)

    def geglu(gate_arg, up_arg):
        return jax.nn.gelu(gate_arg, approximate=True) * up_arg

    hidden, pull_hidden = jax.vjp(geglu, gate, up)
    hidden_low = hidden.astype(BF)
    mlp_part = jnp.einsum("tf,df->td", hidden_low, w_down, preferred_element_type=F32)
    mlp_proj = exchange_back(mlp_part)
    post_mlp, pull_mlp = jax.vjp(rms_gain, mlp_proj, gain_f[:, 3])
    output_low = (residual_mid + post_mlp).astype(BF)
    out_grad = cot * row_valid[:, None].astype(F32)
    mlp_grad, grad_three = pull_mlp(out_grad)
    mlp_grad_low = exchange(mlp_grad.astype(BF))
    hidden_grad = jnp.dot(mlp_grad_low, w_down, preferred_element_type=F32)
    gate_grad, up_grad = pull_hidden(hidden_grad)
    gate_low, up_low = gate_grad.astype(BF), up_grad.astype(BF)
    mid_part = jnp.einsum("tc,dc->td", gate_low, w_gate, preferred_element_type=F32)
    mid_part += jnp.einsum("tc,dc->td", up_low, w_up, preferred_element_type=F32)
    mid_grad = exchange_back(mid_part)
    grad_down = jnp.einsum("td,tf->df", mlp_grad_low, hidden_low, preferred_element_type=F32)
    grad_gate = jnp.einsum("td,tf->df", mid_low, gate_low, preferred_element_type=F32)
    grad_up = jnp.einsum("td,tf->df", mid_low, up_low, preferred_element_type=F32)
    sum_down = group_collect(scatter_blocks(grad_down.astype(BF)).astype(BF))[:, :FF]
    sum_gate = group_collect(scatter_blocks(grad_gate.astype(BF)).astype(BF))[:, :FF]
    sum_up = group_collect(scatter_blocks(grad_up.astype(BF)).astype(BF))[:, :FF]

    resid_part, grad_two = pull_mid(mid_grad)
    residual_grad = out_grad + resid_part
    attn_grad, grad_one = pull_attn(residual_grad)
    attn_low = attn_grad.astype(BF)
    grad_out = jnp.einsum("td,tc->dc", attn_low, mixed_low, preferred_element_type=F32)
    row_shape = (r_count, z_count, 2, 2, rows)
    sum_out = scatter_rows(grad_out.astype(BF).reshape(row_shape + (Q_COLS,)))
    mixed_grad = jnp.dot(attn_low, w_out, preferred_element_type=F32).astype(BF)
    query_heads = query_low.transpose(1, 0, 2)
    grad_heads = mixed_grad.reshape(tok_rows, H, HD).transpose(1, 0, 2)

    def head_back(head_in):
        query_one, grad_one_head, total_one = head_in
        head_scores = jnp.einsum("td,sd->ts", query_one, all_keys, preferred_element_type=F32)
        head_scores = jnp.where(allowed, head_scores, NEG_LARGE)
        head_probs = jnp.exp(head_scores - total_one[:, None])
        prob_grad = jnp.einsum("td,sd->ts", grad_one_head, all_values, preferred_element_type=F32)
        delta_row = jnp.sum(head_probs * prob_grad, axis=-1, keepdims=True)
        score_low = (head_probs * (prob_grad - delta_row)).astype(BF)
        query_grad = jnp.dot(score_low, all_keys, preferred_element_type=F32)
        key_part = jnp.einsum("ts,td->sd", score_low, query_one, preferred_element_type=F32)
        value_part = jnp.einsum(
            "ts,td->sd", head_probs.astype(BF), grad_one_head, preferred_element_type=F32
        )
        return (query_grad, key_part, value_part)

    query_grads, key_parts, value_parts = lax.map(head_back, (query_heads, grad_heads, log_total))
    key_value_part = jnp.concatenate(
        [jnp.sum(key_parts, axis=0), jnp.sum(value_parts, axis=0)], axis=1
    )
    key_value_grad = scatter_line(
        key_value_part.astype(BF).reshape(z_count, tok_rows, 2 * HD), "z", 0
    )
    raw_query, raw_key, grad_head = pull_qk(
        (query_grads.transpose(1, 0, 2), key_value_grad[:, :HD])
    )
    proj_low = jnp.concatenate([raw_query, raw_key, key_value_grad[:, HD:]], axis=1).astype(BF)
    grad_qkv = jnp.einsum("td,tc->dc", normed_low, proj_low, preferred_element_type=F32)
    in_part = jnp.einsum("tc,dc->td", proj_low, w_qkv, preferred_element_type=F32)
    input_part, grad_zero = pull_in(in_part)
    grad_input_low = (residual_grad + input_part).astype(BF)

    gain_grads = jnp.stack([grad_zero, grad_one, grad_two, grad_three], axis=1)
    gain_grads = gain_grads.reshape(row_shape + (4,))
    head_grads = grad_head.reshape(r_count, 2, 2, z_count, head_rows, 2).transpose(0, 3, 1, 2, 4, 5)
    side = jnp.zeros((r_count, z_count, 2, 2, rows, LANES), BF)
    side = side.at[..., :4].set(gain_grads.astype(BF))
    side = side.at[..., :head_rows, 4:6].set(head_grads.astype(BF))
    qkv_parts = jnp.concatenate(
        [grad_qkv.astype(BF).reshape(row_shape + (START_GATE,)), side], axis=-1
    )
    sum_first = scatter_rows(qkv_parts)
    sum_qkv = sum_first[:, :START_GATE]
    sum_gains = sum_first[:, START_GATE : START_GATE + 4]
    sum_head = sum_first[:head_rows, START_GATE + 4 : START_GATE + 6]

    output = lax.dot_general(
        output_low, place, (((1,), (1,)), ((), ())), preferred_element_type=F32
    ).astype(BF)
    grad_input = lax.dot_general(
        grad_input_low, place, (((1,), (1,)), ((), ())), preferred_element_type=F32
    ).astype(BF)

    sum_weights = jnp.concatenate(
        [sum_qkv, sum_gate.astype(F32), sum_up.astype(F32), sum_out, sum_down.astype(F32)], axis=1
    )
    new_w, first_w, second_w = adamw(
        weights, sum_weights, moment_weights, square_weights, RATE_WEIGHTS, WEIGHT_DECAY
    )
    new_g, first_g, second_g = adamw(
        norm_gains, sum_gains, moment_gains, square_gains, RATE_GAINS, 0.0
    )
    new_h, first_h, second_h = adamw(
        head_gains, sum_head, moment_head, square_head, RATE_GAINS, 0.0
    )
    return (
        output,
        grad_input,
        new_w,
        new_g,
        new_h,
        first_w,
        first_g,
        first_h,
        second_w,
        second_g,
        second_h,
        new_w.astype(BF),
    )


def solution(mesh):
    dp_count, ctx_count = mesh.shape["dp"], mesh.shape["ctx"]
    inner = Mesh(mesh.devices.reshape(dp_count // 4, 2, 2, ctx_count), ("r", "x", "c", "z"))
    rows = P(("r", "x", "c", "z"), None)
    in_specs = (rows, rows, P(("r", "x", "c"))) + (rows,) * 9
    return jax.shard_map(
        body, mesh=inner, in_specs=in_specs, out_specs=(rows,) * 12, check_vma=False
    )
```

time: 4210 us -> 1380 us (0.33)
  blocking collectives: 3220 us -> 0 us
  starting transfers between devices: 164 us -> 304 us
  local copies, waits for them, and re-layouts: 210 us -> 323 us
  waiting for transfers between devices: 258 us -> 346 us
  other arithmetic: 86.7 us -> 145 us
    unnamed x3 -> x0, blocking collectives: 3080 us -> none
    ppermute x0 -> x156, waiting for transfers between devices: none -> 346 us  [the longest x42 162 us: swap(): lax.ppermute(values, axis, [((i + distance) % count, i) for i in range(co...]
    ppermute x0 -> x156, starting transfers between devices: none -> 304 us  [the longest x24 116 us: scatter_line(): lax.ppermute(up_out.astype(BF), axis, [(i, i + 1) for i in range(step)])]
    all_gather x3 -> x0, waiting for transfers between devices: 202 us -> none  [the longest x1 186 us: body(): lax.all_gather(weights.astype(jnp.bfloat16), ('dp', 'ctx'), axis=0, tiled...]
    unnamed x169 -> x356, local copies, waits for them, and re-layouts: 193 us -> 18.6 us
    unnamed x20 -> x0, starting transfers between devices: 163 us -> none
    dynamic_update_slice x0 -> x74, local copies, waits for them, and re-layouts: none -> 136 us  [the longest x13 47.4 us: gather_line(): out = lax.dynamic_update_index_in_dim(out, got, (me + offset) % count, 0)]
    all_gather x2 -> x0, blocking collectives: 135 us -> none  [the longest x1 71.1 us: body(): lax.all_gather(norm_gains.astype(jnp.bfloat16), ('dp', 'ctx'), axis=0, ti...]
  transfers between devices with their start and end apart: 25 -> 156, of which waited for: 5 -> 46; matrix products, arithmetic and copies ran while one was open for 31% -> 44% of each run, Pallas kernels for 0% -> 0%
where the time goes in v1:
time: 1380 us; the launch traced here: 1360 us
  waiting for transfers between devices  346 us (25%)
  local copies, waits for them, and re-layouts  323 us (23%)
  starting transfers between devices  304 us (22%)
  matrix products  233 us (17%)
  other arithmetic  145 us (11%)
    ppermute x42, waiting for transfers between devices, swap(): lax.ppermute(values, axis, [((i + distance) % count, i) for i in range(co...  162 us
    ppermute x24, starting transfers between devices, scatter_line(): lax.ppermute(up_out.astype(BF), axis, [(i, i + 1) for i in range(step)])  116 us
    ppermute x24, waiting for transfers between devices, line_steps(): lax.ppermute(down, axis, [(i, i - 1) for i in range(1, count - step + 1)])  87 us
    ppermute x24, starting transfers between devices, line_steps(): lax.ppermute(up, axis, [(i, i + 1) for i in range(step - 1, count - 1)])  73 us
    ppermute x24, waiting for transfers between devices, scatter_line(): lax.ppermute(up_out.astype(BF), axis, [(i, i + 1) for i in range(step)])  58.7 us
    dynamic_update_slice x13, local copies, waits for them, and re-layouts, gather_line(): out = lax.dynamic_update_index_in_dim(out, got, (me + offset) % count, 0)  47.4 us
    ppermute x24, starting transfers between devices, line_steps(): lax.ppermute(down, axis, [(i, i - 1) for i in range(1, count - step + 1)])  31.5 us
    ppermute x42, starting transfers between devices, swap(): lax.ppermute(values, axis, [((i + distance) % count, i) for i in range(co...  31.4 us
  transfers between devices with their start and end apart: 156, of which 46 were waited for; matrix products, arithmetic and copies ran while one was open for 44% of the time, Pallas kernels for 0%

profile of v1, /device:TPU:0, one launch (start us, length us, event | category | flops | bytes accessed | tf_op | source)
XLA Modules:
  0.0 1357.3 jit_solution(11172948734092700738)
XLA Ops:
  46.3 6.1 collective-permute-start.66
  54.4 5.8 collective-permute-start.67
  102.9 5.2 collective-permute-start.26
  114.6 5.6 collective-permute-start.11
  140.5 7.4 collective-permute-start.2
  151.3 7.3 collective-permute-done.29
  172.5 6.2 collective-permute-start.69
  215.1 10.1 collective-permute-start.59
  230.0 6.8 collective-permute-done.5
  250.0 5.5 dynamic_update_slice.298
  255.5 5.5 dynamic_update_slice.299
  260.9 5.5 dynamic_update_slice.300
  317.1 8.7 collective-permute-start.49
  348.0 5.6 collective-permute-done.72
  357.8 6.9 collective-permute-done.62
  367.9 7.8 collective-permute-done.52
  377.2 9.5 collective-permute-done.73
  404.7 6.9 copy.1953
  419.8 5.7 reshape.777
  426.3 5.1 fusion.239
  438.3 7.4 collective-permute-start.19
  470.3 16.4 %collective-permute-done.22 = bf16[512,512]{1,0:T(8,128)(2,1)S(1)} collective-permute-done((bf16[512,512]{1,0:T(8,128)(2,1)}, bf16[512,512]{1,0:T(8,128)(2,1)S(1)}, u32[]{:S(2)}, u32[]{:S(2)}) %collective-permute-start.22) | collective-permute-done | bytes 524320 | tf_op jit(solution)/shard_map/ppermute | solution.py:92
  489.4 11.3 collective-permute-done.23
  500.9 7.7 fusion.19
  508.7 9.1 fusion.27
  517.8 8.9 fusion.79
  544.4 16.7 %collective-permute-done.43 = bf16[512,1152]{0,1:T(8,128)(2,1)S(1)} collective-permute-done((bf16[512,1152]{0,1:T(8,128)(2,1)S(1)}, bf16[512,1152]{0,1:T(8,128)(2,1)S(1)}, u32[]{:S(2)}, u32[]{:S(2)}) %collective-permute-start.43) | collective-permute-done | bytes 1179680 | tf_op jit(solution)/shard_map/ppermute | solution.py:73
  566.4 17.1 %collective-permute-done.54 = bf16[4,144,1792]{2,1,0:T(8,128)(2,1)S(1)} collective-permute-done((bf16[4,144,1792]{2,1,0:T(8,128)(2,1)}, bf16[4,144,1792]{2,1,0:T(8,128)(2,1)S(1)}, u32[]{:S(2)}, u32[]{:S(2)}) %collective-permute-start.54) | collective-permute-done | bytes 2064416 | tf_op jit(solution)/shard_map/ppermute | solution.py:73
  583.8 14.2 %fusion.241 = f32[2048,1792]{1,0:T(8,128)} fusion(bf16[1152,1792]{1,0:T(8,128)(2,1)S(1)} %bitcast.627, bf16[512,1152]{0,1:T(8,128)(2,1)S(1)} %collective-permute-done.44, bf16[512,1152]{0,1:T(8,128)(2,1)S(1)} %collective-permute-done.43, bf16[512,1152]{0,1:T(8,128)(2,1)S(1)} %collective-permute-done.42, bf16[512,1152]{0,1:T(8,128)(2,1)S(1)} %multiply_convert_fusion.3), kind=kOutput, calls=%fused_computation.580 | convolution fusion | flops 8474591232 | bytes 23527424 | tf_op jit(solution)/shard_map/dot_general | solution.py:312
  598.1 23.1 %multiply_convert_fusion.2 = (bf16[2048,1792]{1,0:T(8,128)(2,1)}, f32[2048,1792]{1,0:T(8,128)}) fusion(f32[2048,1792]{1,0:T(8,128)} %fusion.241, bf16[1152,1792]{1,0:T(8,128)(2,1)} %bitcast.625, bf16[512,1152]{0,1:T(8,128)(2,1)} %copy-done.169, bf16[512,1152]{0,1:T(8,128)(2,1)S(1)} %collective-permute-done.43, bf16[512,1152]{0,1:T(8,128)(2,1)} %copy-done.167, ...), kind=kOutput, calls=%fused_computation.39 | convolution fusion | flops 8511291392 | bytes 45547520 | tf_op jit(solution)/shard_map/dot_general | solution.py:313
  621.2 12.7 fusion.257
  638.7 26.9 %collective-permute-done.77 = bf16[512,1152]{0,1:T(8,128)(2,1)S(1)} collective-permute-done((bf16[512,1152]{0,1:T(8,128)(2,1)S(1)}, bf16[512,1152]{0,1:T(8,128)(2,1)S(1)}, u32[]{:S(2)}, u32[]{:S(2)}) %collective-permute-start.77) | collective-permute-done | bytes 1179680 | tf_op jit(solution)/shard_map/ppermute | solution.py:73
  673.2 24.7 %collective-permute-done.79 = bf16[512,1152]{0,1:T(8,128)(2,1)} collective-permute-done((bf16[512,1152]{0,1:T(8,128)(2,1)}, bf16[512,1152]{0,1:T(8,128)(2,1)}, u32[]{:S(2)}, u32[]{:S(2)}) %collective-permute-start.79) | collective-permute-done | bytes 1179680 | tf_op jit(solution)/shard_map/ppermute | solution.py:73
  707.2 12.7 convolution_convert_fusion.1
  722.2 28.1 %fusion.26 = (bf16[2048,1792]{1,0:T(8,128)(2,1)}, bf16[2048,1792]{1,0:T(8,128)(2,1)}) fusion(f32[2048,1792]{1,0:T(8,128)} %fusion.241, f32[2048,1792]{1,0:T(8,128)} %get-tuple-element.487, bf16[1152,1792]{1,0:T(8,128)(2,1)} %bitcast.94, bf16[512,1152]{0,1:T(8,128)(2,1)} %collective-permute-done.80, bf16[512,1152]{0,1:T(8,128)(2,1)} %collective-permute-done.79, ...), kind=kOutput, calls=%fused_computation.37 | convolution fusion | flops 8562671616 | bytes 52887552 | tf_op jit(solution)/shard_map/dot_general | solution.py:327
  750.3 13.2 fusion.259
  763.5 15.0 %fusion.258 = (bf16[2048,1152]{0,1:T(8,128)(2,1)}, f32[2048,1152]{0,1:T(8,128)S(1)}) fusion(f32[2048,1152]{0,1:T(8,128)} %fusion.259, bf16[2048,1792]{1,0:T(8,128)(2,1)} %get-tuple-element.395, bf16[1152,1792]{1,0:T(8,128)(2,1)} %bitcast.628), kind=kOutput, calls=%fused_computation.592 | convolution fusion | flops 8460435456 | bytes 35061760 | tf_op jit(solution)/shard_map/tc,dc->td/dot_general | solution.py:330
  782.5 12.4 convolution_convert_fusion.2
  798.7 12.2 convolution_convert_fusion.3
  821.2 24.3 %collective-permute-done.118 = bf16[4,144,1792]{2,1,0:T(8,128)(2,1)} collective-permute-done((bf16[4,144,1792]{2,1,0:T(8,128)(2,1)}, bf16[4,144,1792]{2,1,0:T(8,128)(2,1)}, u32[]{:S(2)}, u32[]{:S(2)}) %collective-permute-start.118) | collective-permute-done | bytes 2064416 | tf_op jit(solution)/shard_map/ppermute | solution.py:73
  850.2 38.8 %collective-permute-done.108 = bf16[4,144,1792]{2,1,0:T(8,128)(2,1)S(1)} collective-permute-done((bf16[4,144,1792]{2,1,0:T(8,128)(2,1)S(1)}, bf16[4,144,1792]{2,1,0:T(8,128)(2,1)S(1)}, u32[]{:S(2)}, u32[]{:S(2)}) %collective-permute-start.108) | collective-permute-done | bytes 2064416 | tf_op jit(solution)/shard_map/ppermute | solution.py:73
  912.5 37.6 %while.19 = (s32[]{:T(128)}, f32[4,512,256]{2,1,0:T(8,128)}, f32[4,2048,256]{2,1,0:T(8,128)}, f32[4,2048,256]{2,1,0:T(8,128)}, bf16[4,512,256]{2,1,0:T(8,128)(2,...) while((s32[]{:T(128)}, f32[4,512,256]{2,1,0:T(8,128)}, ...), condition=%wide.region_15.16_spmd.clone, body=%wide.region_13.15_spmd.clone.sunk | while | flops 2694839808 | bytes 44589732 | solution.py:366
  959.4 5.3 reduce_sum.218
  978.8 6.4 collective-permute-done.84
  995.8 7.1 collective-permute-done.148
  1018.2 6.8 collective-permute-done.110
  1026.9 5.0 collective-permute-start.139
  1071.4 15.8 %collective-permute-start.132 = (bf16[2,36,512]{2,1,0:T(8,128)(2,1)S(1)}, bf16[2,36,512]{2,1,0:T(8,128)(2,1)S(1)}, u32[]{:S(2)}, u32[]{:S(2)}) collective-permute-start(bf16[2,36,512]{2,1,0:T(8,128)(2,1)S(1)} %get-tuple-element.470), channel_id=1, source_target_pairs={{0,1},{1,2},{2,3},{4,5},{5,6},{6,7},{8,9},{9,10},{10,11},{12,13},{... | collective-permute-start | bytes 221192 | tf_op jit(solution)/shard_map/ppermute | solution.py:131
  1089.7 5.3 collective-permute-start.121
  1103.4 11.8 collective-permute-start.111
  1117.9 7.4 collective-permute-start.152
  1133.2 5.4 convolution_convert_fusion
  1142.3 5.6 reshape.789
  1150.9 11.9 copy.2008
  1163.1 5.9 fusion.56
  1203.6 5.1 collective-permute-done.114
  1223.0 5.5 collective-permute-done.155
  1230.7 5.2 collective-permute-done.126
  1235.9 5.5 collective-permute-done.127
  1273.2 6.1 collective-permute-done.100
  1288.3 9.5 collective-permute-done.101
  1306.3 6.2 collective-permute-done.102
  1314.9 14.1 %collective-permute-start.103 = (bf16[2,36,896]{1,2,0:T(8,128)(2,1)S(1)}, bf16[2,36,896]{1,2,0:T(8,128)(2,1)S(1)}, u32[]{:S(2)}, u32[]{:S(2)}) collective-permute-start(bf16[2,36,896]{1,2,0:T(8,128)(2,1)S(1)} %get-tuple-element.436), channel_id=1, source_target_pairs={{0,1},{1,2},{2,3},{4,5},{5,6},{6,7},{8,9},{9,10},{10,11},{12,13},{... | collective-permute-start | bytes 387080 | tf_op jit(solution)/shard_map/ppermute | solution.py:131
  1349.2 7.9 fusion.242
  (1029 shorter events, 700.5 us)
Async XLA Ops:
  6.1 76.2 %collective-permute-start.65 = (bf16[36,1792]{1,0:T(8,128)(2,1)}, bf16[36,1792]{1,0:T(8,128)(2,1)}, u32[]{:S(2)}, u32[]{:S(2)}) collective-permute-start(bf16[36,1792]{1,0:T(8,128)(2,1)} %get-tuple-element.450), channel_id=1, source_target_pairs={{4,0},{0,4},{12,8},{8,12},{5,1},{1,5},{13,9},{9,13},{6,2},{2,6},{1... | collective-permute-start | bytes 387080 | tf_op jit(solution)/shard_map/ppermute | solution.py:165
  7.2 39.1 %collective-permute-start.33 = (bf16[36,512]{1,0:T(8,128)(2,1)}, bf16[36,512]{1,0:T(8,128)(2,1)}, u32[]{:S(2)}, u32[]{:S(2)}) collective-permute-start(bf16[36,512]{1,0:T(8,128)(2,1)} %get-tuple-element.433), channel_id=1, source_target_pairs={{16,0},{0,16},{17,1},{1,17},{18,2},{2,18},{19,3},{3,19},{20,4},{4,... | collective-permute-start | bytes 110600 | tf_op jit(solution)/shard_map/ppermute | solution.py:73
  9.7 44.6 %collective-permute-start.24 = (bf16[36,512]{1,0:T(8,128)(2,1)}, bf16[36,512]{1,0:T(8,128)(2,1)}, u32[]{:S(2)}, u32[]{:S(2)}) collective-permute-start(bf16[36,512]{1,0:T(8,128)(2,1)} %get-tuple-element.430), channel_id=1, source_target_pairs={{8,0},{0,8},{9,1},{1,9},{10,2},{2,10},{11,3},{3,11},{12,4},{4,12},... | collective-permute-start | bytes 110600 | tf_op jit(solution)/shard_map/ppermute | solution.py:73
  11.8 55.8 %collective-permute-start.9 = (bf16[36,768]{1,0:T(8,128)(2,1)}, bf16[36,768]{1,0:T(8,128)(2,1)}, u32[]{:S(2)}, u32[]{:S(2)}) collective-permute-start(bf16[36,768]{1,0:T(8,128)(2,1)} %get-tuple-element.434), channel_id=1, source_target_pairs={{8,0},{0,8},{9,1},{1,9},{10,2},{2,10},{11,3},{3,11},{12,4},{4,12},... | collective-permute-start | bytes 165896 | tf_op jit(solution)/shard_map/ppermute | solution.py:73
  18.1 55.9 %collective-permute-start = (bf16[36,896]{1,0:T(8,128)(2,1)S(1)}, bf16[36,896]{1,0:T(8,128)(2,1)S(1)}, u32[]{:S(2)}, u32[]{:S(2)}) collective-permute-start(bf16[36,896]{1,0:T(8,128)(2,1)S(1)} %pad_maximum_fusion.11), channel_id=1, source_target_pairs={{16,0},{0,16},{17,1},{1,17},{18,2},{2,18},{19,3},{3,19},{20,4},{4,... | collective-permute-start | bytes 193544 | tf_op jit(solution)/shard_map/ppermute | solution.py:73
  46.3 44.0 %collective-permute-start.66 = (bf16[36,1792]{1,0:T(8,128)(2,1)}, bf16[36,1792]{1,0:T(8,128)(2,1)}, u32[]{:S(2)}, u32[]{:S(2)}) collective-permute-start(bf16[36,1792]{1,0:T(8,128)(2,1)} %get-tuple-element.451), channel_id=1, source_target_pairs={{8,0},{12,4},{0,8},{4,12},{9,1},{13,5},{1,9},{5,13},{10,2},{14,6},... | collective-permute-start | bytes 387080 | tf_op jit(solution)/shard_map/ppermute | solution.py:165
  54.4 40.8 %collective-permute-start.67 = (bf16[36,1792]{1,0:T(8,128)(2,1)}, bf16[36,1792]{1,0:T(8,128)(2,1)}, u32[]{:S(2)}, u32[]{:S(2)}) collective-permute-start(bf16[36,1792]{1,0:T(8,128)(2,1)} %get-tuple-element.449), channel_id=1, source_target_pairs={{12,0},{8,4},{4,8},{0,12},{13,1},{9,5},{5,9},{1,13},{14,2},{10,6},... | collective-permute-start | bytes 387080 | tf_op jit(solution)/shard_map/ppermute | solution.py:165
  93.6 28.0 %collective-permute-start.47 = (bf16[36,1792]{1,0:T(8,128)(2,1)}, bf16[36,1792]{1,0:T(8,128)(2,1)}, u32[]{:S(2)}, u32[]{:S(2)}) collective-permute-start(bf16[36,1792]{1,0:T(8,128)(2,1)} %get-tuple-element.452), channel_id=1, source_target_pairs={{12,0},{8,4},{4,8},{0,12},{13,1},{9,5},{5,9},{1,13},{14,2},{10,6},... | collective-permute-start | bytes 387080 | tf_op jit(solution)/shard_map/ppermute | solution.py:165
  102.9 36.3 %collective-permute-start.26 = (bf16[2,36,512]{2,0,1:T(2,128)(2,1)S(1)}, bf16[2,36,512]{2,0,1:T(2,128)(2,1)}, u32[]{:S(2)}, u32[]{:S(2)}) collective-permute-start(bf16[2,36,512]{2,0,1:T(2,128)(2,1)S(1)} %dynamic_update_slice.310), channel_id=1, source_target_pairs={{0,1},{1,2},{2,3},{4,5},{5,6},{6,7},{8,9},{9,10},{10,11},{12,13},{... | collective-permute-start | bytes 221192 | tf_op jit(solution)/shard_map/ppermute | solution.py:91
  108.8 31.7 %collective-permute-start.25 = (bf16[2,36,512]{2,0,1:T(2,128)(2,1)S(1)}, bf16[2,36,512]{2,0,1:T(2,128)(2,1)}, u32[]{:S(2)}, u32[]{:S(2)}) collective-permute-start(bf16[2,36,512]{2,0,1:T(2,128)(2,1)S(1)} %dynamic_update_slice.310), channel_id=1, source_target_pairs={{1,0},{2,1},{3,2},{5,4},{6,5},{7,6},{9,8},{10,9},{11,10},{13,12},{... | collective-permute-start | bytes 221192 | tf_op jit(solution)/shard_map/ppermute | solution.py:92
  114.6 57.9 %collective-permute-start.11 = (bf16[2,36,768]{2,0,1:T(2,128)(2,1)S(1)}, bf16[2,36,768]{2,0,1:T(2,128)(2,1)}, u32[]{:S(2)}, u32[]{:S(2)}) collective-permute-start(bf16[2,36,768]{2,0,1:T(2,128)(2,1)S(1)} %dynamic_update_slice.296), channel_id=1, source_target_pairs={{0,1},{1,2},{2,3},{4,5},{5,6},{6,7},{8,9},{9,10},{10,11},{12,13},{... | collective-permute-start | bytes 331784 | tf_op jit(solution)/shard_map/ppermute | solution.py:91
  120.3 27.6 %collective-permute-start.36 = (bf16[2,36,512]{2,0,1:T(2,128)(2,1)}, bf16[2,36,512]{2,0,1:T(2,128)(2,1)}, u32[]{:S(2)}, u32[]{:S(2)}) collective-permute-start(bf16[2,36,512]{2,0,1:T(2,128)(2,1)} %collective-permute-done.35), channel_id=1, source_target_pairs={{1,2},{2,3},{5,6},{6,7},{9,10},{10,11},{13,14},{14,15},{17,18},{18... | collective-permute-start | bytes 221192 | tf_op jit(solution)/shard_map/ppermute | solution.py:91
  121.6 27.0 %collective-permute-start.38 = (bf16[2,36,512]{2,0,1:T(2,128)(2,1)}, bf16[2,36,512]{2,0,1:T(2,128)(2,1)S(1)}, u32[]{:S(2)}, u32[]{:S(2)}) collective-permute-start(bf16[2,36,512]{2,0,1:T(2,128)(2,1)} %collective-permute-done.34), channel_id=1, source_target_pairs={{1,0},{2,1},{5,4},{6,5},{9,8},{10,9},{13,12},{14,13},{17,16},{18,1... | collective-permute-start | bytes 221192 | tf_op jit(solution)/shard_map/ppermute | solution.py:92
  139.2 39.5 %collective-permute-start.10 = (bf16[2,36,768]{2,0,1:T(2,128)(2,1)S(1)}, bf16[2,36,768]{2,0,1:T(2,128)(2,1)}, u32[]{:S(2)}, u32[]{:S(2)}) collective-permute-start(bf16[2,36,768]{2,0,1:T(2,128)(2,1)S(1)} %dynamic_update_slice.296), channel_id=1, source_target_pairs={{1,0},{2,1},{3,2},{5,4},{6,5},{7,6},{9,8},{10,9},{11,10},{13,12},{... | collective-permute-start | bytes 331784 | tf_op jit(solution)/shard_map/ppermute | solution.py:92
  140.5 73.3 %collective-permute-start.2 = (bf16[2,36,896]{2,0,1:T(2,128)(2,1)}, bf16[2,36,896]{2,0,1:T(2,128)(2,1)}, u32[]{:S(2)}, u32[]{:S(2)}) collective-permute-start(bf16[2,36,896]{2,0,1:T(2,128)(2,1)} %dynamic_update_slice.286), channel_id=1, source_target_pairs={{0,1},{1,2},{2,3},{4,5},{5,6},{6,7},{8,9},{9,10},{10,11},{12,13},{... | collective-permute-start | bytes 387080 | tf_op jit(solution)/shard_map/ppermute | solution.py:91
  150.0 65.1 %collective-permute-start.1 = (bf16[2,36,896]{2,0,1:T(2,128)(2,1)}, bf16[2,36,896]{2,0,1:T(2,128)(2,1)}, u32[]{:S(2)}, u32[]{:S(2)}) collective-permute-start(bf16[2,36,896]{2,0,1:T(2,128)(2,1)} %dynamic_update_slice.286), channel_id=1, source_target_pairs={{1,0},{2,1},{3,2},{5,4},{6,5},{7,6},{9,8},{10,9},{11,10},{13,12},{... | collective-permute-start | bytes 387080 | tf_op jit(solution)/shard_map/ppermute | solution.py:92
  172.5 127.8 %collective-permute-start.69 = (bf16[144,1792]{1,0:T(8,128)(2,1)}, bf16[144,1792]{1,0:T(8,128)(2,1)}, u32[]{:S(2)}, u32[]{:S(2)}) collective-permute-start(bf16[144,1792]{1,0:T(8,128)(2,1)} %reshape.785), channel_id=1, source_target_pairs={{0,1},{1,2},{2,3},{4,5},{5,6},{6,7},{8,9},{9,10},{10,11},{12,13},{... | collective-permute-start | bytes 1548296 | tf_op jit(solution)/shard_map/ppermute | solution.py:91
  178.7 46.5 %collective-permute-start.12 = (bf16[2,36,768]{2,0,1:T(2,128)(2,1)}, bf16[2,36,768]{2,0,1:T(2,128)(2,1)}, u32[]{:S(2)}, u32[]{:S(2)}) collective-permute-start(bf16[2,36,768]{2,0,1:T(2,128)(2,1)} %collective-permute-done.11), channel_id=1, source_target_pairs={{1,2},{2,3},{5,6},{6,7},{9,10},{10,11},{13,14},{14,15},{17,18},{18... | collective-permute-start | bytes 331784 | tf_op jit(solution)/shard_map/ppermute | solution.py:91
  180.0 45.8 %collective-permute-start.14 = (bf16[2,36,768]{2,0,1:T(2,128)(2,1)}, bf16[2,36,768]{2,0,1:T(2,128)(2,1)}, u32[]{:S(2)}, u32[]{:S(2)}) collective-permute-start(bf16[2,36,768]{2,0,1:T(2,128)(2,1)} %collective-permute-done.10), channel_id=1, source_target_pairs={{1,0},{2,1},{5,4},{6,5},{9,8},{10,9},{13,12},{14,13},{17,16},{18,1... | collective-permute-start | bytes 331784 | tf_op jit(solution)/shard_map/ppermute | solution.py:92
  213.8 96.5 %collective-permute-start.68 = (bf16[144,1792]{1,0:T(8,128)(2,1)}, bf16[144,1792]{1,0:T(8,128)(2,1)}, u32[]{:S(2)}, u32[]{:S(2)}) collective-permute-start(bf16[144,1792]{1,0:T(8,128)(2,1)} %reshape.785), channel_id=1, source_target_pairs={{1,0},{2,1},{3,2},{5,4},{6,5},{7,6},{9,8},{10,9},{11,10},{13,12},{... | collective-permute-start | bytes 1548296 | tf_op jit(solution)/shard_map/ppermute | solution.py:92
  215.1 102.0 %collective-permute-start.59 = (bf16[144,1792]{1,0:T(8,128)(2,1)}, bf16[144,1792]{1,0:T(8,128)(2,1)}, u32[]{:S(2)}, u32[]{:S(2)}) collective-permute-start(bf16[144,1792]{1,0:T(8,128)(2,1)} %reshape.783), channel_id=1, source_target_pairs={{0,1},{1,2},{2,3},{4,5},{5,6},{6,7},{8,9},{9,10},{10,11},{12,13},{... | collective-permute-start | bytes 1548296 | tf_op jit(solution)/shard_map/ppermute | solution.py:91
  228.4 56.6 %collective-permute-start.40 = (bf16[4,2,36,512]{3,0,2,1:T(4,128)(2,1)}, bf16[4,2,36,512]{3,0,2,1:T(4,128)(2,1)}, u32[]{:S(2)}, u32[]{:S(2)}) collective-permute-start(bf16[4,2,36,512]{3,0,2,1:T(4,128)(2,1)} %dynamic_update_slice.324), channel_id=1, source_target_pairs={{8,0},{0,8},{9,1},{1,9},{10,2},{2,10},{11,3},{3,11},{12,4},{4,12},... | collective-permute-start | bytes 884744 | tf_op jit(solution)/shard_map/ppermute | solution.py:73
  295.4 30.5 %collective-permute-start.32 = (bf16[2,4,2,36,512]{4,1,3,2,0:T(4,128)(2,1)}, bf16[2,4,2,36,512]{4,1,3,2,0:T(4,128)(2,1)}, u32[]{:S(2)}, u32[]{:S(2)}) collective-permute-start(bf16[2,4,2,36,512]{4,1,3,2,0:T(4,128)(2,1)} %bitcast_dynamic-update-slice_fusion.29), channel_id=1, source_target_pairs={{4,0},{0,4},{5,1},{1,5},{6,2},{2,6},{7,3},{3,7},{12,8},{8,12},{13,... | collective-permute-start | bytes 1769480 | tf_op jit(solution)/shard_map/ppermute | solution.py:73
  301.7 27.0 %collective-permute-start.70 = (bf16[144,1792]{1,0:T(8,128)(2,1)}, bf16[144,1792]{1,0:T(8,128)(2,1)}, u32[]{:S(2)}, u32[]{:S(2)}) collective-permute-start(bf16[144,1792]{1,0:T(8,128)(2,1)} %collective-permute-done.69), channel_id=1, source_target_pairs={{1,2},{2,3},{5,6},{6,7},{9,10},{10,11},{13,14},{14,15},{17,18},{18... | collective-permute-start | bytes 1548296 | tf_op jit(solution)/shard_map/ppermute | solution.py:91
  344.0 31.7 %collective-permute-start.52 = (bf16[144,1792]{1,0:T(8,128)(2,1)}, bf16[144,1792]{1,0:T(8,128)(2,1)}, u32[]{:S(2)}, u32[]{:S(2)}) collective-permute-start(bf16[144,1792]{1,0:T(8,128)(2,1)} %collective-permute-done.48), channel_id=1, source_target_pairs={{1,0},{2,1},{5,4},{6,5},{9,8},{10,9},{13,12},{14,13},{17,16},{18,1... | collective-permute-start | bytes 1548296 | tf_op jit(solution)/shard_map/ppermute | solution.py:92
  353.6 40.8 %collective-permute-start.17 = (bf16[2,4,2,36,768]{4,1,3,2,0:T(4,128)(2,1)}, bf16[2,4,2,36,768]{4,1,3,2,0:T(4,128)(2,1)S(1)}, u32[]{:S(2)}, u32[]{:S(2)}) collective-permute-start(bf16[2,4,2,36,768]{4,1,3,2,0:T(4,128)(2,1)} %bitcast_dynamic-update-slice_fusion.25), channel_id=1, source_target_pairs={{4,0},{0,4},{5,1},{1,5},{6,2},{2,6},{7,3},{3,7},{12,8},{8,12},{13,... | collective-permute-start | bytes 2654216 | tf_op jit(solution)/shard_map/ppermute | solution.py:73
  355.6 31.1 %collective-permute-start.73 = (bf16[144,1792]{1,0:T(8,128)(2,1)}, bf16[144,1792]{1,0:T(8,128)(2,1)S(1)}, u32[]{:S(2)}, u32[]{:S(2)}) collective-permute-start(bf16[144,1792]{1,0:T(8,128)(2,1)} %collective-permute-done.72), channel_id=1, source_target_pairs={{1,0},{5,4},{9,8},{13,12},{17,16},{21,20},{25,24},{29,28}} | collective-permute-start | bytes 1548296 | tf_op jit(solution)/shard_map/ppermute | solution.py:92
  364.7 32.3 %collective-permute-start.8 = (bf16[2,4,2,36,896]{4,1,3,2,0:T(4,128)(2,1)S(1)}, bf16[2,4,2,36,896]{4,1,3,2,0:T(4,128)(2,1)S(1)}, u32[]{:S(2)}, u32[]{:S(2)}) collective-permute-start(bf16[2,4,2,36,896]{4,1,3,2,0:T(4,128)(2,1)S(1)} %copy.1942), channel_id=1, source_target_pairs={{4,0},{0,4},{5,1},{1,5},{6,2},{2,6},{7,3},{3,7},{12,8},{8,12},{13,... | collective-permute-start | bytes 3096584 | tf_op jit(solution)/shard_map/ppermute | solution.py:73
  366.6 79.2 %collective-permute-start.63 = (bf16[144,1792]{1,0:T(8,128)(2,1)}, bf16[144,1792]{1,0:T(8,128)(2,1)}, u32[]{:S(2)}, u32[]{:S(2)}) collective-permute-start(bf16[144,1792]{1,0:T(8,128)(2,1)} %collective-permute-done.62), channel_id=1, source_target_pairs={{1,0},{5,4},{9,8},{13,12},{17,16},{21,20},{25,24},{29,28}} | collective-permute-start | bytes 1548296 | tf_op jit(solution)/shard_map/ppermute | solution.py:92
  375.7 72.8 %collective-permute-start.51 = (bf16[144,1792]{1,0:T(8,128)(2,1)}, bf16[144,1792]{1,0:T(8,128)(2,1)}, u32[]{:S(2)}, u32[]{:S(2)}) collective-permute-start(bf16[144,1792]{1,0:T(8,128)(2,1)} %collective-permute-done.50), channel_id=1, source_target_pairs={{2,3},{6,7},{10,11},{14,15},{18,19},{22,23},{26,27},{30,31}} | collective-permute-start | bytes 1548296 | tf_op jit(solution)/shard_map/ppermute | solution.py:91
  386.7 150.7 %collective-permute-start.53 = (bf16[144,1792]{1,0:T(8,128)(2,1)}, bf16[144,1792]{1,0:T(8,128)(2,1)}, u32[]{:S(2)}, u32[]{:S(2)}) collective-permute-start(bf16[144,1792]{1,0:T(8,128)(2,1)} %collective-permute-done.52), channel_id=1, source_target_pairs={{1,0},{5,4},{9,8},{13,12},{17,16},{21,20},{25,24},{29,28}} | collective-permute-start | bytes 1548296 | tf_op jit(solution)/shard_map/ppermute | solution.py:92
  394.4 166.7 %collective-permute-start.74 = (bf16[4,144,1792]{2,1,0:T(8,128)(2,1)}, bf16[4,144,1792]{2,1,0:T(8,128)(2,1)}, u32[]{:S(2)}, u32[]{:S(2)}) collective-permute-start(bf16[4,144,1792]{2,1,0:T(8,128)(2,1)} %bitcast_dynamic-update-slice_fusion.16), channel_id=1, source_target_pairs={{16,0},{0,16},{17,1},{1,17},{18,2},{2,18},{19,3},{3,19},{20,4},{4,... | collective-permute-start | bytes 6193160 | tf_op jit(solution)/shard_map/ppermute | solution.py:73
  447.7 116.8 %collective-permute-start.64 = (bf16[4,144,1792]{2,1,0:T(8,128)(2,1)}, bf16[4,144,1792]{2,1,0:T(8,128)(2,1)}, u32[]{:S(2)}, u32[]{:S(2)}) collective-permute-start(bf16[4,144,1792]{2,1,0:T(8,128)(2,1)} %bitcast_dynamic-update-slice_fusion.19), channel_id=1, source_target_pairs={{16,0},{0,16},{17,1},{1,17},{18,2},{2,18},{19,3},{3,19},{20,4},{4,... | collective-permute-start | bytes 6193160 | tf_op jit(solution)/shard_map/ppermute | solution.py:73
  539.4 44.1 %collective-permute-start.54 = (bf16[4,144,1792]{2,1,0:T(8,128)(2,1)}, bf16[4,144,1792]{2,1,0:T(8,128)(2,1)S(1)}, u32[]{:S(2)}, u32[]{:S(2)}) collective-permute-start(bf16[4,144,1792]{2,1,0:T(8,128)(2,1)} %bitcast_dynamic-update-slice_fusion.22), channel_id=1, source_target_pairs={{16,0},{0,16},{17,1},{1,17},{18,2},{2,18},{19,3},{3,19},{20,4},{4,... | collective-permute-start | bytes 6193160 | tf_op jit(solution)/shard_map/ppermute | solution.py:73
  544.3 39.4 %collective-permute-start.42 = (bf16[512,1152]{0,1:T(8,128)(2,1)S(1)}, bf16[512,1152]{0,1:T(8,128)(2,1)S(1)}, u32[]{:S(2)}, u32[]{:S(2)}) collective-permute-start(bf16[512,1152]{0,1:T(8,128)(2,1)S(1)} %multiply_convert_fusion.3), channel_id=1, source_target_pairs={{4,0},{0,4},{5,1},{1,5},{6,2},{2,6},{7,3},{3,7},{12,8},{8,12},{13,... | collective-permute-start | bytes 3538952 | tf_op jit(solution)/shard_map/ppermute | solution.py:73
  637.5 28.1 %collective-permute-start.77 = (bf16[512,1152]{0,1:T(8,128)(2,1)S(1)}, bf16[512,1152]{0,1:T(8,128)(2,1)S(1)}, u32[]{:S(2)}, u32[]{:S(2)}) collective-permute-start(bf16[512,1152]{0,1:T(8,128)(2,1)S(1)} %fusion.68), channel_id=1, source_target_pairs={{8,0},{0,8},{9,1},{1,9},{10,2},{2,10},{11,3},{3,11},{12,4},{4,12},... | collective-permute-start | bytes 3538952 | tf_op jit(solution)/shard_map/ppermute | solution.py:73
  670.5 27.5 %collective-permute-start.79 = (bf16[512,1152]{0,1:T(8,128)(2,1)}, bf16[512,1152]{0,1:T(8,128)(2,1)}, u32[]{:S(2)}, u32[]{:S(2)}) collective-permute-start(bf16[512,1152]{0,1:T(8,128)(2,1)} %fusion.61), channel_id=1, source_target_pairs={{8,0},{0,8},{9,1},{1,9},{10,2},{2,10},{11,3},{3,11},{12,4},{4,12},... | collective-permute-start | bytes 3538952 | tf_op jit(solution)/shard_map/ppermute | solution.py:73
  673.2 34.0 %collective-permute-start.78 = (bf16[512,1152]{0,1:T(8,128)(2,1)}, bf16[512,1152]{0,1:T(8,128)(2,1)}, u32[]{:S(2)}, u32[]{:S(2)}) collective-permute-start(bf16[512,1152]{0,1:T(8,128)(2,1)} %fusion.61), channel_id=1, source_target_pairs={{4,0},{0,4},{5,1},{1,5},{6,2},{2,6},{7,3},{3,7},{12,8},{8,12},{13,... | collective-permute-start | bytes 3538952 | tf_op jit(solution)/shard_map/ppermute | solution.py:73
  721.5 93.1 %collective-permute-start.146 = (bf16[4,144,1792]{2,1,0:T(8,128)(2,1)}, bf16[4,144,1792]{2,1,0:T(8,128)(2,1)}, u32[]{:S(2)}, u32[]{:S(2)}) collective-permute-start(bf16[4,144,1792]{2,1,0:T(8,128)(2,1)} %dynamic-slice_bitcast_fusion), channel_id=1, source_target_pairs={{16,0},{0,16},{17,1},{1,17},{18,2},{2,18},{19,3},{3,19},{20,4},{4,... | collective-permute-start | bytes 6193160 | tf_op jit(solution)/shard_map/ppermute | solution.py:73
  781.9 29.9 %collective-permute-start.82 = (bf16[512,1152]{0,1:T(8,128)(2,1)}, bf16[512,1152]{0,1:T(8,128)(2,1)}, u32[]{:S(2)}, u32[]{:S(2)}) collective-permute-start(bf16[512,1152]{0,1:T(8,128)(2,1)} %get-tuple-element.398), channel_id=1, source_target_pairs={{4,0},{0,4},{5,1},{1,5},{6,2},{2,6},{7,3},{3,7},{12,8},{8,12},{13,... | collective-permute-start | bytes 3538952 | tf_op jit(solution)/shard_map/ppermute | solution.py:73
  782.2 111.8 %collective-permute-start.81 = (bf16[512,1152]{0,1:T(8,128)(2,1)}, bf16[512,1152]{0,1:T(8,128)(2,1)S(1)}, u32[]{:S(2)}, u32[]{:S(2)}) collective-permute-start(bf16[512,1152]{0,1:T(8,128)(2,1)} %get-tuple-element.397), channel_id=1, source_target_pairs={{4,0},{0,4},{5,1},{1,5},{6,2},{2,6},{7,3},{3,7},{12,8},{8,12},{13,... | collective-permute-start | bytes 3538952 | tf_op jit(solution)/shard_map/ppermute | solution.py:73
  797.5 48.1 %collective-permute-start.118 = (bf16[4,144,1792]{2,1,0:T(8,128)(2,1)}, bf16[4,144,1792]{2,1,0:T(8,128)(2,1)}, u32[]{:S(2)}, u32[]{:S(2)}) collective-permute-start(bf16[4,144,1792]{2,1,0:T(8,128)(2,1)} %dynamic-slice_bitcast_fusion.1), channel_id=1, source_target_pairs={{16,0},{0,16},{17,1},{1,17},{18,2},{2,18},{19,3},{3,19},{20,4},{4,... | collective-permute-start | bytes 6193160 | tf_op jit(solution)/shard_map/ppermute | solution.py:73
  811.1 77.9 %collective-permute-start.108 = (bf16[4,144,1792]{2,1,0:T(8,128)(2,1)S(1)}, bf16[4,144,1792]{2,1,0:T(8,128)(2,1)S(1)}, u32[]{:S(2)}, u32[]{:S(2)}) collective-permute-start(bf16[4,144,1792]{2,1,0:T(8,128)(2,1)S(1)} %dynamic-slice_bitcast_fusion.2), channel_id=1, source_target_pairs={{16,0},{0,16},{17,1},{1,17},{18,2},{2,18},{19,3},{3,19},{20,4},{4,... | collective-permute-start | bytes 6193160 | tf_op jit(solution)/shard_map/ppermute | solution.py:73
  813.6 81.9 %collective-permute-start.83 = (bf16[512,1152]{0,1:T(8,128)(2,1)S(1)}, bf16[512,1152]{0,1:T(8,128)(2,1)S(1)}, u32[]{:S(2)}, u32[]{:S(2)}) collective-permute-start(bf16[512,1152]{0,1:T(8,128)(2,1)S(1)} %fusion.66), channel_id=1, source_target_pairs={{8,0},{0,8},{9,1},{1,9},{10,2},{2,10},{11,3},{3,11},{12,4},{4,12},... | collective-permute-start | bytes 3538952 | tf_op jit(solution)/shard_map/ppermute | solution.py:73
  817.9 154.6 %collective-permute-start.147 = (bf16[144,1792]{1,0:T(8,128)(2,1)}, bf16[144,1792]{1,0:T(8,128)(2,1)}, u32[]{:S(2)}, u32[]{:S(2)}) collective-permute-start(bf16[144,1792]{1,0:T(8,128)(2,1)} %get-tuple-element.417), channel_id=1, source_target_pairs={{0,1},{4,5},{8,9},{12,13},{16,17},{20,21},{24,25},{28,29}} | collective-permute-start | bytes 1548296 | tf_op jit(solution)/shard_map/ppermute | solution.py:131
  845.6 148.3 %collective-permute-start.150 = (bf16[144,1792]{1,0:T(8,128)(2,1)}, bf16[144,1792]{1,0:T(8,128)(2,1)}, u32[]{:S(2)}, u32[]{:S(2)}) collective-permute-start(bf16[144,1792]{1,0:T(8,128)(2,1)} %get-tuple-element.418), channel_id=1, source_target_pairs={{3,2},{7,6},{11,10},{15,14},{19,18},{23,22},{27,26},{31,30}} | collective-permute-start | bytes 1548296 | tf_op jit(solution)/shard_map/ppermute | solution.py:132
  889.0 86.5 %collective-permute-start.119 = (bf16[144,1792]{1,0:T(8,128)(2,1)}, bf16[144,1792]{1,0:T(8,128)(2,1)}, u32[]{:S(2)}, u32[]{:S(2)}) collective-permute-start(bf16[144,1792]{1,0:T(8,128)(2,1)} %get-tuple-element.421), channel_id=1, source_target_pairs={{0,1},{4,5},{8,9},{12,13},{16,17},{20,21},{24,25},{28,29}} | collective-permute-start | bytes 1548296 | tf_op jit(solution)/shard_map/ppermute | solution.py:131
  893.9 115.5 %collective-permute-start.122 = (bf16[144,1792]{1,0:T(8,128)(2,1)}, bf16[144,1792]{1,0:T(8,128)(2,1)}, u32[]{:S(2)}, u32[]{:S(2)}) collective-permute-start(bf16[144,1792]{1,0:T(8,128)(2,1)} %get-tuple-element.422), channel_id=1, source_target_pairs={{3,2},{7,6},{11,10},{15,14},{19,18},{23,22},{27,26},{31,30}} | collective-permute-start | bytes 1548296 | tf_op jit(solution)/shard_map/ppermute | solution.py:132
  895.5 82.0 %collective-permute-start.109 = (bf16[144,1792]{1,0:T(8,128)(2,1)}, bf16[144,1792]{1,0:T(8,128)(2,1)}, u32[]{:S(2)}, u32[]{:S(2)}) collective-permute-start(bf16[144,1792]{1,0:T(8,128)(2,1)} %get-tuple-element.425), channel_id=1, source_target_pairs={{0,1},{4,5},{8,9},{12,13},{16,17},{20,21},{24,25},{28,29}} | collective-permute-start | bytes 1548296 | tf_op jit(solution)/shard_map/ppermute | solution.py:131
  985.2 31.7 %collective-permute-start.112 = (bf16[144,1792]{1,0:T(8,128)(2,1)S(1)}, bf16[144,1792]{1,0:T(8,128)(2,1)S(1)}, u32[]{:S(2)}, u32[]{:S(2)}) collective-permute-start(bf16[144,1792]{1,0:T(8,128)(2,1)S(1)} %copy-done.92), channel_id=1, source_target_pairs={{3,2},{7,6},{11,10},{15,14},{19,18},{23,22},{27,26},{31,30}} | collective-permute-start | bytes 1548296 | tf_op jit(solution)/shard_map/ppermute | solution.py:132
  993.8 31.1 %collective-permute-start.110 = (bf16[144,1792]{1,0:T(8,128)(2,1)S(1)}, bf16[144,1792]{1,0:T(8,128)(2,1)S(1)}, u32[]{:S(2)}, u32[]{:S(2)}) collective-permute-start(bf16[144,1792]{1,0:T(8,128)(2,1)S(1)} %fusion.113), channel_id=1, source_target_pairs={{0,1},{1,2},{4,5},{5,6},{8,9},{9,10},{12,13},{13,14},{16,17},{17,1... | collective-permute-start | bytes 1548296 | tf_op jit(solution)/shard_map/ppermute | solution.py:131
  1002.9 56.4 %collective-permute-start.85 = (bf16[512,512]{1,0:T(8,128)(2,1)S(1)}, bf16[512,512]{1,0:T(8,128)(2,1)S(1)}, u32[]{:S(2)}, u32[]{:S(2)}) collective-permute-start(bf16[512,512]{1,0:T(8,128)(2,1)S(1)} %get-tuple-element.409), channel_id=1, source_target_pairs={{0,1},{1,2},{4,5},{5,6},{8,9},{9,10},{12,13},{13,14},{16,17},{17,1... | collective-permute-start | bytes 1572872 | tf_op jit(solution)/shard_map/ppermute | solution.py:131
  1009.4 50.5 %collective-permute-start.88 = (bf16[512,512]{1,0:T(8,128)(2,1)S(1)}, bf16[512,512]{1,0:T(8,128)(2,1)S(1)}, u32[]{:S(2)}, u32[]{:S(2)}) collective-permute-start(bf16[512,512]{1,0:T(8,128)(2,1)S(1)} %get-tuple-element.410), channel_id=1, source_target_pairs={{2,1},{3,2},{6,5},{7,6},{10,9},{11,10},{14,13},{15,14},{18,17},{19... | collective-permute-start | bytes 1572872 | tf_op jit(solution)/shard_map/ppermute | solution.py:132
  1025.0 71.4 %collective-permute-start.151 = (bf16[144,1792]{1,0:T(8,128)(2,1)S(1)}, bf16[144,1792]{1,0:T(8,128)(2,1)S(1)}, u32[]{:S(2)}, u32[]{:S(2)}) collective-permute-start(bf16[144,1792]{1,0:T(8,128)(2,1)S(1)} %get-tuple-element.416), channel_id=1, source_target_pairs={{2,1},{3,2},{6,5},{7,6},{10,9},{11,10},{14,13},{15,14},{18,17},{19... | collective-permute-start | bytes 1548296 | tf_op jit(solution)/shard_map/ppermute | solution.py:132
  1054.7 130.1 %collective-permute-start.149 = (bf16[144,1792]{1,0:T(8,128)(2,1)}, bf16[144,1792]{1,0:T(8,128)(2,1)}, u32[]{:S(2)}, u32[]{:S(2)}) collective-permute-start(bf16[144,1792]{1,0:T(8,128)(2,1)} %get-tuple-element.415), channel_id=1, source_target_pairs={{0,1},{1,2},{2,3},{4,5},{5,6},{6,7},{8,9},{9,10},{10,11},{12,13},{... | collective-permute-start | bytes 1548296 | tf_op jit(solution)/shard_map/ppermute | solution.py:131
  1058.5 42.7 %collective-permute-start.123 = (bf16[144,1792]{1,0:T(8,128)(2,1)S(1)}, bf16[144,1792]{1,0:T(8,128)(2,1)S(1)}, u32[]{:S(2)}, u32[]{:S(2)}) collective-permute-start(bf16[144,1792]{1,0:T(8,128)(2,1)S(1)} %get-tuple-element.420), channel_id=1, source_target_pairs={{2,1},{3,2},{6,5},{7,6},{10,9},{11,10},{14,13},{15,14},{18,17},{19... | collective-permute-start | bytes 1548296 | tf_op jit(solution)/shard_map/ppermute | solution.py:132
  1089.7 102.6 %collective-permute-start.121 = (bf16[144,1792]{1,0:T(8,128)(2,1)}, bf16[144,1792]{1,0:T(8,128)(2,1)}, u32[]{:S(2)}, u32[]{:S(2)}) collective-permute-start(bf16[144,1792]{1,0:T(8,128)(2,1)} %get-tuple-element.419), channel_id=1, source_target_pairs={{0,1},{1,2},{2,3},{4,5},{5,6},{6,7},{8,9},{9,10},{10,11},{12,13},{... | collective-permute-start | bytes 1548296 | tf_op jit(solution)/shard_map/ppermute | solution.py:131
  1103.4 99.7 %collective-permute-start.111 = (bf16[144,1792]{1,0:T(8,128)(2,1)}, bf16[144,1792]{1,0:T(8,128)(2,1)}, u32[]{:S(2)}, u32[]{:S(2)}) collective-permute-start(bf16[144,1792]{1,0:T(8,128)(2,1)} %get-tuple-element.423), channel_id=1, source_target_pairs={{0,1},{1,2},{2,3},{4,5},{5,6},{6,7},{8,9},{9,10},{10,11},{12,13},{... | collective-permute-start | bytes 1548296 | tf_op jit(solution)/shard_map/ppermute | solution.py:131
  1117.9 68.7 %collective-permute-start.152 = (bf16[144,1792]{1,0:T(8,128)(2,1)}, bf16[144,1792]{1,0:T(8,128)(2,1)}, u32[]{:S(2)}, u32[]{:S(2)}) collective-permute-start(bf16[144,1792]{1,0:T(8,128)(2,1)} %fusion.100), channel_id=1, source_target_pairs={{1,0},{2,1},{3,2},{5,4},{6,5},{7,6},{9,8},{10,9},{11,10},{13,12},{... | collective-permute-start | bytes 1548296 | tf_op jit(solution)/shard_map/ppermute | solution.py:132
  1125.3 68.5 %collective-permute-start.124 = (bf16[144,1792]{1,0:T(8,128)(2,1)}, bf16[144,1792]{1,0:T(8,128)(2,1)}, u32[]{:S(2)}, u32[]{:S(2)}) collective-permute-start(bf16[144,1792]{1,0:T(8,128)(2,1)} %fusion.106), channel_id=1, source_target_pairs={{1,0},{2,1},{3,2},{5,4},{6,5},{7,6},{9,8},{10,9},{11,10},{13,12},{... | collective-permute-start | bytes 1548296 | tf_op jit(solution)/shard_map/ppermute | solution.py:132
  1184.7 163.1 %collective-permute-start.145 = (bf16[36,512]{1,0:T(8,128)(2,1)}, bf16[36,512]{1,0:T(8,128)(2,1)S(1)}, u32[]{:S(2)}, u32[]{:S(2)}) collective-permute-start(bf16[36,512]{1,0:T(8,128)(2,1)} %fusion.202), channel_id=1, source_target_pairs={{16,0},{0,16},{17,1},{1,17},{18,2},{2,18},{19,3},{3,19},{20,4},{4,... | collective-permute-start | bytes 110600 | tf_op jit(solution)/shard_map/ppermute | solution.py:73
  1186.6 159.8 %collective-permute-start.136 = (bf16[36,512]{1,0:T(8,128)(2,1)}, bf16[36,512]{1,0:T(8,128)(2,1)}, u32[]{:S(2)}, u32[]{:S(2)}) collective-permute-start(bf16[36,512]{1,0:T(8,128)(2,1)} %fusion.200), channel_id=1, source_target_pairs={{8,0},{0,8},{9,1},{1,9},{10,2},{2,10},{11,3},{3,11},{12,4},{4,12},... | collective-permute-start | bytes 110600 | tf_op jit(solution)/shard_map/ppermute | solution.py:73
  1193.8 55.6 %collective-permute-start.90 = (bf16[2,4,2,36,768]{4,1,3,2,0:T(4,128)(2,1)}, bf16[2,4,2,36,768]{4,1,3,2,0:T(4,128)(2,1)}, u32[]{:S(2)}, u32[]{:S(2)}) collective-permute-start(bf16[2,4,2,36,768]{4,1,3,2,0:T(4,128)(2,1)} %copy.1997), channel_id=1, source_target_pairs={{4,0},{0,4},{5,1},{1,5},{6,2},{2,6},{7,3},{3,7},{12,8},{8,12},{13,... | collective-permute-start | bytes 2654216 | tf_op jit(solution)/shard_map/ppermute | solution.py:73
  1203.1 49.6 %collective-permute-start.99 = (bf16[2,4,2,36,896]{4,1,3,2,0:T(4,128)(2,1)}, bf16[2,4,2,36,896]{4,1,3,2,0:T(4,128)(2,1)}, u32[]{:S(2)}, u32[]{:S(2)}) collective-permute-start(bf16[2,4,2,36,896]{4,1,3,2,0:T(4,128)(2,1)} %copy.2010), channel_id=1, source_target_pairs={{4,0},{0,4},{5,1},{1,5},{6,2},{2,6},{7,3},{3,7},{12,8},{8,12},{13,... | collective-permute-start | bytes 3096584 | tf_op jit(solution)/shard_map/ppermute | solution.py:73
  (274 other events, 4047.6 us)

commit v2 on v1

v2 whole, which is shorter than its diff:
```python
import numpy as np
import jax
import jax.numpy as jnp
from jax import lax
from jax.experimental import pallas as pl
from jax.experimental.pallas import tpu as pltpu
from jax.sharding import PartitionSpec as P

H = 4
HD = 256
FF = 6912
STEP = 10


NORM_EPS = 1e-06
ROPE_BASE = 1000000.0
QUERY_SCALE = 0.0625
BETA_ONE = 0.9
BETA_TWO = 0.95
ADAM_EPS = 1e-08
RATE_WEIGHTS = 0.03
RATE_GAINS = 0.1
WEIGHT_DECAY = 0.1
NEG_LARGE = -1e30

LANES = 128
Q_COLS = H * HD
START_GATE = Q_COLS + 2 * HD
START_OUT = START_GATE + 2 * FF
START_DOWN = START_OUT + Q_COLS
BF = jnp.bfloat16
F32 = jnp.float32


def block_positions(slots, rows, count):
    half_rows = rows // 2
    device = slots // rows
    within = slots % rows
    block = jnp.where(within < half_rows, device, 2 * count - 1 - device)
    return block * half_rows + within % half_rows


def rms_gain(values, gain):
    return values * lax.rsqrt(jnp.mean(values * values, axis=-1, keepdims=True) + NORM_EPS) * gain


def rotate(values, positions):
    half_dim = values.shape[-1] // 2
    freqs = jnp.power(ROPE_BASE, -2.0 * jnp.arange(half_dim).astype(jnp.float32) / values.shape[-1])
    angles = positions.astype(jnp.float32)[:, None] * freqs[None, :]
    cosine = jnp.cos(angles)[:, None, :]
    sine = jnp.sin(angles)[:, None, :]
    first = values[..., :half_dim]
    second = values[..., half_dim:]
    return jnp.concatenate(
        [first * cosine - second * sine, second * cosine + first * sine], axis=-1
    )


def adamw(weight, grad, first, second, rate, decay):
    first_new = BETA_ONE * first + (1.0 - BETA_ONE) * grad
    second_new = BETA_TWO * second + (1.0 - BETA_TWO) * grad * grad
    update = (
        first_new
        / (1.0 - BETA_ONE**STEP)
        / (jnp.sqrt(second_new / (1.0 - BETA_TWO**STEP)) + ADAM_EPS)
    )
    return (weight - rate * (update + decay * weight), first_new, second_new)


def shift(values, axis, distance):
    count = lax.axis_size(axis)
    return lax.ppermute(values, axis, [((i + distance) % count, i) for i in range(count)])


def flip(values, bit):
    return lax.ppermute(values, "dp", [(i ^ bit, i) for i in range(lax.axis_size("dp"))])


def my_bit(bit):
    return (lax.axis_index("dp") // bit) % 2


def chip_orders():
    bits = [1 << i for i in range(1, lax.axis_size("dp").bit_length() - 1)]
    return bits, bits[::-1]


def bit_orders():
    return tuple(bits + [1] for bits in chip_orders())


def place_blocks(blocks, axis):
    count, me = len(blocks), lax.axis_index(axis)
    return jnp.stack([lax.select_n((j - me) % count, *blocks) for j in range(count)])


def gather_direct(values, axis):
    count = lax.axis_size(axis)
    blocks = [values] + [shift(values, axis, distance) for distance in range(1, count)]
    return place_blocks(blocks, axis)


def gather_line(values, axis):
    count, me = lax.axis_size(axis), lax.axis_index(axis)
    below, above = [], []
    up, down = values, values
    for step in range(1, count):
        up = lax.ppermute(up, axis, [(i, i + 1) for i in range(step - 1, count - 1)])
        down = lax.ppermute(down, axis, [(i, i - 1) for i in range(1, count - step + 1)])
        below.append(up)
        above.append(down)
    blocks = [values]
    for offset in range(1, count):
        blocks.append(
            jnp.where(me + offset < count, above[offset - 1], below[count - offset - 1])
        )
    return place_blocks(blocks, axis)


def scatter_direct(parts, axis):
    count, me = lax.axis_size(axis), lax.axis_index(axis)
    total = lax.dynamic_index_in_dim(parts, me, 0, keepdims=False).astype(F32)
    for distance in range(1, count):
        mine = lax.dynamic_index_in_dim(parts, (me - distance) % count, 0, keepdims=False)
        total = total + shift(mine.astype(BF), axis, distance).astype(F32)
    return total


def scatter_line(parts, axis):
    count, me = lax.axis_size(axis), lax.axis_index(axis)

    def own(index):
        return lax.dynamic_index_in_dim(parts, jnp.clip(index, 0, count - 1), 0, keepdims=False)

    up = down = None
    for step in range(1, count):
        far = count - step
        up_out = own(me + far).astype(F32)
        down_out = own(me - far).astype(F32)
        if step > 1:
            up_out, down_out = up_out + up.astype(F32), down_out + down.astype(F32)
        up = lax.ppermute(up_out.astype(BF), axis, [(i, i + 1) for i in range(step)])
        down = lax.ppermute(
            down_out.astype(BF), axis, [(i, i - 1) for i in range(count - step, count)]
        )
    return own(me).astype(F32) + up.astype(F32) + down.astype(F32)


def split_cols(cols):
    half = cols // 2 // LANES * LANES
    return ((0, half), (half, cols))


def gather_rows(shard):
    rows, cols = shard.shape
    z_block = gather_direct(shard, "ctx")
    z_count = z_block.shape[0]
    halves = []
    for (low, high), bits in zip(split_cols(cols), bit_orders()):
        part = z_block[..., low:high]
        for bit in bits:
            got, mine = flip(part, bit), my_bit(bit)
            part = jnp.stack([jnp.where(mine == 0, part, got), jnp.where(mine == 0, got, part)])
        axes = bits[::-1]
        order = [axes.index(bit) for bit in sorted(bits, reverse=True)]
        count = len(bits)
        part = part.transpose([count] + order + [count + 1, count + 2])
        halves.append(part.reshape(z_count, -1, rows, high - low))
    return jnp.concatenate(halves, axis=-1).reshape(-1, cols)


def scatter_rows(parts):
    z_count, dp_count, rows, cols = parts.shape
    halves = []
    for (low, high), bits in zip(split_cols(cols), bit_orders()):
        part = parts[..., low:high]
        part = part.reshape((z_count,) + (2,) * len(bits) + (rows, high - low))
        left = sorted(bits, reverse=True)
        for bit in bits[::-1]:
            dim, mine = 1 + left.index(bit), my_bit(bit)
            keep = lax.dynamic_index_in_dim(part, mine, dim, keepdims=False)
            send = lax.dynamic_index_in_dim(part, 1 - mine, dim, keepdims=False)
            part = (keep.astype(F32) + flip(send, bit).astype(F32)).astype(BF)
            left.remove(bit)
        halves.append(part)
    return scatter_direct(jnp.concatenate(halves, axis=-1), "ctx")


def spread(values):
    half = values.shape[0] // 2
    out = []
    for part, bits in zip((values[:half], values[half:]), chip_orders()):
        for bit in bits:
            part = jnp.concatenate([part, flip(part, bit)], axis=0)
        out.append(part)
    return jnp.concatenate(out, axis=0)


def collect(parts):
    half = parts.shape[0] // 2
    out = []
    for part, bits in zip((parts[:half], parts[half:]), chip_orders()):
        for bit in bits[::-1]:
            count = part.shape[0] // 2
            got = flip(part[count:].astype(BF), bit)
            part = part[:count].astype(F32) + got.astype(F32)
        out.append(part)
    return jnp.concatenate(out, axis=0)


def pad_cols(values, cols):
    return jnp.pad(values, ((0, 0), (0, cols - values.shape[1])))


VMEM_LIMIT = 60 * 1024 * 1024
NT = (((1,), (1,)), ((), ()))
TN = (((0,), (0,)), ((), ()))


def dot(left, right, dims=(((1,), (0,)), ((), ()))):
    return lax.dot_general(left, right, dims, preferred_element_type=F32)


def whole(shape):
    return pl.BlockSpec(shape, lambda i: (0,) * len(shape))


def tie_kernel(value_ref, other_ref, out_ref):
    del value_ref, other_ref, out_ref


def tie(value, other):
    return pl.pallas_call(
        tie_kernel,
        out_shape=jax.ShapeDtypeStruct(value.shape, value.dtype),
        in_specs=[pl.BlockSpec(memory_space=pl.ANY)] * 2,
        out_specs=pl.BlockSpec(memory_space=pl.ANY),
        input_output_aliases={0: 0},
        compiler_params=pltpu.CompilerParams(has_side_effects=True),
    )(value, other)


def key_row(block, rows, count):
    first = block * 2 * rows
    second = (2 * count - 1 - block) * 2 * rows + rows
    return pl.multiple_of(jnp.where(block < count, first, second), rows)


def key_bias(block, rows, length):
    spots = block * rows + lax.broadcasted_iota(jnp.int32, (1, rows), 1)
    return jnp.where(spots < length, 0.0, NEG_LARGE)


def attend_kernel(info_ref, query_ref, kv_ref, mixed_ref, total_ref, acc_ref, sum_ref):
    rows = query_ref.shape[0]
    count = kv_ref.shape[0] // (2 * rows)
    place, length = info_ref[0], info_ref[1]
    mine = jnp.where(pl.program_id(0) == 0, place, 2 * count - 1 - place)
    acc_ref[...] = jnp.zeros_like(acc_ref)
    sum_ref[...] = jnp.zeros_like(sum_ref)

    def step(block, causal):
        at = pl.ds(key_row(block, rows, count), rows)
        keys, values = kv_ref[at, :HD], kv_ref[at, HD:]
        bias = key_bias(block, rows, length)
        for head in range(H):
            cols = slice(head * HD, (head + 1) * HD)
            scores = dot(query_ref[:, cols], keys, NT) + bias
            weight = jnp.exp(scores)
            if causal:
                row = lax.broadcasted_iota(jnp.int32, (rows, rows), 0)
                col = lax.broadcasted_iota(jnp.int32, (rows, rows), 1)
                weight = jnp.where(col <= row, weight, 0.0)
            parts = weight[:, :LANES]
            for low in range(LANES, rows, LANES):
                parts = parts + weight[:, low : low + LANES]
            sum_ref[:, head * LANES : (head + 1) * LANES] += parts
            acc_ref[:, cols] += dot(weight.astype(BF), values)

    def loop(block, carry):
        step(block, False)
        return carry

    lax.fori_loop(0, mine, loop, 0)
    step(mine, True)
    for head in range(H):
        cols = slice(head * HD, (head + 1) * HD)
        total = jnp.sum(sum_ref[:, head * LANES : (head + 1) * LANES], axis=1, keepdims=True)
        inverse = 1.0 / total
        mixed_ref[:, cols] = (acc_ref[:, cols] * inverse).astype(BF)
        total_ref[:, head * LANES : (head + 1) * LANES] = jnp.broadcast_to(
            inverse, (rows, LANES)
        )


def attend(info, query, kv):
    half = query.shape[0] // 2
    spec = lambda cols: pl.BlockSpec((half, cols), lambda i, info: (i, 0))
    return pl.pallas_call(
        attend_kernel,
        grid_spec=pltpu.PrefetchScalarGridSpec(
            num_scalar_prefetch=1,
            grid=(2,),
            in_specs=[spec(Q_COLS), pl.BlockSpec(kv.shape, lambda i, info: (0, 0))],
            out_specs=[spec(Q_COLS), spec(H * LANES)],
            scratch_shapes=[pltpu.VMEM((half, Q_COLS), F32), pltpu.VMEM((half, H * LANES), F32)],
        ),
        out_shape=[
            jax.ShapeDtypeStruct((2 * half, Q_COLS), BF),
            jax.ShapeDtypeStruct((2 * half, H * LANES), F32),
        ],
        compiler_params=pltpu.CompilerParams(vmem_limit_bytes=VMEM_LIMIT),
        cost_estimate=pl.CostEstimate(
            flops=4 * half * half * Q_COLS * 9, bytes_accessed=8 << 20, transcendentals=0
        ),
    )(info, query, kv)


def attend_back_kernel(
    info_ref, query_ref, grad_ref, mixed_ref, total_ref, kv_ref, dq_ref, dkv_ref, acc_ref, dq_acc
):
    rows = query_ref.shape[0]
    count = kv_ref.shape[0] // (2 * rows)
    place, length = info_ref[0], info_ref[1]
    step_id = pl.program_id(0)
    mine = jnp.where(step_id == 0, place, 2 * count - 1 - place)

    @pl.when(step_id == 0)
    def _():
        acc_ref[...] = jnp.zeros_like(acc_ref)

    dq_acc[...] = jnp.zeros_like(dq_acc)
    delta, inverse = [], []
    for head in range(H):
        cols = slice(head * HD, (head + 1) * HD)
        delta.append(
            jnp.sum(
                grad_ref[:, cols].astype(F32) * mixed_ref[:, cols].astype(F32),
                axis=1,
                keepdims=True,
            )
        )
        inverse.append(total_ref[:, head * LANES : head * LANES + 1])

    def step(block, causal):
        at = pl.ds(key_row(block, rows, count), rows)
        keys, values = kv_ref[at, :HD], kv_ref[at, HD:]
        bias = key_bias(block, rows, length)
        dk = jnp.zeros((rows, HD), F32)
        dv = jnp.zeros((rows, HD), F32)
        for head in range(H):
            cols = slice(head * HD, (head + 1) * HD)
            query, grad = query_ref[:, cols], grad_ref[:, cols]
            weight = jnp.exp(dot(query, keys, NT) + bias) * inverse[head]
            if causal:
                row = lax.broadcasted_iota(jnp.int32, (rows, rows), 0)
                col = lax.broadcasted_iota(jnp.int32, (rows, rows), 1)
                weight = jnp.where(col <= row, weight, 0.0)
            score = (weight * (dot(grad, values, NT) - delta[head])).astype(BF)
            dq_acc[:, cols] += dot(score, keys)
            dk = dk + dot(score, query, TN)
            dv = dv + dot(weight.astype(BF), grad, TN)
        acc_ref[at, :HD] += dk
        acc_ref[at, HD:] += dv

    def loop(block, carry):
        step(block, False)
        return carry

    lax.fori_loop(0, mine, loop, 0)
    step(mine, True)
    dq_ref[...] = dq_acc[...]

    @pl.when(step_id == pl.num_programs(0) - 1)
    def _():
        dkv_ref[...] = acc_ref[...].astype(BF)


def attend_back(info, query, grad, mixed, total, kv):
    half = query.shape[0] // 2
    spec = lambda cols: pl.BlockSpec((half, cols), lambda i, info: (i, 0))
    full = pl.BlockSpec(kv.shape, lambda i, info: (0, 0))
    return pl.pallas_call(
        attend_back_kernel,
        grid_spec=pltpu.PrefetchScalarGridSpec(
            num_scalar_prefetch=1,
            grid=(2,),
            in_specs=[spec(Q_COLS), spec(Q_COLS), spec(Q_COLS), spec(H * LANES), full],
            out_specs=[spec(Q_COLS), full],
            scratch_shapes=[pltpu.VMEM(kv.shape, F32), pltpu.VMEM((half, Q_COLS), F32)],
        ),
        out_shape=[
            jax.ShapeDtypeStruct((2 * half, Q_COLS), F32),
            jax.ShapeDtypeStruct(kv.shape, BF),
        ],
        compiler_params=pltpu.CompilerParams(vmem_limit_bytes=VMEM_LIMIT),
        cost_estimate=pl.CostEstimate(
            flops=10 * half * half * Q_COLS * 9, bytes_accessed=12 << 20, transcendentals=0
        ),
    )(info, query, grad, mixed, total, kv)


GELU_A = 0.7978845608028654
GELU_B = 0.044715


def mlp_kernel(x_ref, own_ref, other_ref, part_ref, gate_up_ref, hidden_ref):
    units = own_ref.shape[1] // 3
    total = None
    for k, w_ref in enumerate((own_ref, other_ref)):
        both = dot(x_ref[...], w_ref[:, : 2 * units])
        gate_up_ref[:, k * 2 * units : (k + 1) * 2 * units] = both.astype(BF)
        gate, up = both[:, :units], both[:, units:]
        inner = jnp.tanh(GELU_A * gate * (1.0 + GELU_B * gate * gate))
        hidden = (0.5 * gate * (1.0 + inner) * up).astype(BF)
        hidden_ref[:, k * units : (k + 1) * units] = hidden
        part = dot(hidden, w_ref[:, 2 * units :], NT)
        total = part if total is None else total + part
    part_ref[...] = total.astype(BF)


def mlp_tile(rows):
    return min(rows, 512)


def mlp_forward(x, own, other):
    rows, width = x.shape
    units = own.shape[1] // 3
    tile = mlp_tile(rows)
    spec = lambda cols: pl.BlockSpec((tile, cols), lambda i: (i, 0))
    return pl.pallas_call(
        mlp_kernel,
        grid=(rows // tile,),
        in_specs=[spec(width), whole(own.shape), whole(own.shape)],
        out_specs=[spec(width), spec(4 * units), spec(2 * units)],
        out_shape=[
            jax.ShapeDtypeStruct((rows, width), BF),
            jax.ShapeDtypeStruct((rows, 4 * units), BF),
            jax.ShapeDtypeStruct((rows, 2 * units), BF),
        ],
        compiler_params=pltpu.CompilerParams(vmem_limit_bytes=VMEM_LIMIT),
        cost_estimate=pl.CostEstimate(
            flops=12 * rows * width * units, bytes_accessed=32 << 20, transcendentals=0
        ),
    )(x, own, other)


def mlp_back_kernel(grad_ref, gate_up_ref, own_ref, other_ref, part_ref, gate_up_grad_ref):
    units = own_ref.shape[1] // 3
    total = None
    for k, w_ref in enumerate((own_ref, other_ref)):
        base = k * 2 * units
        hidden_grad = dot(grad_ref[...], w_ref[:, 2 * units :])
        gate = gate_up_ref[:, base : base + units].astype(F32)
        up = gate_up_ref[:, base + units : base + 2 * units].astype(F32)
        square = gate * gate
        inner = jnp.tanh(GELU_A * gate * (1.0 + GELU_B * square))
        half = 0.5 * (1.0 + inner)
        slope = half + 0.5 * gate * (1.0 - inner * inner) * (
            GELU_A * (1.0 + 3.0 * GELU_B * square)
        )
        gate_grad = (hidden_grad * up * slope).astype(BF)
        up_grad = (hidden_grad * (gate * half)).astype(BF)
        gate_up_grad_ref[:, base : base + units] = gate_grad
        gate_up_grad_ref[:, base + units : base + 2 * units] = up_grad
        part = dot(gate_up_grad_ref[:, base : base + 2 * units], w_ref[:, : 2 * units], NT)
        total = part if total is None else total + part
    part_ref[...] = total.astype(BF)


def mlp_backward(grad, gate_up, own, other):
    rows, width = grad.shape
    units = own.shape[1] // 3
    tile = mlp_tile(rows)
    spec = lambda cols: pl.BlockSpec((tile, cols), lambda i: (i, 0))
    return pl.pallas_call(
        mlp_back_kernel,
        grid=(rows // tile,),
        in_specs=[spec(width), spec(4 * units), whole(own.shape), whole(own.shape)],
        out_specs=[spec(width), spec(4 * units)],
        out_shape=[
            jax.ShapeDtypeStruct((rows, width), BF),
            jax.ShapeDtypeStruct((rows, 4 * units), BF),
        ],
        compiler_params=pltpu.CompilerParams(vmem_limit_bytes=VMEM_LIMIT),
        cost_estimate=pl.CostEstimate(
            flops=12 * rows * width * units, bytes_accessed=32 << 20, transcendentals=0
        ),
    )(grad, gate_up, own, other)


def body(
    layer_input,
    cotangent,
    lengths,
    weights,
    norm_gains,
    head_gains,
    moment_weights,
    moment_gains,
    moment_head,
    square_weights,
    square_gains,
    square_head,
):
    rows = weights.shape[0]
    head_rows = head_gains.shape[0]
    width = layer_input.shape[1]
    dp_count, z_count = lax.axis_size("dp"), lax.axis_size("ctx")
    units = -(-FF // (dp_count * LANES)) * LANES

    weights_low = weights.astype(BF)
    gain_cols = jnp.zeros((max(rows, head_rows), LANES), BF)
    gain_cols = gain_cols.at[:rows, :4].set(norm_gains.astype(BF))
    gain_cols = gain_cols.at[:head_rows, 4:6].set(head_gains.astype(BF))[:rows]
    first_shard = jnp.concatenate([weights_low[:, :START_GATE], gain_cols], axis=1)
    mlp_shard = jnp.concatenate(
        [
            pad_cols(weights_low[:, start : start + FF], dp_count * units)
            .reshape(rows, dp_count, units)
            .transpose(1, 0, 2)
            for start in (START_GATE, START_GATE + FF, START_DOWN)
        ],
        axis=2,
    )
    mlp_block = lax.all_to_all(mlp_shard, "dp", split_axis=0, concat_axis=0, tiled=True)
    mlp_block = mlp_block.reshape(dp_count * rows, 3 * units)
    w_own = lax.all_gather(mlp_block, "ctx", axis=0, tiled=True)
    w_other = flip(w_own, 1)
    first_full = gather_rows(first_shard)
    w_qkv = first_full[:, :START_GATE]
    gain_part = first_full[:, START_GATE:].astype(F32)
    gain_f = 1.0 + gain_part[:, :4]
    head_f = gain_part.reshape(z_count, dp_count, rows, LANES)[:, :, :head_rows, 4:6]
    head_f = 1.0 + head_f.transpose(1, 0, 2, 3).reshape(HD, 2)
    w_out = gather_rows(tie(weights_low[:, START_OUT:START_DOWN], first_full))

    order = np.arange(width).reshape(dp_count, z_count, rows).transpose(1, 0, 2).reshape(width)
    place = (jnp.arange(width)[:, None] == jnp.asarray(order)[None, :]).astype(BF)

    tok_rows = layer_input.shape[0]
    ctx_count = z_count
    local_slots = lax.axis_index("ctx") * tok_rows + jnp.arange(tok_rows, dtype=jnp.int32)
    positions = block_positions(local_slots, tok_rows, ctx_count)
    seq_length = lengths[0]
    row_valid = positions < seq_length
    inputs = jnp.dot(layer_input, place, preferred_element_type=F32)
    cot = jnp.dot(cotangent, place, preferred_element_type=F32)
    normed_in, pull_in = jax.vjp(rms_gain, inputs, gain_f[:, 0])
    normed_low = normed_in.astype(BF)
    projected = jnp.dot(normed_low, w_qkv, preferred_element_type=F32)

    def query_key(query_raw, key_raw, head_arg):
        query_out = (
            rotate(rms_gain(query_raw.reshape(tok_rows, H, HD), head_arg[:, 0]), positions)
            * QUERY_SCALE
        )
        key_out = rotate(rms_gain(key_raw[:, None, :], head_arg[:, 1]), positions)[:, 0]
        return (query_out, key_out)

    (queries, keys), pull_qk = jax.vjp(
        query_key, projected[:, :Q_COLS], projected[:, Q_COLS : Q_COLS + HD], head_f
    )
    query_low = queries.astype(BF)
    key_low = keys.astype(BF)
    value_low = projected[:, Q_COLS + HD :].astype(BF)
    key_value = gather_line(jnp.concatenate([key_low, value_low], axis=1), "ctx")
    key_value = key_value.reshape(z_count * tok_rows, 2 * HD)
    info = jnp.stack([lax.axis_index("ctx"), seq_length]).astype(jnp.int32)
    query_low = query_low.reshape(tok_rows, Q_COLS)
    mixed_low, inverse_total = attend(info, query_low, key_value)
    attn_proj = jnp.einsum("tc,dc->td", mixed_low, w_out, preferred_element_type=F32)
    post_attn, pull_attn = jax.vjp(rms_gain, attn_proj, gain_f[:, 1])
    residual_mid = inputs + post_attn
    normed_mid, pull_mid = jax.vjp(rms_gain, residual_mid, gain_f[:, 2])

    mid_low = normed_mid.astype(BF)
    out_grad = cot * row_valid[:, None].astype(F32)
    chunks = 2
    size = tok_rows // chunks
    spans = [slice(i * size, (i + 1) * size) for i in range(chunks)]
    mids = [spread(mid_low[span]) for span in spans]
    forward = [mlp_forward(mid, w_own, w_other) for mid in mids]
    grad_three = 0.0
    output_low, mlp_grads = [], []
    for span, (part, _, _) in zip(spans, forward):
        post_mlp, pull_mlp = jax.vjp(rms_gain, collect(part), gain_f[:, 3])
        output_low.append((residual_mid[span] + post_mlp).astype(BF))
        mlp_grad, gain_part_three = pull_mlp(out_grad[span])
        grad_three = grad_three + gain_part_three
        mlp_grads.append(spread(mlp_grad.astype(BF)))
    output_low = jnp.concatenate(output_low, axis=0)
    backward = [
        mlp_backward(grad, gate_up, w_own, w_other)
        for grad, (_, gate_up, _) in zip(mlp_grads, forward)
    ]
    mid_grad = jnp.concatenate([collect(part) for part, _ in backward], axis=0)

    def shard_sum(lefts, rights, cols):
        def product(low):
            total = 0.0
            for left, right in zip(lefts, rights):
                total = total + dot(left, right[:, low : low + cols], TN)
            return total

        other = product(cols).astype(BF)
        grad = (product(0) + flip(other, 1).astype(F32)).astype(BF)
        summed = lax.psum_scatter(grad, "ctx", scatter_dimension=0, tiled=True)
        back = lax.all_to_all(
            summed.reshape(dp_count, rows, cols), "dp", split_axis=0, concat_axis=0, tiled=True
        )
        return [
            back[:, :, low : low + units]
            .transpose(1, 0, 2)
            .reshape(rows, dp_count * units)[:, :FF]
            .astype(F32)
            for low in range(0, cols, units)
        ]

    (sum_down,) = shard_sum(mlp_grads, [hidden for _, _, hidden in forward], units)
    sum_gate, sum_up = shard_sum(mids, [grad for _, grad in backward], 2 * units)

    resid_part, grad_two = pull_mid(mid_grad)
    residual_grad = out_grad + resid_part
    attn_grad, grad_one = pull_attn(residual_grad)
    attn_low = attn_grad.astype(BF)
    grad_out = jnp.einsum("td,tc->dc", attn_low, mixed_low, preferred_element_type=F32)
    row_shape = (z_count, dp_count, rows)
    sum_out = scatter_rows(grad_out.astype(BF).reshape(row_shape + (Q_COLS,)))
    mixed_grad = jnp.dot(attn_low, w_out, preferred_element_type=F32).astype(BF)
    query_grads, key_value_part = attend_back(
        info, query_low, mixed_grad, mixed_low, inverse_total, key_value
    )
    key_value_grad = scatter_line(key_value_part.reshape(z_count, tok_rows, 2 * HD), "ctx")
    raw_query, raw_key, grad_head = pull_qk(
        (query_grads.reshape(tok_rows, H, HD), key_value_grad[:, :HD])
    )
    proj_low = jnp.concatenate([raw_query, raw_key, key_value_grad[:, HD:]], axis=1).astype(BF)
    grad_qkv = jnp.einsum("td,tc->dc", normed_low, proj_low, preferred_element_type=F32)
    in_part = jnp.einsum("tc,dc->td", proj_low, w_qkv, preferred_element_type=F32)
    input_part, grad_zero = pull_in(in_part)
    grad_input_low = (residual_grad + input_part).astype(BF)

    gain_grads = jnp.stack([grad_zero, grad_one, grad_two, grad_three], axis=1)
    gain_grads = gain_grads.reshape(row_shape + (4,))
    head_grads = grad_head.reshape(dp_count, z_count, head_rows, 2).transpose(1, 0, 2, 3)
    side = jnp.zeros(row_shape + (LANES,), BF)
    side = side.at[..., :4].set(gain_grads.astype(BF))
    side = side.at[..., :head_rows, 4:6].set(head_grads.astype(BF))
    qkv_parts = jnp.concatenate(
        [grad_qkv.astype(BF).reshape(row_shape + (START_GATE,)), side], axis=-1
    )
    sum_first = scatter_rows(qkv_parts)
    sum_qkv = sum_first[:, :START_GATE]
    sum_gains = sum_first[:, START_GATE : START_GATE + 4]
    sum_head = sum_first[:head_rows, START_GATE + 4 : START_GATE + 6]

    output = lax.dot_general(
        output_low, place, (((1,), (1,)), ((), ())), preferred_element_type=F32
    ).astype(BF)
    grad_input = lax.dot_general(
        grad_input_low, place, (((1,), (1,)), ((), ())), preferred_element_type=F32
    ).astype(BF)

    sum_weights = jnp.concatenate(
        [sum_qkv, sum_gate, sum_up, sum_out, sum_down], axis=1
    )
    new_w, first_w, second_w = adamw(
        weights, sum_weights, moment_weights, square_weights, RATE_WEIGHTS, WEIGHT_DECAY
    )
    new_g, first_g, second_g = adamw(
        norm_gains, sum_gains, moment_gains, square_gains, RATE_GAINS, 0.0
    )
    new_h, first_h, second_h = adamw(
        head_gains, sum_head, moment_head, square_head, RATE_GAINS, 0.0
    )
    return (
        output,
        grad_input,
        new_w,
        new_g,
        new_h,
        first_w,
        first_g,
        first_h,
        second_w,
        second_g,
        second_h,
        new_w.astype(BF),
    )


def solution(mesh):
    rows = P(("dp", "ctx"), None)
    in_specs = (rows, rows, P("dp")) + (rows,) * 9
    return jax.shard_map(
        body, mesh=mesh, in_specs=in_specs, out_specs=(rows,) * 12, check_vma=False
    )
```

time: 1380 us -> 838 us (0.61)
  local copies, waits for them, and re-layouts: 323 us -> 123 us
  starting transfers between devices: 304 us -> 140 us
  matrix products: 233 us -> 94.3 us
  Pallas kernels: 0 us -> 127 us
  waiting for transfers between devices: 346 us -> 229 us
  other arithmetic: 145 us -> 97 us
    dot_general x31 -> x8, matrix products: 193 us -> 56.9 us  [dot(): return lax.dot_general(left, right, dims, preferred_element_type=F32)]
    dynamic_update_slice x74 -> x0, local copies, waits for them, and re-layouts: 136 us -> none  [the longest x13 47.4 us: gather_line(): out = lax.dynamic_update_index_in_dim(out, got, (me + offset) % count, 0)]
    pallas_call x0 -> x7, Pallas kernels: none -> 127 us  [the longest x2 54.4 us: mlp_backward(): pl.pallas_call(mlp_back_kernel, grid=(rows // tile,), in_specs=[spec(widt...]
    ppermute x24 -> x3, starting transfers between devices: 116 us -> 18 us  [scatter_line(): lax.ppermute(up_out.astype(BF), axis, [(i, i + 1) for i in range(step)])]
    ppermute x108 -> x77, waiting for transfers between devices: 277 us -> 200 us  [the longest x59 124 us: flip(): lax.ppermute(values, 'dp', [(i ^ bit, i) for i in range(lax.axis_size('dp...]
    ppermute x108 -> x77, starting transfers between devices: 159 us -> 106 us  [the longest x59 52.8 us: flip(): lax.ppermute(values, 'dp', [(i ^ bit, i) for i in range(lax.axis_size('dp...]
    ppermute x24 -> x3, waiting for transfers between devices: 58.7 us -> 18 us  [scatter_line(): lax.ppermute(up_out.astype(BF), axis, [(i, i + 1) for i in range(step)])]
    broadcast_in_dim x36 -> x0, local copies, waits for them, and re-layouts: 27.5 us -> none  [the longest x12 9.86 us: gather_line(): out = lax.dynamic_update_index_in_dim(out, got, (me + offset) % count, 0)]
  transfers between devices with their start and end apart: 156 -> 89, of which waited for: 46 -> 32; matrix products, arithmetic and copies ran while one was open for 44% -> 32% of each run, Pallas kernels for 0% -> 13%
where the time goes in v2:
time: 838 us; the launch traced here: 828 us
  waiting for transfers between devices  229 us (27%)
  starting transfers between devices  140 us (17%)
  Pallas kernels  127 us (15%)
  local copies, waits for them, and re-layouts  123 us (15%)
  other arithmetic  97 us (12%)
  matrix products  94.3 us (11%)
  between operations  17.6 us (2%)
    ppermute x59, waiting for transfers between devices, flip(): lax.ppermute(values, 'dp', [(i ^ bit, i) for i in range(lax.axis_size('dp...  124 us
    ppermute x3, waiting for transfers between devices, gather_line(): lax.ppermute(down, axis, [(i, i - 1) for i in range(1, count - step + 1)])  75.8 us
    dot_general x8, matrix products, dot(): return lax.dot_general(left, right, dims, preferred_element_type=F32)  56.9 us
    pallas_call x2, Pallas kernels, mlp_backward(): pl.pallas_call(mlp_back_kernel, grid=(rows // tile,), in_specs=[spec(widt...  54.4 us
    ppermute x59, starting transfers between devices, flip(): lax.ppermute(values, 'dp', [(i ^ bit, i) for i in range(lax.axis_size('dp...  52.8 us
    pallas_call x2, Pallas kernels, mlp_forward(): pl.pallas_call(mlp_kernel, grid=(rows // tile,), in_specs=[spec(width), w...  42.8 us
    ppermute x12, starting transfers between devices, shift(): lax.ppermute(values, axis, [((i + distance) % count, i) for i in range(co...  41 us
    unnamed x297, local copies, waits for them, and re-layouts  31.3 us
  transfers between devices with their start and end apart: 89, of which 32 were waited for; matrix products, arithmetic and copies ran while one was open for 32% of the time, Pallas kernels for 13%

profile of v2, /device:TPU:0, one launch (start us, length us, event | category | flops | bytes accessed | tf_op | source)
XLA Modules:
  0.0 827.5 jit_solution(3006281074651946968)
XLA Ops:
  18.1 5.0 collective-permute-start
  26.3 4.4 all-to-all-start
  31.0 3.3 multiply_reduce_fusion.8
  39.6 18.1 %collective-permute-done.6 = bf16[4,36,768]{2,1,0:T(8,128)(2,1)S(1)} collective-permute-done((bf16[4,36,768]{2,1,0:T(8,128)(2,1)S(1)}, bf16[4,36,768]{2,1,0:T(8,128)(2,1)S(1)}, u32[]{:S(2)}, u32[]{:S(2)}) %collective-permute-start.6) | collective-permute-done | bytes 221216 | tf_op jit(solution)/shard_map/ppermute | solution.py:77
  60.4 10.3 %collective-permute-done.7 = bf16[2,4,36,768]{3,2,1,0:T(8,128)(2,1)S(1)} collective-permute-done((bf16[2,4,36,768]{3,2,1,0:T(8,128)(2,1)S(1)}, bf16[2,4,36,768]{3,2,1,0:T(8,128)(2,1)S(1)}, u32[]{:S(2)}, u32[]{:S(2)}) %collective-permute-start.7) | collective-permute-done | bytes 442400 | tf_op jit(solution)/shard_map/ppermute | solution.py:77
  84.5 2.8 constant_dynamic-update-slice_fusion.1
  91.0 2.7 concatenate.114
  95.2 2.8 collective-permute-start.15
  103.6 4.3 fusion.22
  111.3 5.1 collective-permute-start.10
  125.7 3.2 collective-permute-done.18
  134.3 3.7 collective-permute-done.22
  141.5 14.3 %collective-permute-done.9 = bf16[512,512]{1,0:T(8,128)(2,1)} collective-permute-done((bf16[512,512]{1,0:T(8,128)(2,1)}, bf16[512,512]{1,0:T(8,128)(2,1)}, u32[]{:S(2)}, u32[]{:S(2)}) %collective-permute-start.9) | collective-permute-done | bytes 524320 | tf_op jit(solution)/shard_map/ppermute | solution.py:110
  162.1 27.8 %collective-permute-done.13 = bf16[512,512]{1,0:T(8,128)(2,1)} collective-permute-done((bf16[512,512]{1,0:T(8,128)(2,1)}, bf16[512,512]{1,0:T(8,128)(2,1)}, u32[]{:S(2)}, u32[]{:S(2)}) %collective-permute-start.13) | collective-permute-done | bytes 524320 | tf_op jit(solution)/shard_map/ppermute | solution.py:110
  198.0 33.7 %collective-permute-done.14 = bf16[512,512]{1,0:T(8,128)(2,1)} collective-permute-done((bf16[512,512]{1,0:T(8,128)(2,1)}, bf16[512,512]{1,0:T(8,128)(2,1)}, u32[]{:S(2)}, u32[]{:S(2)}) %collective-permute-start.14) | collective-permute-done | bytes 524320 | tf_op jit(solution)/shard_map/ppermute | solution.py:110
  235.8 10.2 %shard_map.220 = (bf16[512,1024]{1,0:T(8,128)(2,1)}, f32[512,512]{1,0:T(8,128)}) custom-call(s32[2]{0:T(128)} %pad_add_fusion.2.info_ref, bf16[512,1024]{1,0:T(8,128)(2,1)} %bitcast.309, bf16[2048,512]{1,0:T(8,128)(2,1)} %bitcast.304), custom_call_target="tpu_custom_call" | custom-call | flops 2415919104 | bytes 8388608 | tf_op jit(solution)/shard_map/pallas_call | solution.py:300
  246.0 3.1 multiply_reduce_fusion.7
  254.2 3.3 fusion.19
  265.0 2.7 collective-permute-done.33
  269.4 4.5 collective-permute-done.24
  277.1 8.0 collective-permute-done.34
  285.2 10.2 %collective-permute-done.25 = bf16[256,1152]{1,0:T(8,128)(2,1)S(1)} collective-permute-done((bf16[256,1152]{1,0:T(8,128)(2,1)S(1)}, bf16[256,1152]{1,0:T(8,128)(2,1)S(1)}, u32[]{:S(2)}, u32[]{:S(2)}) %collective-permute-start.25) | collective-permute-done | bytes 589856 | tf_op jit(solution)/shard_map/ppermute | solution.py:77
  300.0 21.4 %shard_map.223 = (bf16[1024,1152]{1,0:T(8,128)(2,1)}, bf16[1024,3584]{1,0:T(8,128)(2,1)}, bf16[1024,1792]{1,0:T(8,128)(2,1)}) custom-call(bf16[1024,1152]{1,0:T(8,128)(2,1)} %copy-done.74, bf16[1152,2688]{1,0:T(8,128)(2,1)} %all-gather.2.cloned.1.call-done.own_ref, bf16[1152,2688]{1,0:T(8,128)(2,1)} %collective-permute-done.28.other_ref), custom_call_target="tpu_custom_call" | custom-call | flops 12683575296 | bytes 33554432 | tf_op jit(solution)/shard_map/pallas_call | solution.py:432
  325.9 21.4 %shard_map.222 = (bf16[1024,1152]{1,0:T(8,128)(2,1)}, bf16[1024,3584]{1,0:T(8,128)(2,1)}, bf16[1024,1792]{1,0:T(8,128)(2,1)}) custom-call(bf16[1024,1152]{1,0:T(8,128)(2,1)} %copy-done.70, bf16[1152,2688]{1,0:T(8,128)(2,1)} %all-gather.2.cloned.1.call-done.own_ref, bf16[1152,2688]{1,0:T(8,128)(2,1)} %collective-permute-done.28.other_ref), custom_call_target="tpu_custom_call" | custom-call | flops 12683575296 | bytes 33554432 | tf_op jit(solution)/shard_map/pallas_call | solution.py:432
  354.8 10.4 %collective-permute-done.29 = bf16[256,1152]{1,0:T(8,128)(2,1)S(1)} collective-permute-done((bf16[256,1152]{1,0:T(8,128)(2,1)S(1)}, bf16[256,1152]{1,0:T(8,128)(2,1)S(1)}, u32[]{:S(2)}, u32[]{:S(2)}) %collective-permute-start.29) | collective-permute-done | bytes 589856 | tf_op jit(solution)/shard_map/ppermute | solution.py:77
  368.4 4.3 collective-permute-done.38
  372.9 3.7 collective-permute-done.30
  384.6 2.9 fusion.24
  401.5 7.4 collective-permute-done.50
  411.1 27.2 %shard_map.225 = (bf16[1024,1152]{1,0:T(8,128)(2,1)}, bf16[1024,3584]{1,0:T(8,128)(2,1)}) custom-call(bf16[1024,1152]{1,0:T(8,128)(2,1)} %copy-done.77, bf16[1024,3584]{1,0:T(8,128)(2,1)} %get-tuple-element.79.gate_up_ref, bf16[1152,2688]{1,0:T(8,128)(2,1)} %all-gather.2.cloned.1.call-done.own_ref, bf16[1152,2688]{1,0:T(8,128)(2,1)} %collective-permute-done.28.other_ref), custom_call_target="tpu_custom_call" | custom-call | flops 12683575296 | bytes 33554432 | tf_op jit(solution)/shard_map/pallas_call | solution.py:477
  438.3 10.7 %fusion.12 = f32[1152,1792]{1,0:T(8,128)} fusion(bf16[1024,1152]{1,0:T(8,128)(2,1)} %copy-done.74, bf16[1024,3584]{1,0:T(8,128)(2,1)} %get-tuple-element.85), kind=kOutput, calls=%fused_computation.22 | convolution fusion | flops 4227858432 | bytes 14286848 | tf_op jit(solution)/shard_map/dot_general | solution.py:222
  449.0 6.9 fusion.9
  457.8 2.7 fusion.37
  461.7 4.1 fusion.16
  465.7 27.1 %shard_map.224 = (bf16[1024,1152]{1,0:T(8,128)(2,1)}, bf16[1024,3584]{1,0:T(8,128)(2,1)}) custom-call(bf16[1024,1152]{1,0:T(8,128)(2,1)} %copy-done.81, bf16[1024,3584]{1,0:T(8,128)(2,1)} %get-tuple-element.77.gate_up_ref, bf16[1152,2688]{1,0:T(8,128)(2,1)} %all-gather.2.cloned.1.call-done.own_ref, bf16[1152,2688]{1,0:T(8,128)(2,1)} %collective-permute-done.28.other_ref), custom_call_target="tpu_custom_call" | custom-call | flops 12683575296 | bytes 33554432 | tf_op jit(solution)/shard_map/pallas_call | solution.py:477
  498.7 9.8 %fusion.1 = bf16[1152,1792]{1,0:T(8,128)(2,1)} fusion(f32[1152,1792]{1,0:T(8,128)} %fusion.9, bf16[1024,1152]{1,0:T(8,128)(2,1)S(1)} %copy-done.71, bf16[1024,3584]{1,0:T(8,128)(2,1)} %get-tuple-element.84), kind=kOutput, calls=%fused_computation.3 | convolution fusion | flops 4231987200 | bytes 18415616 | tf_op jit(solution)/shard_map/dot_general | solution.py:222
  508.5 4.6 fusion.40
  514.4 8.4 %collective-permute-done.53 = bf16[256,1152]{1,0:T(8,128)(2,1)S(1)} collective-permute-done((bf16[256,1152]{1,0:T(8,128)(2,1)S(1)}, bf16[256,1152]{1,0:T(8,128)(2,1)S(1)}, u32[]{:S(2)}, u32[]{:S(2)}) %collective-permute-start.53) | collective-permute-done | bytes 589856 | tf_op jit(solution)/shard_map/ppermute | solution.py:77
  525.7 4.6 collective-permute-done.46
  531.8 4.1 collective-permute-done.54
  540.3 2.7 multiply_reduce_fusion.1
  555.8 2.5 convolution_convert_fusion.2.grad_ref
  558.4 19.4 %shard_map.226 = (f32[512,1024]{1,0:T(8,128)}, bf16[2048,512]{1,0:T(8,128)(2,1)}) custom-call(s32[2]{0:T(128)} %pad_add_fusion.2.info_ref, bf16[512,1024]{1,0:T(8,128)(2,1)} %bitcast.310, bf16[512,1024]{1,0:T(8,128)(2,1)} %convolution_convert_fusion.2.grad_ref, bf16[512,1024]{1,0:T(8,128)(2,1)} %get-tuple-element.74.mixed_ref, ...), custom_call_target="tpu_custom_call" | custom-call | flops 6039797760 | bytes 12582912 | tf_op jit(solution)/shard_map/pallas_call | solution.py:384
  582.2 7.4 fusion.15
  601.9 2.8 multiply_reduce_fusion.9
  606.7 18.0 %collective-permute-done.58 = bf16[512,512]{1,0:T(8,128)(2,1)} collective-permute-done((bf16[512,512]{1,0:T(8,128)(2,1)}, bf16[512,512]{1,0:T(8,128)(2,1)}, u32[]{:S(2)}, u32[]{:S(2)}) %collective-permute-start.58) | collective-permute-done | bytes 524320 | tf_op jit(solution)/shard_map/ppermute | solution.py:143
  624.6 2.8 fusion.60
  637.5 13.7 %collective-permute-start.59 = (bf16[512,512]{1,0:T(8,128)(2,1)}, bf16[512,512]{1,0:T(8,128)(2,1)}, u32[]{:S(2)}, u32[]{:S(2)}) collective-permute-start(bf16[512,512]{1,0:T(8,128)(2,1)} %get-tuple-element.203), channel_id=1, source_target_pairs={{0,1},{1,2},{2,3},{4,5},{5,6},{6,7},{8,9},{9,10},{10,11},{12,13},{... | collective-permute-start | bytes 1572872 | tf_op jit(solution)/shard_map/ppermute | solution.py:143
  653.7 10.7 %fusion.2 = bf16[1152,1792]{1,0:T(8,128)(2,1)} fusion(bf16[1152,1792]{1,0:T(8,128)(2,1)} %collective-permute-done.72, f32[1152,1792]{1,0:T(8,128)} %fusion.12, bf16[1024,1152]{1,0:T(8,128)(2,1)S(1)} %copy-done.72, bf16[1024,3584]{1,0:T(8,128)(2,1)} %get-tuple-element.84), kind=kOutput, calls=%fused_computation.4 | convolution fusion | flops 4236115968 | bytes 22544384 | tf_op jit(solution)/shard_map/dot_general | solution.py:222
  674.8 3.9 convolution_convert_fusion
  678.7 5.6 reshape.645
  690.1 6.9 multiply_reduce_fusion.2
  699.8 11.2 %scatter.19 = bf16[4,8,36,128]{3,2,1,0:T(8,128)(2,1)S(1)} dynamic-update-slice(bf16[4,8,36,128]{3,2,1,0:T(8,128)(2,1)S(1)} %fusion.87, bf16[4,8,8,2]{3,2,1,0:T(8,128)(2,1)S(1)} %bitcast_select_fusion, s32[]{:T(128)} %constant.508.clone.1, s32[]{:T(128)} %constant.508.clone.1, s32[]{:T(128)} %bitcast.2, s32[]{:T(128)} %bitcast.3) | dynamic-update-slice | bytes 2052 | tf_op jit(solution)/shard_map/scatter | solution.py:650
  718.4 3.2 collective-permute-done.78
  725.9 8.7 %collective-permute-start.79 = (bf16[36,1024]{1,0:T(8,128)(2,1)}, bf16[36,1024]{1,0:T(8,128)(2,1)}, u32[]{:S(2)}, u32[]{:S(2)}) collective-permute-start(bf16[36,1024]{1,0:T(8,128)(2,1)} %get-tuple-element.266), channel_id=1, source_target_pairs={{1,0},{2,1},{3,2},{0,3},{5,4},{6,5},{7,6},{4,7},{9,8},{10,9},{11,1... | collective-permute-start | bytes 221192 | tf_op jit(solution)/shard_map/ppermute | solution.py:73
  735.7 2.7 collective-permute-done.67
  742.1 3.1 collective-permute-done.68
  749.4 8.2 collective-permute-start.69
  762.2 3.5 all-to-all-start.2
  765.8 5.7 fusion.25
  774.0 13.4 %collective-permute-start.81 = (bf16[36,1024]{1,0:T(8,128)(2,1)}, bf16[36,1024]{1,0:T(8,128)(2,1)S(1)}, u32[]{:S(2)}, u32[]{:S(2)}) collective-permute-start(bf16[36,1024]{1,0:T(8,128)(2,1)} %get-tuple-element.268), channel_id=1, source_target_pairs={{3,0},{0,1},{1,2},{2,3},{7,4},{4,5},{5,6},{6,7},{11,8},{8,9},{9,10... | collective-permute-start | bytes 221192 | tf_op jit(solution)/shard_map/ppermute | solution.py:73
  788.2 3.8 all-to-all-start.1
  797.7 10.7 %all-to-all-done.1 = bf16[8,36,1792]{2,1,0:T(8,128)(2,1)S(1)} async-done(((bf16[8,36,1792]{2,1,0:T(8,128)(2,1)}), bf16[8,36,1792]{2,1,0:T(8,128)(2,1)S(1)}, u32[]{:S(2)}, u32[]{:S(2)}) %all-to-all-start.1) | async-done | bytes 1032224 | tf_op jit(solution)/shard_map/all_to_all | solution.py:610
  813.2 7.4 fusion.131
  (685 shorter events, 266.7 us)
Async XLA Ops:
  18.1 16.8 %collective-permute-start = (bf16[36,1664]{1,0:T(8,128)(2,1)}, bf16[36,1664]{1,0:T(8,128)(2,1)S(1)}, u32[]{:S(2)}, u32[]{:S(2)}) collective-permute-start(bf16[36,1664]{1,0:T(8,128)(2,1)} %pad_maximum_fusion.29), channel_id=1, source_target_pairs={{1,0},{2,1},{3,2},{0,3},{5,4},{6,5},{7,6},{4,7},{9,8},{10,9},{11,1... | collective-permute-start | bytes 359432 | tf_op jit(solution)/shard_map/ppermute | solution.py:73
  26.3 52.4 %all-to-all-start = ((bf16[8,36,2688]{2,1,0:T(8,128)(2,1)}), bf16[8,36,2688]{2,1,0:T(8,128)(2,1)}, u32[]{:S(2)}, u32[]{:S(2)}) async-start(bf16[8,36,2688]{2,1,0:T(8,128)(2,1)} %pad_maximum_fusion.3), calls=%async_computation | async-start | bytes 3440640 | tf_op jit(solution)/shard_map/all_to_all | solution.py:527
  30.8 215.2 %all-gather.2.cloned.1.call-start = ((), (), s32[]{:S(2)}) async-start(), calls=%async_computation.5 | async-start | bytes 7741440 | tf_op jit(solution)/shard_map/all_gather | solution.py:529
  36.1 21.6 %collective-permute-start.6 = (bf16[4,36,768]{2,1,0:T(8,128)(2,1)S(1)}, bf16[4,36,768]{2,1,0:T(8,128)(2,1)S(1)}, u32[]{:S(2)}, u32[]{:S(2)}) collective-permute-start(bf16[4,36,768]{2,1,0:T(8,128)(2,1)S(1)} %pad_maximum_fusion.28), channel_id=1, source_target_pairs={{8,0},{12,4},{0,8},{4,12},{24,16},{28,20},{16,24},{20,28},{9,1},{1... | collective-permute-start | bytes 663560 | tf_op jit(solution)/shard_map/ppermute | solution.py:77
  38.0 21.4 %collective-permute-start.3 = (bf16[4,36,896]{2,1,0:T(8,128)(2,1)S(1)}, bf16[4,36,896]{2,1,0:T(8,128)(2,1)S(1)}, u32[]{:S(2)}, u32[]{:S(2)}) collective-permute-start(bf16[4,36,896]{2,1,0:T(8,128)(2,1)S(1)} %slice.514), channel_id=1, source_target_pairs={{16,0},{20,4},{24,8},{28,12},{0,16},{4,20},{8,24},{12,28},{17,1},{... | collective-permute-start | bytes 774152 | tf_op jit(solution)/shard_map/ppermute | solution.py:77
  59.8 13.6 %collective-permute-start.4 = (bf16[2,4,36,896]{3,1,2,0:T(4,128)(2,1)S(1)}, bf16[2,4,36,896]{3,1,2,0:T(4,128)(2,1)S(1)}, u32[]{:S(2)}, u32[]{:S(2)}) collective-permute-start(bf16[2,4,36,896]{3,1,2,0:T(4,128)(2,1)S(1)} %copy.291), channel_id=1, source_target_pairs={{8,0},{12,4},{0,8},{4,12},{24,16},{28,20},{16,24},{20,28},{9,1},{1... | collective-permute-start | bytes 1548296 | tf_op jit(solution)/shard_map/ppermute | solution.py:77
  81.3 679.0 %reduce-scatter.5.cloned.1.call-start = ((), (), s32[]{:S(2)}) async-start(), calls=%async_computation.7 | async-start | bytes 2580480 | tf_op jit(solution)/shard_map/reduce_scatter | solution.py:609
  95.2 26.9 %collective-permute-start.15 = (bf16[36,1024]{1,0:T(8,128)(2,1)}, bf16[36,1024]{1,0:T(8,128)(2,1)}, u32[]{:S(2)}, u32[]{:S(2)}) collective-permute-start(bf16[36,1024]{1,0:T(8,128)(2,1)} %shard_map.221), channel_id=1, source_target_pairs={{1,0},{2,1},{3,2},{0,3},{5,4},{6,5},{7,6},{4,7},{9,8},{10,9},{11,1... | collective-permute-start | bytes 221192 | tf_op jit(solution)/shard_map/ppermute | solution.py:73
  98.0 24.2 %collective-permute-start.16 = (bf16[36,1024]{1,0:T(8,128)(2,1)}, bf16[36,1024]{1,0:T(8,128)(2,1)}, u32[]{:S(2)}, u32[]{:S(2)}) collective-permute-start(bf16[36,1024]{1,0:T(8,128)(2,1)} %shard_map.221), channel_id=1, source_target_pairs={{2,0},{3,1},{0,2},{1,3},{6,4},{7,5},{4,6},{5,7},{10,8},{11,9},{8,1... | collective-permute-start | bytes 221192 | tf_op jit(solution)/shard_map/ppermute | solution.py:73
  99.1 23.1 %collective-permute-start.17 = (bf16[36,1024]{1,0:T(8,128)(2,1)}, bf16[36,1024]{1,0:T(8,128)(2,1)}, u32[]{:S(2)}, u32[]{:S(2)}) collective-permute-start(bf16[36,1024]{1,0:T(8,128)(2,1)} %shard_map.221), channel_id=1, source_target_pairs={{3,0},{0,1},{1,2},{2,3},{7,4},{4,5},{5,6},{6,7},{11,8},{8,9},{9,10... | collective-permute-start | bytes 221192 | tf_op jit(solution)/shard_map/ppermute | solution.py:73
  111.3 28.8 %collective-permute-start.10 = (bf16[512,512]{1,0:T(8,128)(2,1)}, bf16[512,512]{1,0:T(8,128)(2,1)}, u32[]{:S(2)}, u32[]{:S(2)}) collective-permute-start(bf16[512,512]{1,0:T(8,128)(2,1)} %pad_maximum_fusion.23), channel_id=1, source_target_pairs={{0,1},{1,2},{2,3},{4,5},{5,6},{6,7},{8,9},{9,10},{10,11},{12,13},{... | collective-permute-start | bytes 1572872 | tf_op jit(solution)/shard_map/ppermute | solution.py:109
  116.4 39.4 %collective-permute-start.9 = (bf16[512,512]{1,0:T(8,128)(2,1)}, bf16[512,512]{1,0:T(8,128)(2,1)}, u32[]{:S(2)}, u32[]{:S(2)}) collective-permute-start(bf16[512,512]{1,0:T(8,128)(2,1)} %pad_maximum_fusion.23), channel_id=1, source_target_pairs={{1,0},{2,1},{3,2},{5,4},{6,5},{7,6},{9,8},{10,9},{11,10},{13,12},{... | collective-permute-start | bytes 1572872 | tf_op jit(solution)/shard_map/ppermute | solution.py:110
  138.5 53.1 %collective-permute-start.23 = (bf16[2,2,4,36,512]{4,2,3,1,0:T(4,128)(2,1)S(1)}, bf16[2,2,4,36,512]{4,2,3,1,0:T(4,128)(2,1)S(1)}, u32[]{:S(2)}, u32[]{:S(2)}) collective-permute-start(bf16[2,2,4,36,512]{4,2,3,1,0:T(4,128)(2,1)S(1)} %copy.309), channel_id=1, source_target_pairs={{4,0},{0,4},{12,8},{8,12},{20,16},{16,20},{28,24},{24,28},{5,1},{1... | collective-permute-start | bytes 1769480 | tf_op jit(solution)/shard_map/ppermute | solution.py:77
  140.0 20.6 %collective-permute-start.11 = (bf16[512,512]{1,0:T(8,128)(2,1)}, bf16[512,512]{1,0:T(8,128)(2,1)}, u32[]{:S(2)}, u32[]{:S(2)}) collective-permute-start(bf16[512,512]{1,0:T(8,128)(2,1)} %collective-permute-done.10), channel_id=1, source_target_pairs={{1,2},{2,3},{5,6},{6,7},{9,10},{10,11},{13,14},{14,15},{17,18},{18... | collective-permute-start | bytes 1572872 | tf_op jit(solution)/shard_map/ppermute | solution.py:109
  155.8 34.1 %collective-permute-start.13 = (bf16[512,512]{1,0:T(8,128)(2,1)}, bf16[512,512]{1,0:T(8,128)(2,1)}, u32[]{:S(2)}, u32[]{:S(2)}) collective-permute-start(bf16[512,512]{1,0:T(8,128)(2,1)} %collective-permute-done.9), channel_id=1, source_target_pairs={{1,0},{2,1},{5,4},{6,5},{9,8},{10,9},{13,12},{14,13},{17,16},{18,1... | collective-permute-start | bytes 1572872 | tf_op jit(solution)/shard_map/ppermute | solution.py:110
  158.3 34.1 %collective-permute-start.20 = (bf16[2,2,4,36,512]{4,2,3,1,0:T(4,128)(2,1)}, bf16[2,2,4,36,512]{4,2,3,1,0:T(4,128)(2,1)}, u32[]{:S(2)}, u32[]{:S(2)}) collective-permute-start(bf16[2,2,4,36,512]{4,2,3,1,0:T(4,128)(2,1)} %copy.305), channel_id=1, source_target_pairs={{4,0},{0,4},{12,8},{8,12},{20,16},{16,20},{28,24},{24,28},{5,1},{1... | collective-permute-start | bytes 1769480 | tf_op jit(solution)/shard_map/ppermute | solution.py:77
  160.7 36.0 %collective-permute-start.12 = (bf16[512,512]{1,0:T(8,128)(2,1)}, bf16[512,512]{1,0:T(8,128)(2,1)}, u32[]{:S(2)}, u32[]{:S(2)}) collective-permute-start(bf16[512,512]{1,0:T(8,128)(2,1)} %collective-permute-done.11), channel_id=1, source_target_pairs={{2,3},{6,7},{10,11},{14,15},{18,19},{22,23},{26,27},{30,31}} | collective-permute-start | bytes 1572872 | tf_op jit(solution)/shard_map/ppermute | solution.py:109
  189.9 41.8 %collective-permute-start.14 = (bf16[512,512]{1,0:T(8,128)(2,1)}, bf16[512,512]{1,0:T(8,128)(2,1)}, u32[]{:S(2)}, u32[]{:S(2)}) collective-permute-start(bf16[512,512]{1,0:T(8,128)(2,1)} %collective-permute-done.13), channel_id=1, source_target_pairs={{1,0},{5,4},{9,8},{13,12},{17,16},{21,20},{25,24},{29,28}} | collective-permute-start | bytes 1572872 | tf_op jit(solution)/shard_map/ppermute | solution.py:110
  246.0 54.0 %collective-permute-start.28 = (bf16[1152,2688]{1,0:T(8,128)(2,1)}, bf16[1152,2688]{1,0:T(8,128)(2,1)}, u32[]{:S(2)}, u32[]{:S(2)}) collective-permute-start(bf16[1152,2688]{1,0:T(8,128)(2,1)} %all-gather.2.cloned.1.call-done.own_ref), channel_id=1, source_target_pairs={{4,0},{0,4},{12,8},{8,12},{20,16},{16,20},{28,24},{24,28},{5,1},{1... | collective-permute-start | bytes 18579464 | tf_op jit(solution)/shard_map/ppermute | solution.py:77
  259.7 14.2 %collective-permute-start.24 = (bf16[128,1152]{1,0:T(8,128)(2,1)}, bf16[128,1152]{1,0:T(8,128)(2,1)S(1)}, u32[]{:S(2)}, u32[]{:S(2)}) collective-permute-start(bf16[128,1152]{1,0:T(8,128)(2,1)} %get-tuple-element.228), channel_id=1, source_target_pairs={{8,0},{12,4},{0,8},{4,12},{24,16},{28,20},{16,24},{20,28},{9,1},{1... | collective-permute-start | bytes 884744 | tf_op jit(solution)/shard_map/ppermute | solution.py:77
  260.4 14.2 %collective-permute-start.26 = (bf16[128,1152]{1,0:T(8,128)(2,1)}, bf16[128,1152]{1,0:T(8,128)(2,1)S(1)}, u32[]{:S(2)}, u32[]{:S(2)}) collective-permute-start(bf16[128,1152]{1,0:T(8,128)(2,1)} %get-tuple-element.223), channel_id=1, source_target_pairs={{16,0},{20,4},{24,8},{28,12},{0,16},{4,20},{8,24},{12,28},{17,1},{... | collective-permute-start | bytes 884744 | tf_op jit(solution)/shard_map/ppermute | solution.py:77
  263.6 33.0 %collective-permute-start.36 = (bf16[256,1152]{1,0:T(8,128)(2,1)S(1)}, bf16[256,1152]{1,0:T(8,128)(2,1)S(1)}, u32[]{:S(2)}, u32[]{:S(2)}) collective-permute-start(bf16[256,1152]{1,0:T(8,128)(2,1)S(1)} %pad_maximum_fusion.16), channel_id=1, source_target_pairs={{8,0},{12,4},{0,8},{4,12},{24,16},{28,20},{16,24},{20,28},{9,1},{1... | collective-permute-start | bytes 1769480 | tf_op jit(solution)/shard_map/ppermute | solution.py:77
  268.8 16.3 %collective-permute-start.34 = (bf16[256,1152]{1,0:T(8,128)(2,1)S(1)}, bf16[256,1152]{1,0:T(8,128)(2,1)S(1)}, u32[]{:S(2)}, u32[]{:S(2)}) collective-permute-start(bf16[256,1152]{1,0:T(8,128)(2,1)S(1)} %pad_maximum_fusion.15), channel_id=1, source_target_pairs={{16,0},{20,4},{24,8},{28,12},{0,16},{4,20},{8,24},{12,28},{17,1},{... | collective-permute-start | bytes 1769480 | tf_op jit(solution)/shard_map/ppermute | solution.py:77
  274.0 21.4 %collective-permute-start.25 = (bf16[256,1152]{1,0:T(8,128)(2,1)S(1)}, bf16[256,1152]{1,0:T(8,128)(2,1)S(1)}, u32[]{:S(2)}, u32[]{:S(2)}) collective-permute-start(bf16[256,1152]{1,0:T(8,128)(2,1)S(1)} %pad_maximum_fusion.13), channel_id=1, source_target_pairs={{16,0},{20,4},{24,8},{28,12},{0,16},{4,20},{8,24},{12,28},{17,1},{... | collective-permute-start | bytes 1769480 | tf_op jit(solution)/shard_map/ppermute | solution.py:77
  274.6 23.9 %collective-permute-start.27 = (bf16[256,1152]{1,0:T(8,128)(2,1)S(1)}, bf16[256,1152]{1,0:T(8,128)(2,1)S(1)}, u32[]{:S(2)}, u32[]{:S(2)}) collective-permute-start(bf16[256,1152]{1,0:T(8,128)(2,1)S(1)} %pad_maximum_fusion.14), channel_id=1, source_target_pairs={{8,0},{12,4},{0,8},{4,12},{24,16},{28,20},{16,24},{20,28},{9,1},{1... | collective-permute-start | bytes 1769480 | tf_op jit(solution)/shard_map/ppermute | solution.py:77
  323.7 27.1 %collective-permute-start.37 = (bf16[256,1152]{1,0:T(8,128)(2,1)}, bf16[256,1152]{1,0:T(8,128)(2,1)}, u32[]{:S(2)}, u32[]{:S(2)}) collective-permute-start(bf16[256,1152]{1,0:T(8,128)(2,1)} %get-tuple-element.199), channel_id=1, source_target_pairs={{16,0},{20,4},{24,8},{28,12},{0,16},{4,20},{8,24},{12,28},{17,1},{... | collective-permute-start | bytes 1769480 | tf_op jit(solution)/shard_map/ppermute | solution.py:77
  324.6 26.2 %collective-permute-start.39 = (bf16[256,1152]{1,0:T(8,128)(2,1)}, bf16[256,1152]{1,0:T(8,128)(2,1)}, u32[]{:S(2)}, u32[]{:S(2)}) collective-permute-start(bf16[256,1152]{1,0:T(8,128)(2,1)} %get-tuple-element.200), channel_id=1, source_target_pairs={{8,0},{12,4},{0,8},{4,12},{24,16},{28,20},{16,24},{20,28},{9,1},{1... | collective-permute-start | bytes 1769480 | tf_op jit(solution)/shard_map/ppermute | solution.py:77
  348.9 16.3 %collective-permute-start.29 = (bf16[256,1152]{1,0:T(8,128)(2,1)S(1)}, bf16[256,1152]{1,0:T(8,128)(2,1)S(1)}, u32[]{:S(2)}, u32[]{:S(2)}) collective-permute-start(bf16[256,1152]{1,0:T(8,128)(2,1)S(1)} %get-tuple-element.195), channel_id=1, source_target_pairs={{16,0},{20,4},{24,8},{28,12},{0,16},{4,20},{8,24},{12,28},{17,1},{... | collective-permute-start | bytes 1769480 | tf_op jit(solution)/shard_map/ppermute | solution.py:77
  350.1 16.3 %collective-permute-start.31 = (bf16[256,1152]{1,0:T(8,128)(2,1)S(1)}, bf16[256,1152]{1,0:T(8,128)(2,1)S(1)}, u32[]{:S(2)}, u32[]{:S(2)}) collective-permute-start(bf16[256,1152]{1,0:T(8,128)(2,1)S(1)} %get-tuple-element.196), channel_id=1, source_target_pairs={{8,0},{12,4},{0,8},{4,12},{24,16},{28,20},{16,24},{20,28},{9,1},{1... | collective-permute-start | bytes 1769480 | tf_op jit(solution)/shard_map/ppermute | solution.py:77
  352.4 20.3 %collective-permute-start.38 = (bf16[128,1152]{1,0:T(8,128)(2,1)S(1)}, bf16[128,1152]{1,0:T(8,128)(2,1)S(1)}, u32[]{:S(2)}, u32[]{:S(2)}) collective-permute-start(bf16[128,1152]{1,0:T(8,128)(2,1)S(1)} %slice.699), channel_id=1, source_target_pairs={{8,0},{12,4},{0,8},{4,12},{24,16},{28,20},{16,24},{20,28},{9,1},{1... | collective-permute-start | bytes 884744 | tf_op jit(solution)/shard_map/ppermute | solution.py:77
  353.9 18.9 %collective-permute-start.40 = (bf16[128,1152]{1,0:T(8,128)(2,1)S(1)}, bf16[128,1152]{1,0:T(8,128)(2,1)S(1)}, u32[]{:S(2)}, u32[]{:S(2)}) collective-permute-start(bf16[128,1152]{1,0:T(8,128)(2,1)S(1)} %slice.698), channel_id=1, source_target_pairs={{16,0},{20,4},{24,8},{28,12},{0,16},{4,20},{8,24},{12,28},{17,1},{... | collective-permute-start | bytes 884744 | tf_op jit(solution)/shard_map/ppermute | solution.py:77
  383.3 13.8 %collective-permute-start.41 = (bf16[128,1152]{1,0:T(8,128)(2,1)}, bf16[128,1152]{1,0:T(8,128)(2,1)}, u32[]{:S(2)}, u32[]{:S(2)}) collective-permute-start(bf16[128,1152]{1,0:T(8,128)(2,1)} %get-tuple-element.245), channel_id=1, source_target_pairs={{8,0},{12,4},{0,8},{4,12},{24,16},{28,20},{16,24},{20,28},{9,1},{1... | collective-permute-start | bytes 884744 | tf_op jit(solution)/shard_map/ppermute | solution.py:77
  391.1 18.5 %collective-permute-start.52 = (bf16[256,1152]{1,0:T(8,128)(2,1)S(1)}, bf16[256,1152]{1,0:T(8,128)(2,1)S(1)}, u32[]{:S(2)}, u32[]{:S(2)}) collective-permute-start(bf16[256,1152]{1,0:T(8,128)(2,1)S(1)} %pad_maximum_fusion.20), channel_id=1, source_target_pairs={{8,0},{12,4},{0,8},{4,12},{24,16},{28,20},{16,24},{20,28},{9,1},{1... | collective-permute-start | bytes 1769480 | tf_op jit(solution)/shard_map/ppermute | solution.py:77
  392.6 16.3 %collective-permute-start.50 = (bf16[256,1152]{1,0:T(8,128)(2,1)S(1)}, bf16[256,1152]{1,0:T(8,128)(2,1)S(1)}, u32[]{:S(2)}, u32[]{:S(2)}) collective-permute-start(bf16[256,1152]{1,0:T(8,128)(2,1)S(1)} %pad_maximum_fusion.19), channel_id=1, source_target_pairs={{16,0},{20,4},{24,8},{28,12},{0,16},{4,20},{8,24},{12,28},{17,1},{... | collective-permute-start | bytes 1769480 | tf_op jit(solution)/shard_map/ppermute | solution.py:77
  395.7 64.8 %collective-permute-start.44 = (bf16[256,1152]{1,0:T(8,128)(2,1)}, bf16[256,1152]{1,0:T(8,128)(2,1)}, u32[]{:S(2)}, u32[]{:S(2)}) collective-permute-start(bf16[256,1152]{1,0:T(8,128)(2,1)} %pad_maximum_fusion.18), channel_id=1, source_target_pairs={{8,0},{12,4},{0,8},{4,12},{24,16},{28,20},{16,24},{20,28},{9,1},{1... | collective-permute-start | bytes 1769480 | tf_op jit(solution)/shard_map/ppermute | solution.py:77
  399.0 57.0 %collective-permute-start.42 = (bf16[256,1152]{1,0:T(8,128)(2,1)}, bf16[256,1152]{1,0:T(8,128)(2,1)}, u32[]{:S(2)}, u32[]{:S(2)}) collective-permute-start(bf16[256,1152]{1,0:T(8,128)(2,1)} %pad_maximum_fusion.17), channel_id=1, source_target_pairs={{16,0},{20,4},{24,8},{28,12},{0,16},{4,20},{8,24},{12,28},{17,1},{... | collective-permute-start | bytes 1769480 | tf_op jit(solution)/shard_map/ppermute | solution.py:77
  465.7 116.5 %collective-permute-start.82 = (bf16[1152,896]{1,0:T(8,128)(2,1)}, bf16[1152,896]{1,0:T(8,128)(2,1)}, u32[]{:S(2)}, u32[]{:S(2)}) collective-permute-start(bf16[1152,896]{1,0:T(8,128)(2,1)} %fusion.16), channel_id=1, source_target_pairs={{4,0},{0,4},{12,8},{8,12},{20,16},{16,20},{28,24},{24,28},{5,1},{1... | collective-permute-start | bytes 6193160 | tf_op jit(solution)/shard_map/ppermute | solution.py:77
  494.4 18.7 %collective-permute-start.45 = (bf16[256,1152]{1,0:T(8,128)(2,1)S(1)}, bf16[256,1152]{1,0:T(8,128)(2,1)S(1)}, u32[]{:S(2)}, u32[]{:S(2)}) collective-permute-start(bf16[256,1152]{1,0:T(8,128)(2,1)S(1)} %get-tuple-element.187), channel_id=1, source_target_pairs={{16,0},{20,4},{24,8},{28,12},{0,16},{4,20},{8,24},{12,28},{17,1},{... | collective-permute-start | bytes 1769480 | tf_op jit(solution)/shard_map/ppermute | solution.py:77
  495.1 18.0 %collective-permute-start.47 = (bf16[256,1152]{1,0:T(8,128)(2,1)S(1)}, bf16[256,1152]{1,0:T(8,128)(2,1)S(1)}, u32[]{:S(2)}, u32[]{:S(2)}) collective-permute-start(bf16[256,1152]{1,0:T(8,128)(2,1)S(1)} %get-tuple-element.188), channel_id=1, source_target_pairs={{8,0},{12,4},{0,8},{4,12},{24,16},{28,20},{16,24},{20,28},{9,1},{1... | collective-permute-start | bytes 1769480 | tf_op jit(solution)/shard_map/ppermute | solution.py:77
  496.6 26.2 %collective-permute-start.53 = (bf16[256,1152]{1,0:T(8,128)(2,1)S(1)}, bf16[256,1152]{1,0:T(8,128)(2,1)S(1)}, u32[]{:S(2)}, u32[]{:S(2)}) collective-permute-start(bf16[256,1152]{1,0:T(8,128)(2,1)S(1)} %get-tuple-element.191), channel_id=1, source_target_pairs={{16,0},{20,4},{24,8},{28,12},{0,16},{4,20},{8,24},{12,28},{17,1},{... | collective-permute-start | bytes 1769480 | tf_op jit(solution)/shard_map/ppermute | solution.py:77
  497.5 26.4 %collective-permute-start.55 = (bf16[256,1152]{1,0:T(8,128)(2,1)S(1)}, bf16[256,1152]{1,0:T(8,128)(2,1)S(1)}, u32[]{:S(2)}, u32[]{:S(2)}) collective-permute-start(bf16[256,1152]{1,0:T(8,128)(2,1)S(1)} %get-tuple-element.192), channel_id=1, source_target_pairs={{8,0},{12,4},{0,8},{4,12},{24,16},{28,20},{16,24},{20,28},{9,1},{1... | collective-permute-start | bytes 1769480 | tf_op jit(solution)/shard_map/ppermute | solution.py:77
  513.1 140.5 %collective-permute-start.72 = (bf16[1152,1792]{1,0:T(8,128)(2,1)}, bf16[1152,1792]{1,0:T(8,128)(2,1)}, u32[]{:S(2)}, u32[]{:S(2)}) collective-permute-start(bf16[1152,1792]{1,0:T(8,128)(2,1)} %fusion.1), channel_id=1, source_target_pairs={{4,0},{0,4},{12,8},{8,12},{20,16},{16,20},{28,24},{24,28},{5,1},{1... | collective-permute-start | bytes 12386312 | tf_op jit(solution)/shard_map/ppermute | solution.py:77
  513.4 16.8 %collective-permute-start.46 = (bf16[128,1152]{1,0:T(8,128)(2,1)S(1)}, bf16[128,1152]{1,0:T(8,128)(2,1)S(1)}, u32[]{:S(2)}, u32[]{:S(2)}) collective-permute-start(bf16[128,1152]{1,0:T(8,128)(2,1)S(1)} %slice.697), channel_id=1, source_target_pairs={{8,0},{12,4},{0,8},{4,12},{24,16},{28,20},{16,24},{20,28},{9,1},{1... | collective-permute-start | bytes 884744 | tf_op jit(solution)/shard_map/ppermute | solution.py:77
  552.9 80.8 %collective-permute-start.76 = (bf16[4,2,2,36,512]{4,0,3,2,1:T(4,128)(2,1)}, bf16[4,2,2,36,512]{4,0,3,2,1:T(4,128)(2,1)}, u32[]{:S(2)}, u32[]{:S(2)}) collective-permute-start(bf16[4,2,2,36,512]{4,0,3,2,1:T(4,128)(2,1)} %get-tuple-element.219), channel_id=1, source_target_pairs={{4,0},{0,4},{12,8},{8,12},{20,16},{16,20},{28,24},{24,28},{5,1},{1... | collective-permute-start | bytes 1769480 | tf_op jit(solution)/shard_map/ppermute | solution.py:77
  555.3 109.1 %collective-permute-start.73 = (bf16[4,2,2,36,512]{4,0,3,2,1:T(4,128)(2,1)}, bf16[4,2,2,36,512]{4,0,3,2,1:T(4,128)(2,1)}, u32[]{:S(2)}, u32[]{:S(2)}) collective-permute-start(bf16[4,2,2,36,512]{4,0,3,2,1:T(4,128)(2,1)} %get-tuple-element.221), channel_id=1, source_target_pairs={{4,0},{0,4},{12,8},{8,12},{20,16},{16,20},{28,24},{24,28},{5,1},{1... | collective-permute-start | bytes 1769480 | tf_op jit(solution)/shard_map/ppermute | solution.py:77
  580.0 17.3 %collective-permute-start.57 = (bf16[512,512]{1,0:T(8,128)(2,1)}, bf16[512,512]{1,0:T(8,128)(2,1)}, u32[]{:S(2)}, u32[]{:S(2)}) collective-permute-start(bf16[512,512]{1,0:T(8,128)(2,1)} %get-tuple-element.205), channel_id=1, source_target_pairs={{0,1},{4,5},{8,9},{12,13},{16,17},{20,21},{24,25},{28,29}} | collective-permute-start | bytes 1572872 | tf_op jit(solution)/shard_map/ppermute | solution.py:143
  589.6 182.2 %reduce-scatter.3.cloned.1.call-start = ((), (), s32[]{:S(2)}) async-start(), calls=%async_computation.6 | async-start | bytes 5160960 | tf_op jit(solution)/shard_map/reduce_scatter | solution.py:609
  593.4 13.2 %collective-permute-start.60 = (bf16[512,512]{1,0:T(8,128)(2,1)}, bf16[512,512]{1,0:T(8,128)(2,1)}, u32[]{:S(2)}, u32[]{:S(2)}) collective-permute-start(bf16[512,512]{1,0:T(8,128)(2,1)} %get-tuple-element.206), channel_id=1, source_target_pairs={{3,2},{7,6},{11,10},{15,14},{19,18},{23,22},{27,26},{31,30}} | collective-permute-start | bytes 1572872 | tf_op jit(solution)/shard_map/ppermute | solution.py:144
  599.8 24.8 %collective-permute-start.58 = (bf16[512,512]{1,0:T(8,128)(2,1)}, bf16[512,512]{1,0:T(8,128)(2,1)}, u32[]{:S(2)}, u32[]{:S(2)}) collective-permute-start(bf16[512,512]{1,0:T(8,128)(2,1)} %fusion.59), channel_id=1, source_target_pairs={{0,1},{1,2},{4,5},{5,6},{8,9},{9,10},{12,13},{13,14},{16,17},{17,1... | collective-permute-start | bytes 1572872 | tf_op jit(solution)/shard_map/ppermute | solution.py:143
  627.4 23.8 %collective-permute-start.61 = (bf16[512,512]{1,0:T(8,128)(2,1)}, bf16[512,512]{1,0:T(8,128)(2,1)}, u32[]{:S(2)}, u32[]{:S(2)}) collective-permute-start(bf16[512,512]{1,0:T(8,128)(2,1)} %get-tuple-element.204), channel_id=1, source_target_pairs={{2,1},{3,2},{6,5},{7,6},{10,9},{11,10},{14,13},{15,14},{18,17},{19... | collective-permute-start | bytes 1572872 | tf_op jit(solution)/shard_map/ppermute | solution.py:144
  636.1 31.4 %collective-permute-start.77 = (bf16[4,2,36,512]{3,2,0,1:T(8,128)(2,1)}, bf16[4,2,36,512]{3,2,0,1:T(8,128)(2,1)}, u32[]{:S(2)}, u32[]{:S(2)}) collective-permute-start(bf16[4,2,36,512]{3,2,0,1:T(8,128)(2,1)} %dynamic-slice_bitcast_fusion.8), channel_id=1, source_target_pairs={{8,0},{12,4},{0,8},{4,12},{24,16},{28,20},{16,24},{20,28},{9,1},{1... | collective-permute-start | bytes 884744 | tf_op jit(solution)/shard_map/ppermute | solution.py:77
  637.5 31.8 %collective-permute-start.59 = (bf16[512,512]{1,0:T(8,128)(2,1)}, bf16[512,512]{1,0:T(8,128)(2,1)}, u32[]{:S(2)}, u32[]{:S(2)}) collective-permute-start(bf16[512,512]{1,0:T(8,128)(2,1)} %get-tuple-element.203), channel_id=1, source_target_pairs={{0,1},{1,2},{2,3},{4,5},{5,6},{6,7},{8,9},{9,10},{10,11},{12,13},{... | collective-permute-start | bytes 1572872 | tf_op jit(solution)/shard_map/ppermute | solution.py:143
  652.4 17.0 %collective-permute-start.62 = (bf16[512,512]{1,0:T(8,128)(2,1)S(1)}, bf16[512,512]{1,0:T(8,128)(2,1)}, u32[]{:S(2)}, u32[]{:S(2)}) collective-permute-start(bf16[512,512]{1,0:T(8,128)(2,1)S(1)} %fusion.58), channel_id=1, source_target_pairs={{1,0},{2,1},{3,2},{5,4},{6,5},{7,6},{9,8},{10,9},{11,10},{13,12},{... | collective-permute-start | bytes 1572872 | tf_op jit(solution)/shard_map/ppermute | solution.py:144
  666.8 50.0 %collective-permute-start.74 = (bf16[4,2,36,512]{3,2,0,1:T(8,128)(2,1)}, bf16[4,2,36,512]{3,2,0,1:T(8,128)(2,1)}, u32[]{:S(2)}, u32[]{:S(2)}) collective-permute-start(bf16[4,2,36,512]{3,2,0,1:T(8,128)(2,1)} %dynamic-slice_bitcast_fusion.9), channel_id=1, source_target_pairs={{16,0},{20,4},{24,8},{28,12},{0,16},{4,20},{8,24},{12,28},{17,1},{... | collective-permute-start | bytes 884744 | tf_op jit(solution)/shard_map/ppermute | solution.py:77
  689.7 32.0 %collective-permute-start.63 = (bf16[4,2,2,36,768]{4,0,3,2,1:T(4,128)(2,1)}, bf16[4,2,2,36,768]{4,0,3,2,1:T(4,128)(2,1)S(1)}, u32[]{:S(2)}, u32[]{:S(2)}) collective-permute-start(bf16[4,2,2,36,768]{4,0,3,2,1:T(4,128)(2,1)} %dynamic-slice_bitcast_fusion.1), channel_id=1, source_target_pairs={{4,0},{0,4},{12,8},{8,12},{20,16},{16,20},{28,24},{24,28},{5,1},{1... | collective-permute-start | bytes 2654216 | tf_op jit(solution)/shard_map/ppermute | solution.py:77
  724.6 13.8 %collective-permute-start.67 = (bf16[4,2,36,896]{3,0,2,1:T(4,128)(2,1)S(1)}, bf16[4,2,36,896]{3,0,2,1:T(4,128)(2,1)S(1)}, u32[]{:S(2)}, u32[]{:S(2)}) collective-permute-start(bf16[4,2,36,896]{3,0,2,1:T(4,128)(2,1)S(1)} %dynamic-slice_bitcast_fusion.6), channel_id=1, source_target_pairs={{8,0},{12,4},{0,8},{4,12},{24,16},{28,20},{16,24},{20,28},{9,1},{1... | collective-permute-start | bytes 1548296 | tf_op jit(solution)/shard_map/ppermute | solution.py:77
  725.9 85.0 %collective-permute-start.79 = (bf16[36,1024]{1,0:T(8,128)(2,1)}, bf16[36,1024]{1,0:T(8,128)(2,1)}, u32[]{:S(2)}, u32[]{:S(2)}) collective-permute-start(bf16[36,1024]{1,0:T(8,128)(2,1)} %get-tuple-element.266), channel_id=1, source_target_pairs={{1,0},{2,1},{3,2},{0,3},{5,4},{6,5},{7,6},{4,7},{9,8},{10,9},{11,1... | collective-permute-start | bytes 221192 | tf_op jit(solution)/shard_map/ppermute | solution.py:73
  734.7 76.3 %collective-permute-start.80 = (bf16[36,1024]{1,0:T(8,128)(2,1)}, bf16[36,1024]{1,0:T(8,128)(2,1)}, u32[]{:S(2)}, u32[]{:S(2)}) collective-permute-start(bf16[36,1024]{1,0:T(8,128)(2,1)} %get-tuple-element.267), channel_id=1, source_target_pairs={{2,0},{3,1},{0,2},{1,3},{6,4},{7,5},{4,6},{5,7},{10,8},{11,9},{8,1... | collective-permute-start | bytes 221192 | tf_op jit(solution)/shard_map/ppermute | solution.py:73
  749.4 24.6 %collective-permute-start.69 = (bf16[36,1664]{0,1:T(8,128)(2,1)}, bf16[36,1664]{0,1:T(8,128)(2,1)}, u32[]{:S(2)}, u32[]{:S(2)}) collective-permute-start(bf16[36,1664]{0,1:T(8,128)(2,1)} %bitcast.315), channel_id=1, source_target_pairs={{1,0},{2,1},{3,2},{0,3},{5,4},{6,5},{7,6},{4,7},{9,8},{10,9},{11,1... | collective-permute-start | bytes 359432 | tf_op jit(solution)/shard_map/ppermute | solution.py:73
  758.6 33.4 %collective-permute-start.70 = (bf16[36,1664]{0,1:T(8,128)(2,1)}, bf16[36,1664]{0,1:T(8,128)(2,1)}, u32[]{:S(2)}, u32[]{:S(2)}) collective-permute-start(bf16[36,1664]{0,1:T(8,128)(2,1)} %bitcast.313), channel_id=1, source_target_pairs={{2,0},{3,1},{0,2},{1,3},{6,4},{7,5},{4,6},{5,7},{10,8},{11,9},{8,1... | collective-permute-start | bytes 359432 | tf_op jit(solution)/shard_map/ppermute | solution.py:73
  759.7 32.4 %collective-permute-start.71 = (bf16[36,1664]{0,1:T(8,128)(2,1)}, bf16[36,1664]{0,1:T(8,128)(2,1)}, u32[]{:S(2)}, u32[]{:S(2)}) collective-permute-start(bf16[36,1664]{0,1:T(8,128)(2,1)} %bitcast.314), channel_id=1, source_target_pairs={{3,0},{0,1},{1,2},{2,3},{7,4},{4,5},{5,6},{6,7},{11,8},{8,9},{9,10... | collective-permute-start | bytes 359432 | tf_op jit(solution)/shard_map/ppermute | solution.py:73
  762.2 25.1 %all-to-all-start.2 = ((bf16[8,36,896]{2,1,0:T(8,128)(2,1)}), bf16[8,36,896]{2,1,0:T(8,128)(2,1)S(1)}, u32[]{:S(2)}, u32[]{:S(2)}) async-start(bf16[8,36,896]{2,1,0:T(8,128)(2,1)} %reshape.654), calls=%async_computation.4 | async-start | bytes 1146880 | tf_op jit(solution)/shard_map/all_to_all | solution.py:610
  774.0 37.0 %collective-permute-start.81 = (bf16[36,1024]{1,0:T(8,128)(2,1)}, bf16[36,1024]{1,0:T(8,128)(2,1)S(1)}, u32[]{:S(2)}, u32[]{:S(2)}) collective-permute-start(bf16[36,1024]{1,0:T(8,128)(2,1)} %get-tuple-element.268), channel_id=1, source_target_pairs={{3,0},{0,1},{1,2},{2,3},{7,4},{4,5},{5,6},{6,7},{11,8},{8,9},{9,10... | collective-permute-start | bytes 221192 | tf_op jit(solution)/shard_map/ppermute | solution.py:73
  788.2 20.2 %all-to-all-start.1 = ((bf16[8,36,1792]{2,1,0:T(8,128)(2,1)}), bf16[8,36,1792]{2,1,0:T(8,128)(2,1)S(1)}, u32[]{:S(2)}, u32[]{:S(2)}) async-start(bf16[8,36,1792]{2,1,0:T(8,128)(2,1)} %reshape.648), calls=%async_computation.2 | async-start | bytes 2293760 | tf_op jit(solution)/shard_map/all_to_all | solution.py:610
  (159 other events, 1170.6 us)
Sparse Core Ops, SparseCore 0:
  81.4 142.4 all-gather.1
  589.7 51.5 reduce-scatter.4
  664.6 83.1 reduce-scatter.2

commit v3 on v2

--- a/solution.py
+++ b/solution.py
@@ -86,10 +86,6 @@
     return bits, bits[::-1]
 
 
-def bit_orders():
-    return tuple(bits + [1] for bits in chip_orders())
-
-
 def place_blocks(blocks, axis):
     count, me = len(blocks), lax.axis_index(axis)
     return jnp.stack([lax.select_n((j - me) % count, *blocks) for j in range(count)])
@@ -101,112 +97,129 @@
     return place_blocks(blocks, axis)
 
 
-def gather_line(values, axis):
+def scatter_parts(parts, axis):
     count, me = lax.axis_size(axis), lax.axis_index(axis)
-    below, above = [], []
-    up, down = values, values
-    for step in range(1, count):
-        up = lax.ppermute(up, axis, [(i, i + 1) for i in range(step - 1, count - 1)])
-        down = lax.ppermute(down, axis, [(i, i - 1) for i in range(1, count - step + 1)])
-        below.append(up)
-        above.append(down)
-    blocks = [values]
-    for offset in range(1, count):
-        blocks.append(
-            jnp.where(me + offset < count, above[offset - 1], below[count - offset - 1])
-        )
-    return place_blocks(blocks, axis)
-
-
-def scatter_direct(parts, axis):
-    count, me = lax.axis_size(axis), lax.axis_index(axis)
-    total = lax.dynamic_index_in_dim(parts, me, 0, keepdims=False).astype(F32)
-    for distance in range(1, count):
-        mine = lax.dynamic_index_in_dim(parts, (me - distance) % count, 0, keepdims=False)
+    return [
+        lax.dynamic_index_in_dim(parts, (me - distance) % count, 0, keepdims=False)
+        for distance in range(count)
+    ]
+
+
+def scatter_direct(slices, axis):
+    total = slices[0].astype(F32)
+    for distance, mine in enumerate(slices[1:], 1):
         total = total + shift(mine.astype(BF), axis, distance).astype(F32)
     return total
 
 
-def scatter_line(parts, axis):
-    count, me = lax.axis_size(axis), lax.axis_index(axis)
-
-    def own(index):
-        return lax.dynamic_index_in_dim(parts, jnp.clip(index, 0, count - 1), 0, keepdims=False)
-
-    up = down = None
-    for step in range(1, count):
-        far = count - step
-        up_out = own(me + far).astype(F32)
-        down_out = own(me - far).astype(F32)
-        if step > 1:
-            up_out, down_out = up_out + up.astype(F32), down_out + down.astype(F32)
-        up = lax.ppermute(up_out.astype(BF), axis, [(i, i + 1) for i in range(step)])
-        down = lax.ppermute(
-            down_out.astype(BF), axis, [(i, i - 1) for i in range(count - step, count)]
-        )
-    return own(me).astype(F32) + up.astype(F32) + down.astype(F32)
-
-
-def split_cols(cols):
+def side_by_side(own, other):
+    mine = my_bit(1)
+    return jnp.concatenate(
+        [jnp.where(mine == 0, own, other), jnp.where(mine == 0, other, own)], axis=-1
+    )
+
+
+def halves_of(values):
+    cols = values.shape[-1] // 2
+    mine = my_bit(1)
+    keep = lax.dynamic_slice_in_dim(values, mine * cols, cols, values.ndim - 1)
+    send = lax.dynamic_slice_in_dim(values, (1 - mine) * cols, cols, values.ndim - 1)
+    return keep, send
+
+
+def column_spans(cols):
     half = cols // 2 // LANES * LANES
     return ((0, half), (half, cols))
 
 
-def gather_rows(shard):
+def gather_rows(shard, after=None):
     rows, cols = shard.shape
-    z_block = gather_direct(shard, "ctx")
-    z_count = z_block.shape[0]
-    halves = []
-    for (low, high), bits in zip(split_cols(cols), bit_orders()):
-        part = z_block[..., low:high]
+    keep, send = halves_of(shard)
+    got, mine = flip(send, 1), my_bit(1)
+    pair = jnp.concatenate([jnp.where(mine == 0, keep, got), jnp.where(mine == 0, got, keep)])
+    z_block = gather_direct(pair, "ctx")
+    if after is not None:
+        z_block = tie(z_block, after)
+    parts = []
+    for (low, high), bits in zip(column_spans(cols // 2), chip_orders()):
+        part, done = z_block[..., low:high], []
         for bit in bits:
             got, mine = flip(part, bit), my_bit(bit)
-            part = jnp.stack([jnp.where(mine == 0, part, got), jnp.where(mine == 0, got, part)])
-        axes = bits[::-1]
-        order = [axes.index(bit) for bit in sorted(bits, reverse=True)]
-        count = len(bits)
-        part = part.transpose([count] + order + [count + 1, count + 2])
-        halves.append(part.reshape(z_count, -1, rows, high - low))
-    return jnp.concatenate(halves, axis=-1).reshape(-1, cols)
-
-
-def scatter_rows(parts):
-    z_count, dp_count, rows, cols = parts.shape
-    halves = []
-    for (low, high), bits in zip(split_cols(cols), bit_orders()):
-        part = parts[..., low:high]
-        part = part.reshape((z_count,) + (2,) * len(bits) + (rows, high - low))
-        left = sorted(bits, reverse=True)
-        for bit in bits[::-1]:
-            dim, mine = 1 + left.index(bit), my_bit(bit)
-            keep = lax.dynamic_index_in_dim(part, mine, dim, keepdims=False)
-            send = lax.dynamic_index_in_dim(part, 1 - mine, dim, keepdims=False)
-            part = (keep.astype(F32) + flip(send, bit).astype(F32)).astype(BF)
-            left.remove(bit)
-        halves.append(part)
-    return scatter_direct(jnp.concatenate(halves, axis=-1), "ctx")
-
-
-def spread(values):
+            at = 1 + sum(other > bit for other in done)
+            part = jnp.stack(
+                [jnp.where(mine == 0, part, got), jnp.where(mine == 0, got, part)], axis=at
+            )
+            done.append(bit)
+        parts.append(part.reshape(-1, high - low))
+    own = jnp.concatenate(parts, axis=-1)
+    return side_by_side(own, flip(own, 1))
+
+
+def scatter_cols(parts, bits):
+    return scatter_cols_sent(parts, bits)[0]
+
+
+def scatter_cols_sent(parts, bits):
+    part, first = parts.astype(BF), None
+    for bit in bits:
+        cols, mine = part.shape[1] // 2, my_bit(bit)
+        keep = lax.dynamic_slice_in_dim(part, mine * cols, cols, 1)
+        send = lax.dynamic_slice_in_dim(part, (1 - mine) * cols, cols, 1)
+        first = send if first is None else first
+        part = (keep.astype(F32) + flip(send, bit).astype(F32)).astype(BF)
+    return part, first
+
+
+def columns_back(blocks, bits):
+    count, rows, cols = blocks.shape
+    axes = sorted(bits, reverse=True)
+    blocks = blocks.reshape((2,) * len(bits) + (rows, cols))
+    order = [len(bits)] + [axes.index(bit) for bit in bits] + [len(bits) + 1]
+    return blocks.transpose(order).reshape(rows, count * cols).astype(F32)
+
+
+def spread_step(parts, step):
+    return [(part, flip(part, bits[step])) for part, bits in zip(parts, chip_orders())]
+
+
+def joined(pairs):
+    return [jnp.concatenate(pair, axis=0) for pair in pairs]
+
+
+def spread_start(values):
     half = values.shape[0] // 2
-    out = []
-    for part, bits in zip((values[:half], values[half:]), chip_orders()):
-        for bit in bits:
-            part = jnp.concatenate([part, flip(part, bit)], axis=0)
-        out.append(part)
-    return jnp.concatenate(out, axis=0)
-
-
-def collect(parts):
+    parts = [values[:half], values[half:]]
+    for step in range(len(chip_orders()[0]) - 1):
+        parts = joined(spread_step(parts, step))
+    return parts
+
+
+def spread_end(parts):
+    return joined(spread_step(parts, len(chip_orders()[0]) - 1))
+
+
+def collect(parts, after=None):
     half = parts.shape[0] // 2
-    out = []
-    for part, bits in zip((parts[:half], parts[half:]), chip_orders()):
-        for bit in bits[::-1]:
-            count = part.shape[0] // 2
-            got = flip(part[count:].astype(BF), bit)
-            part = part[:count].astype(F32) + got.astype(F32)
-        out.append(part)
-    return jnp.concatenate(out, axis=0)
+    parts = [parts[:half], parts[half:]]
+    count = len(chip_orders()[0])
+    sent = []
+    for step in reversed(range(count)):
+        sums, sends = [], []
+        for part, bits in zip(parts, chip_orders()):
+            size = part.shape[0] // 2
+            send = part[size:].astype(BF)
+            sends.append(tie(send, after) if after is not None and step == 0 else send)
+            got = flip(sends[-1], bits[step])
+            sums.append(part[:size].astype(F32) + got.astype(F32))
+        parts = sums
+        sent.append(sends)
+    return jnp.concatenate(parts, axis=0), sent
+
+
+def tie_all(value, others):
+    for other in others:
+        value = tie(value, other)
+    return value
 
 
 def pad_cols(values, cols):
@@ -214,6 +227,7 @@
 
 
 VMEM_LIMIT = 60 * 1024 * 1024
+NO_COST = pl.CostEstimate(flops=0, bytes_accessed=0, transcendentals=0)
 NT = (((1,), (1,)), ((), ()))
 TN = (((0,), (0,)), ((), ()))
 
@@ -238,6 +252,7 @@
         out_specs=pl.BlockSpec(memory_space=pl.ANY),
         input_output_aliases={0: 0},
         compiler_params=pltpu.CompilerParams(has_side_effects=True),
+        cost_estimate=NO_COST,
     )(value, other)
 
 
@@ -311,9 +326,7 @@
             jax.ShapeDtypeStruct((2 * half, H * LANES), F32),
         ],
         compiler_params=pltpu.CompilerParams(vmem_limit_bytes=VMEM_LIMIT),
-        cost_estimate=pl.CostEstimate(
-            flops=4 * half * half * Q_COLS * 9, bytes_accessed=8 << 20, transcendentals=0
-        ),
+        cost_estimate=NO_COST,
     )(info, query, kv)
 
 
@@ -395,9 +408,7 @@
             jax.ShapeDtypeStruct(kv.shape, BF),
         ],
         compiler_params=pltpu.CompilerParams(vmem_limit_bytes=VMEM_LIMIT),
-        cost_estimate=pl.CostEstimate(
-            flops=10 * half * half * Q_COLS * 9, bytes_accessed=12 << 20, transcendentals=0
-        ),
+        cost_estimate=NO_COST,
     )(info, query, grad, mixed, total, kv)
 
 
@@ -405,53 +416,76 @@
 GELU_B = 0.044715
 
 
-def mlp_kernel(x_ref, own_ref, other_ref, part_ref, gate_up_ref, hidden_ref):
-    units = own_ref.shape[1] // 3
-    total = None
+def mlp_up_kernel(x_ref, own_ref, other_ref, gate_up_ref, hidden_ref):
+    units = own_ref.shape[1] // 2
     for k, w_ref in enumerate((own_ref, other_ref)):
-        both = dot(x_ref[...], w_ref[:, : 2 * units])
+        both = dot(x_ref[...], w_ref[...])
         gate_up_ref[:, k * 2 * units : (k + 1) * 2 * units] = both.astype(BF)
         gate, up = both[:, :units], both[:, units:]
         inner = jnp.tanh(GELU_A * gate * (1.0 + GELU_B * gate * gate))
         hidden = (0.5 * gate * (1.0 + inner) * up).astype(BF)
         hidden_ref[:, k * units : (k + 1) * units] = hidden
-        part = dot(hidden, w_ref[:, 2 * units :], NT)
-        total = part if total is None else total + part
-    part_ref[...] = total.astype(BF)
+
+
+def mlp_down_kernel(hidden_ref, own_ref, other_ref, part_ref):
+    units = own_ref.shape[1]
+    total = dot(hidden_ref[:, :units], own_ref[...], NT)
+    part_ref[...] = (total + dot(hidden_ref[:, units:], other_ref[...], NT)).astype(BF)
 
 
 def mlp_tile(rows):
     return min(rows, 512)
 
 
-def mlp_forward(x, own, other):
+def mlp_up(x, own, other):
     rows, width = x.shape
-    units = own.shape[1] // 3
+    units = own.shape[1] // 2
     tile = mlp_tile(rows)
     spec = lambda cols: pl.BlockSpec((tile, cols), lambda i: (i, 0))
     return pl.pallas_call(
-        mlp_kernel,
+        mlp_up_kernel,
         grid=(rows // tile,),
         in_specs=[spec(width), whole(own.shape), whole(own.shape)],
-        out_specs=[spec(width), spec(4 * units), spec(2 * units)],
+        out_specs=[spec(4 * units), spec(2 * units)],
         out_shape=[
-            jax.ShapeDtypeStruct((rows, width), BF),
             jax.ShapeDtypeStruct((rows, 4 * units), BF),
             jax.ShapeDtypeStruct((rows, 2 * units), BF),
         ],
         compiler_params=pltpu.CompilerParams(vmem_limit_bytes=VMEM_LIMIT),
-        cost_estimate=pl.CostEstimate(
-            flops=12 * rows * width * units, bytes_accessed=32 << 20, transcendentals=0
-        ),
+        cost_estimate=NO_COST,
     )(x, own, other)
 
 
-def mlp_back_kernel(grad_ref, gate_up_ref, own_ref, other_ref, part_ref, gate_up_grad_ref):
-    units = own_ref.shape[1] // 3
+def mlp_down(hidden, own, other):
+    rows, (width, units) = hidden.shape[0], own.shape
+    tile = mlp_tile(rows)
+    spec = lambda cols: pl.BlockSpec((tile, cols), lambda i: (i, 0))
+    return pl.pallas_call(
+        mlp_down_kernel,
+        grid=(rows // tile,),
+        in_specs=[spec(2 * units), whole(own.shape), whole(own.shape)],
+        out_specs=spec(width),
+        out_shape=jax.ShapeDtypeStruct((rows, width), BF),
+        compiler_params=pltpu.CompilerParams(vmem_limit_bytes=VMEM_LIMIT),
+        cost_estimate=NO_COST,
+    )(hidden, own, other)
+
+
+def mlp_back_kernel(
+    grad_ref,
+    gate_up_ref,
+    own_ref,
+    other_ref,
+    own_down_ref,
+    other_down_ref,
+    part_ref,
+    gate_up_grad_ref,
+):
+    units = own_down_ref.shape[1]
     total = None
-    for k, w_ref in enumerate((own_ref, other_ref)):
+    for k, (w_ref, down_ref) in enumerate(((own_ref, own_down_ref), (other_ref, other_down_ref))):
         base = k * 2 * units
-        hidden_grad = dot(grad_ref[...], w_ref[:, 2 * units :])
+        hidden_grad = dot(grad_ref[...], down_ref[...])
         gate = gate_up_ref[:, base : base + units].astype(F32)
         up = gate_up_ref[:, base + units : base + 2 * units].astype(F32)
         square = gate * gate
@@ -464,30 +498,67 @@
         up_grad = (hidden_grad * (gate * half)).astype(BF)
         gate_up_grad_ref[:, base : base + units] = gate_grad
         gate_up_grad_ref[:, base + units : base + 2 * units] = up_grad
-        part = dot(gate_up_grad_ref[:, base : base + 2 * units], w_ref[:, : 2 * units], NT)
+        part = dot(gate_up_grad_ref[:, base : base + 2 * units], w_ref[...], NT)
         total = part if total is None else total + part
     part_ref[...] = total.astype(BF)
 
 
-def mlp_backward(grad, gate_up, own, other):
+def mlp_backward(grad, gate_up, weights):
     rows, width = grad.shape
-    units = own.shape[1] // 3
+    units = weights[2].shape[1]
     tile = mlp_tile(rows)
     spec = lambda cols: pl.BlockSpec((tile, cols), lambda i: (i, 0))
     return pl.pallas_call(
         mlp_back_kernel,
         grid=(rows // tile,),
-        in_specs=[spec(width), spec(4 * units), whole(own.shape), whole(own.shape)],
+        in_specs=[spec(width), spec(4 * units)] + [whole(w.shape) for w in weights],
         out_specs=[spec(width), spec(4 * units)],
         out_shape=[
             jax.ShapeDtypeStruct((rows, width), BF),
             jax.ShapeDtypeStruct((rows, 4 * units), BF),
         ],
         compiler_params=pltpu.CompilerParams(vmem_limit_bytes=VMEM_LIMIT),
-        cost_estimate=pl.CostEstimate(
-            flops=12 * rows * width * units, bytes_accessed=32 << 20, transcendentals=0
-        ),
-    )(grad, gate_up, own, other)
+        cost_estimate=NO_COST,
+    )(grad, gate_up, *weights)
+
+
+def products(lefts, rights, units, kind):
+    rows, width = lefts[0].shape
+    kinds = rights[0].shape[1] // (2 * units)
+    left = pl.BlockSpec((rows, width), lambda j: (0, 0))
+    right = pl.BlockSpec((rows, units), lambda j: (0, kind + kinds * (1 - j)))
+    out = pl.BlockSpec((width, units), lambda j: (0, 0))
+    shape = jax.ShapeDtypeStruct((width, units), BF)
+
+    def kernel(*refs):
+        left_refs, right_refs, (other_ref, own_ref, turned_ref) = refs[:2], refs[2:4], refs[4:]
+
+        @pl.when(pl.program_id(0) == 0)
+        def _():
+            for k in range(2):
+                turned_ref[:, k * rows : (k + 1) * rows] = left_refs[k][...].T
+
+        total = dot(turned_ref[:, :rows], right_refs[0][...])
+        total = (total + dot(turned_ref[:, rows:], right_refs[1][...])).astype(BF)
+
+        @pl.when(pl.program_id(0) == 0)
+        def _():
+            other_ref[...] = total
+
+        @pl.when(pl.program_id(0) == 1)
+        def _():
+            own_ref[...] = total
+
+    return pl.pallas_call(
+        kernel,
+        grid=(2,),
+        in_specs=[left, left, right, right],
+        out_specs=[out, out],
+        out_shape=[shape, shape],
+        scratch_shapes=[pltpu.VMEM((width, 2 * rows), BF)],
+        compiler_params=pltpu.CompilerParams(vmem_limit_bytes=VMEM_LIMIT),
+        cost_estimate=NO_COST,
+    )(*lefts, *rights)
 
 
 def body(
@@ -514,7 +585,7 @@
     gain_cols = jnp.zeros((max(rows, head_rows), LANES), BF)
     gain_cols = gain_cols.at[:rows, :4].set(norm_gains.astype(BF))
     gain_cols = gain_cols.at[:head_rows, 4:6].set(head_gains.astype(BF))[:rows]
-    first_shard = jnp.concatenate([weights_low[:, :START_GATE], gain_cols], axis=1)
+    first_shard = jnp.concatenate([weights_low[:, :START_GATE], pad_cols(gain_cols, 2 * LANES)], axis=1)
     mlp_shard = jnp.concatenate(
         [
             pad_cols(weights_low[:, start : start + FF], dp_count * units)
@@ -526,15 +597,14 @@
     )
     mlp_block = lax.all_to_all(mlp_shard, "dp", split_axis=0, concat_axis=0, tiled=True)
     mlp_block = mlp_block.reshape(dp_count * rows, 3 * units)
-    w_own = lax.all_gather(mlp_block, "ctx", axis=0, tiled=True)
-    w_other = flip(w_own, 1)
-    first_full = gather_rows(first_shard)
+    gate_up_block = mlp_block[:, : 2 * units]
+    gate_up_own = lax.all_gather(gate_up_block, "ctx", axis=0, tiled=True)
+    first_full = gather_rows(first_shard, gate_up_block)
     w_qkv = first_full[:, :START_GATE]
-    gain_part = first_full[:, START_GATE:].astype(F32)
+    gain_part = first_full[:, START_GATE : START_GATE + LANES].astype(F32)
     gain_f = 1.0 + gain_part[:, :4]
     head_f = gain_part.reshape(z_count, dp_count, rows, LANES)[:, :, :head_rows, 4:6]
     head_f = 1.0 + head_f.transpose(1, 0, 2, 3).reshape(HD, 2)
-    w_out = gather_rows(tie(weights_low[:, START_OUT:START_DOWN], first_full))
 
     order = np.arange(width).reshape(dp_count, z_count, rows).transpose(1, 0, 2).reshape(width)
     place = (jnp.arange(width)[:, None] == jnp.asarray(order)[None, :]).astype(BF)
@@ -549,26 +619,29 @@
     cot = jnp.dot(cotangent, place, preferred_element_type=F32)
     normed_in, pull_in = jax.vjp(rms_gain, inputs, gain_f[:, 0])
     normed_low = normed_in.astype(BF)
-    projected = jnp.dot(normed_low, w_qkv, preferred_element_type=F32)
-
-    def query_key(query_raw, key_raw, head_arg):
-        query_out = (
-            rotate(rms_gain(query_raw.reshape(tok_rows, H, HD), head_arg[:, 0]), positions)
-            * QUERY_SCALE
+    key_value_raw = jnp.dot(normed_low, w_qkv[:, Q_COLS:], preferred_element_type=F32)
+    query_raw = jnp.dot(normed_low, w_qkv[:, :Q_COLS], preferred_element_type=F32)
+
+    def query_part(query_arg, head_arg):
+        return (
+            rotate(rms_gain(query_arg.reshape(tok_rows, H, HD), head_arg), positions) * QUERY_SCALE
         )
-        key_out = rotate(rms_gain(key_raw[:, None, :], head_arg[:, 1]), positions)[:, 0]
-        return (query_out, key_out)
-
-    (queries, keys), pull_qk = jax.vjp(
-        query_key, projected[:, :Q_COLS], projected[:, Q_COLS : Q_COLS + HD], head_f
-    )
-    query_low = queries.astype(BF)
-    key_low = keys.astype(BF)
-    value_low = projected[:, Q_COLS + HD :].astype(BF)
-    key_value = gather_line(jnp.concatenate([key_low, value_low], axis=1), "ctx")
-    key_value = key_value.reshape(z_count * tok_rows, 2 * HD)
+
+    def key_part(key_arg, head_arg):
+        return rotate(rms_gain(key_arg[:, None, :], head_arg), positions)[:, 0]
+
+    keys, pull_key = jax.vjp(key_part, key_value_raw[:, :HD], head_f[:, 1])
+    key_value = jnp.concatenate([keys.astype(BF), key_value_raw[:, HD:].astype(BF)], axis=1)
+    w_out = gather_rows(tie(weights_low[:, START_OUT:START_DOWN], first_full))
+    queries, pull_query = jax.vjp(query_part, query_raw, head_f[:, 0])
+    query_low = queries.astype(BF).reshape(tok_rows, Q_COLS)
+    key_value = tie_all(key_value, [gate_up_own, w_out, query_low])
+    key_value = lax.all_gather(key_value, "ctx", axis=0, tiled=True)
+    down_own = lax.all_gather(
+        tie(mlp_block[:, 2 * units :], key_value), "ctx", axis=0, tiled=True
+    )
+    gate_up_weights = (gate_up_own, flip(gate_up_own, 1))
     info = jnp.stack([lax.axis_index("ctx"), seq_length]).astype(jnp.int32)
-    query_low = query_low.reshape(tok_rows, Q_COLS)
     mixed_low, inverse_total = attend(info, query_low, key_value)
     attn_proj = jnp.einsum("tc,dc->td", mixed_low, w_out, preferred_element_type=F32)
     post_attn, pull_attn = jax.vjp(rms_gain, attn_proj, gain_f[:, 1])
@@ -580,91 +653,146 @@
     chunks = 2
     size = tok_rows // chunks
     spans = [slice(i * size, (i + 1) * size) for i in range(chunks)]
-    mids = [spread(mid_low[span]) for span in spans]
-    forward = [mlp_forward(mid, w_own, w_other) for mid in mids]
+    assert chunks == 2
+    mids = [None, None]
+    starts = [spread_start(mid_low[span]) for span in spans]
+    mids[0] = jnp.concatenate(spread_end(starts[0]), axis=0)
+    mids[0] = tie_all(mids[0], starts[1] + [down_own])
+    second = spread_end(starts[1])
+    first_up = mlp_up(mids[0], *gate_up_weights)
+    mids[1] = tie(jnp.concatenate(second, axis=0), first_up[1])
+    forward = [first_up, mlp_up(mids[1], *gate_up_weights)]
+    gate_ups, hiddens = (list(kind) for kind in zip(*forward))
+    down_own = tie(down_own, mids[1])
+    mlp_weights = gate_up_weights + (down_own, flip(down_own, 1))
+    hiddens[0] = tie(hiddens[0], gate_ups[1])
+    parts = [mlp_down(hiddens[0], *mlp_weights[2:])]
+    first, sent = collect(parts[0])
+    hiddens[1] = tie_all(hiddens[1], sent[0])
+    parts.append(mlp_down(hiddens[1], *mlp_weights[2:]))
     grad_three = 0.0
-    output_low, mlp_grads = [], []
-    for span, (part, _, _) in zip(spans, forward):
-        post_mlp, pull_mlp = jax.vjp(rms_gain, collect(part), gain_f[:, 3])
+    output_low, starts = [], []
+    for i, span in enumerate(spans):
+        mlp_proj = collect(parts[1], starts[0][0])[0] if i else first
+        post_mlp, pull_mlp = jax.vjp(rms_gain, mlp_proj, gain_f[:, 3])
         output_low.append((residual_mid[span] + post_mlp).astype(BF))
         mlp_grad, gain_part_three = pull_mlp(out_grad[span])
         grad_three = grad_three + gain_part_three
-        mlp_grads.append(spread(mlp_grad.astype(BF)))
+        starts.append(spread_start(mlp_grad.astype(BF)))
     output_low = jnp.concatenate(output_low, axis=0)
-    backward = [
-        mlp_backward(grad, gate_up, w_own, w_other)
-        for grad, (_, gate_up, _) in zip(mlp_grads, forward)
-    ]
-    mid_grad = jnp.concatenate([collect(part) for part, _ in backward], axis=0)
-
-    def shard_sum(lefts, rights, cols):
-        def product(low):
-            total = 0.0
-            for left, right in zip(lefts, rights):
-                total = total + dot(left, right[:, low : low + cols], TN)
-            return total
-
-        other = product(cols).astype(BF)
-        grad = (product(0) + flip(other, 1).astype(F32)).astype(BF)
-        summed = lax.psum_scatter(grad, "ctx", scatter_dimension=0, tiled=True)
-        back = lax.all_to_all(
-            summed.reshape(dp_count, rows, cols), "dp", split_axis=0, concat_axis=0, tiled=True
+    mlp_grads = [jnp.concatenate(spread_end(starts[0]), axis=0)]
+    starts[1] = [tie(part, mlp_grads[0]) for part in starts[1]]
+    mlp_grads[0] = tie(tie(mlp_grads[0], starts[1][0]), starts[1][1])
+    second = spread_end(starts[1])
+
+    def both_cores(other, own):
+        return (own.astype(F32) + flip(other, 1).astype(F32)).astype(BF)
+
+    def shard_sum(grad):
+        return lax.psum_scatter(grad, "ctx", scatter_dimension=0, tiled=True)
+
+    def to_rows(summed):
+        return lax.all_to_all(
+            summed.reshape(dp_count, rows, summed.shape[1]), "dp", 0, 0, tiled=True
         )
-        return [
-            back[:, :, low : low + units]
-            .transpose(1, 0, 2)
-            .reshape(rows, dp_count * units)[:, :FF]
-            .astype(F32)
-            for low in range(0, cols, units)
-        ]
-
-    (sum_down,) = shard_sum(mlp_grads, [hidden for _, _, hidden in forward], units)
-    sum_gate, sum_up = shard_sum(mids, [grad for _, grad in backward], 2 * units)
-
+
+    backward = [mlp_backward(mlp_grads[0], gate_ups[0], mlp_weights)]
+    mlp_grads.append(jnp.concatenate(second, axis=0))
+    first, sent = collect(backward[0][0])
+    hiddens = [tie_all(hidden, sent[0]) for hidden in hiddens]
+    down_other, down_mine = products(mlp_grads, hiddens, units, 0)
+    down_grad = both_cores(down_other, tie_all(down_mine, sent[1]))
+    summed_down = shard_sum(down_grad)
+    backward.append(mlp_backward(mlp_grads[1], tie(gate_ups[1], down_mine), mlp_weights))
+    second, sent = collect(backward[1][0])
+    mid_grad = jnp.concatenate([first, second], axis=0)
+    gate_up_grads = [tie_all(grad, sent[1]) for _, grad in backward]
+    gate_other, gate_mine = products(mids, gate_up_grads, units, 0)
+    gate_grad = both_cores(gate_other, gate_mine)
+    summed_gate = shard_sum(gate_grad)
+    output = lax.dot_general(
+        tie(output_low, gate_mine), place, NT, preferred_element_type=F32
+    ).astype(BF)
+
+    mid_grad = tie_all(mid_grad, [gate_mine, summed_down, output])
     resid_part, grad_two = pull_mid(mid_grad)
     residual_grad = out_grad + resid_part
     attn_grad, grad_one = pull_attn(residual_grad)
     attn_low = attn_grad.astype(BF)
-    grad_out = jnp.einsum("td,tc->dc", attn_low, mixed_low, preferred_element_type=F32)
-    row_shape = (z_count, dp_count, rows)
-    sum_out = scatter_rows(grad_out.astype(BF).reshape(row_shape + (Q_COLS,)))
     mixed_grad = jnp.dot(attn_low, w_out, preferred_element_type=F32).astype(BF)
     query_grads, key_value_part = attend_back(
         info, query_low, mixed_grad, mixed_low, inverse_total, key_value
     )
-    key_value_grad = scatter_line(key_value_part.reshape(z_count, tok_rows, 2 * HD), "ctx")
-    raw_query, raw_key, grad_head = pull_qk(
-        (query_grads.reshape(tok_rows, H, HD), key_value_grad[:, :HD])
-    )
-    proj_low = jnp.concatenate([raw_query, raw_key, key_value_grad[:, HD:]], axis=1).astype(BF)
-    grad_qkv = jnp.einsum("td,tc->dc", normed_low, proj_low, preferred_element_type=F32)
-    in_part = jnp.einsum("tc,dc->td", proj_low, w_qkv, preferred_element_type=F32)
+    key_value_grad = lax.psum_scatter(
+        tie(key_value_part, summed_gate), "ctx", scatter_dimension=0, tiled=True
+    ).astype(F32)
+    gate_up_grads = [tie(grad, query_grads) for grad in gate_up_grads]
+    up_other, up_mine = products(mids, gate_up_grads, units, 1)
+    up_grad = both_cores(up_other, up_mine)
+    attn_late = tie(attn_low, query_grads)
+    summed_up = shard_sum(tie(up_grad, key_value_grad))
+
+    raw_query, grad_head_query = pull_query(query_grads.reshape(tok_rows, H, HD))
+    query_grad_low = raw_query.astype(BF)
+    bits_out, bits_query = ([1] + bits[::-1] for bits in chip_orders())
+    out_share = scatter_cols(dot(attn_late, mixed_low, TN), bits_out)
+    query_share = scatter_cols(dot(normed_low, query_grad_low, TN), bits_query)
+
+    key_value_grad = tie(key_value_grad, up_grad)
+    raw_key, grad_head_key = pull_key(key_value_grad[:, :HD])
+    key_value_low = jnp.concatenate([raw_key, key_value_grad[:, HD:]], axis=1).astype(BF)
+    late_bits, same_bits = bits_out[:2], bits_out[2:]
+    late_share, sent = scatter_cols_sent(dot(normed_low, key_value_low, TN), late_bits)
+    in_part = dot(query_grad_low, w_qkv[:, :Q_COLS], NT)
+    in_part = in_part + dot(tie(key_value_low, sent), w_qkv[:, Q_COLS:], NT)
     input_part, grad_zero = pull_in(in_part)
     grad_input_low = (residual_grad + input_part).astype(BF)
 
-    gain_grads = jnp.stack([grad_zero, grad_one, grad_two, grad_three], axis=1)
-    gain_grads = gain_grads.reshape(row_shape + (4,))
-    head_grads = grad_head.reshape(dp_count, z_count, head_rows, 2).transpose(1, 0, 2, 3)
-    side = jnp.zeros(row_shape + (LANES,), BF)
-    side = side.at[..., :4].set(gain_grads.astype(BF))
-    side = side.at[..., :head_rows, 4:6].set(head_grads.astype(BF))
-    qkv_parts = jnp.concatenate(
-        [grad_qkv.astype(BF).reshape(row_shape + (START_GATE,)), side], axis=-1
-    )
-    sum_first = scatter_rows(qkv_parts)
-    sum_qkv = sum_first[:, :START_GATE]
-    sum_gains = sum_first[:, START_GATE : START_GATE + 4]
-    sum_head = sum_first[:head_rows, START_GATE + 4 : START_GATE + 6]
-
-    output = lax.dot_general(
-        output_low, place, (((1,), (1,)), ((), ())), preferred_element_type=F32
-    ).astype(BF)
+    for bit in same_bits:
+        late_share = (late_share.astype(F32) + flip(late_share, bit).astype(F32)).astype(BF)
+    back = to_rows(jnp.concatenate([summed_gate, summed_up, summed_down], axis=1))
+    early = shard_sum(jnp.concatenate([query_share, out_share], axis=1))
+    late_share = tie(tie(late_share, back), early)
+    slices = scatter_parts(late_share.reshape(z_count, -1, late_share.shape[1]), "ctx")
+    back_attn = jnp.concatenate([early, scatter_direct(slices, "ctx").astype(BF)], axis=1)
+    back_attn = to_rows(back_attn)
+    share = Q_COLS // dp_count
+    sum_query = columns_back(back_attn[:, :, :share], bits_query)
+    sum_out = columns_back(back_attn[:, :, share : 2 * share], bits_out)
+    back_late = back_attn[:, :, 2 * share :]
+    back_late = back_late.reshape((2,) * len(bits_out) + back_late.shape[1:])
+    for bit in sorted(same_bits):
+        back_late = back_late[(slice(None),) * (len(bits_out) - bit.bit_length()) + (0,)]
+    back_late = back_late.reshape((-1,) + back_late.shape[-2:])
+    sum_late = columns_back(back_late, late_bits)
+
+    gains = jnp.stack([grad_zero, grad_one, grad_two, grad_three]).reshape(-1)
+    gains = jnp.concatenate([gains, grad_head_query, grad_head_key]).reshape(-1, LANES)
+    for bit in bits_out:
+        gains = gains + flip(gains, bit)
+    gains = sum(shift(gains, "ctx", distance) for distance in range(1, z_count)) + gains
+    gains = gains.reshape(-1)
+    dp_me, z_me = lax.axis_index("dp"), lax.axis_index("ctx")
+    sum_gains = lax.dynamic_slice_in_dim(
+        gains[: 4 * width].reshape(4, width), (z_me * dp_count + dp_me) * rows, rows, 1
+    ).T
+    sum_head = lax.dynamic_slice_in_dim(
+        gains[4 * width :].reshape(2, HD), (dp_me * z_count + z_me) * head_rows, head_rows, 1
+    ).T
+    sum_gate, sum_up, sum_down = (
+        back[:, :, at : at + units]
+        .transpose(1, 0, 2)
+        .reshape(rows, dp_count * units)[:, :FF]
+        .astype(F32)
+        for at in (0, units, 2 * units)
+    )
+
     grad_input = lax.dot_general(
         grad_input_low, place, (((1,), (1,)), ((), ())), preferred_element_type=F32
     ).astype(BF)
 
     sum_weights = jnp.concatenate(
-        [sum_qkv, sum_gate, sum_up, sum_out, sum_down], axis=1
+        [sum_query, sum_late, sum_gate, sum_up, sum_out, sum_down], axis=1
     )
     new_w, first_w, second_w = adamw(
         weights, sum_weights, moment_weights, square_weights, RATE_WEIGHTS, WEIGHT_DECAY

time: 838 us -> 800 us (0.955)
  Pallas kernels: 127 us -> 189 us
  matrix products: 94.3 us -> 37.2 us
  starting transfers between devices: 140 us -> 95.2 us
  local copies, waits for them, and re-layouts: 123 us -> 94.6 us
  other arithmetic: 97 us -> 114 us
  waiting for transfers between devices: 229 us -> 243 us
    ppermute x12 -> x0, waiting for transfers between devices: 93.8 us -> none  [the longest x3 75.8 us: gather_line(): lax.ppermute(down, axis, [(i, i - 1) for i in range(1, count - step + 1)])]
    all_gather x1 -> x3, waiting for transfers between devices: 0.01 us -> 73.2 us  [the longest x1 45.3 us: body(): key_value = lax.all_gather(key_value, 'ctx', axis=0, tiled=True)]
    pallas_call x2 -> x7, Pallas kernels: 42.8 us -> 106 us  [the longest x3 53.7 us: products(): pl.pallas_call(kernel, grid=(2,), in_specs=[left, left, right, right], ou...]
    dot_general x8 -> x5, matrix products: 56.9 us -> 12.1 us  [dot(): return lax.dot_general(left, right, dims, preferred_element_type=F32)]
    ppermute x12 -> x0, starting transfers between devices: 34.7 us -> none  [the longest x3 18 us: scatter_line(): lax.ppermute(up_out.astype(BF), axis, [(i, i + 1) for i in range(step)])]
    ppermute x59 -> x61, waiting for transfers between devices: 124 us -> 143 us  [flip(): lax.ppermute(values, 'dp', [(i ^ bit, i) for i in range(lax.axis_size('dp...]
    ppermute x12, waiting for transfers between devices: 0.04 us -> 17.9 us  [shift(): lax.ppermute(values, axis, [((i + distance) % count, i) for i in range(co...]
    ppermute x12, starting transfers between devices: 41 us -> 25.5 us  [shift(): lax.ppermute(values, axis, [((i + distance) % count, i) for i in range(co...]
  transfers between devices with their start and end apart: 89 -> 84, of which waited for: 32 -> 37; matrix products, arithmetic and copies ran while one was open for 32% -> 23% of each run, Pallas kernels for 13% -> 18%
where the time goes in v3:
time: 800 us; the launch traced here: 791 us
  waiting for transfers between devices  243 us (30%)
  Pallas kernels  189 us (24%)
  other arithmetic  114 us (14%)
  starting transfers between devices  95.2 us (12%)
  local copies, waits for them, and re-layouts  94.6 us (12%)
  matrix products  37.2 us (5%)
  between operations  17.8 us (2%)
    ppermute x61, waiting for transfers between devices, flip(): lax.ppermute(values, 'dp', [(i ^ bit, i) for i in range(lax.axis_size('dp...  143 us
    ppermute x61, starting transfers between devices, flip(): lax.ppermute(values, 'dp', [(i ^ bit, i) for i in range(lax.axis_size('dp...  56.7 us
    pallas_call x2, Pallas kernels, mlp_backward(): pl.pallas_call(mlp_back_kernel, grid=(rows // tile,), in_specs=[spec(widt...  54.1 us
    pallas_call x3, Pallas kernels, products(): pl.pallas_call(kernel, grid=(2,), in_specs=[left, left, right, right], ou...  53.7 us
    all_gather x1, waiting for transfers between devices, body(): key_value = lax.all_gather(key_value, 'ctx', axis=0, tiled=True)  45.3 us
    unnamed x319, local copies, waits for them, and re-layouts  43.9 us
    pallas_call x2, Pallas kernels, mlp_up(): pl.pallas_call(mlp_up_kernel, grid=(rows // tile,), in_specs=[spec(width)...  32.5 us
    all_gather x1, waiting for transfers between devices, body(): gate_up_own = lax.all_gather(gate_up_block, 'ctx', axis=0, tiled=True)  27.9 us
  transfers between devices with their start and end apart: 84, of which 37 were waited for; matrix products, arithmetic and copies ran while one was open for 23% of the time, Pallas kernels for 18%

profile of v3, /device:TPU:0, one launch (start us, length us, event | category | flops | bytes accessed | tf_op | source)
XLA Modules:
  0.0 791.3 jit_solution(17834377723325899792)
XLA Ops:
  11.7 5.3 all-to-all-start
  24.7 3.1 collective-permute-start.2
  31.7 6.0 collective-permute-done.2
  48.3 2.4 collective-permute-done.4
  53.4 3.0 collective-permute-done.6
  56.6 7.5 collective-permute-done.5
  64.5 3.6 collective-permute-done.7
  71.3 3.3 multiply_reduce_fusion.8
  76.6 3.9 broadcast_select_fusion
  86.3 2.8 fusion.76
  96.6 6.1 collective-permute-start.11
  102.7 3.8 collective-permute-start.10
  107.3 4.8 collective-permute-done.11
  117.2 2.6 collective-permute-done.13
  124.4 3.0 collective-permute-done.16
  136.9 27.9 %all-gather.4.cloned.1.call-done.other_ref.own_ref = bf16[1152,1792]{1,0:T(8,128)(2,1)} async-done(((bf16[288,1792]{1,0:T(8,128)(2,1)}), bf16[1152,1792]{1,0:T(8,128)(2,1)}) %all-gather.4.cloned.1.call-update) | async-done | bytes 4128784 | tf_op jit(solution)/shard_map/all_gather | solution.py:601
  166.2 45.3 %all-gather.6.cloned.1.call-done.kv_ref.other_ref = bf16[2048,512]{1,0:T(8,128)(2,1)} async-done(((bf16[512,512]{1,0:T(8,128)(2,1)}), bf16[2048,512]{1,0:T(8,128)(2,1)}) %all-gather.6.cloned.1.call-update) | async-done | bytes 2097168 | tf_op jit(solution)/shard_map/all_gather | solution.py:639
  211.4 10.0 %shard_map.225 = (bf16[512,1024]{1,0:T(8,128)(2,1)}, f32[512,512]{1,0:T(8,128)}) custom-call(s32[2]{0:T(128)} %pad_add_fusion.2.info_ref, bf16[512,1024]{1,0:T(8,128)(2,1)} %bitcast.181, bf16[2048,512]{1,0:T(8,128)(2,1)} %all-gather.6.cloned.1.call-done.kv_ref.other_ref), custom_call_target="tpu_custom_call" | custom-call | tf_op jit(solution)/shard_map/pallas_call | solution.py:315
  221.5 3.1 multiply_reduce_fusion.7
  234.1 4.2 collective-permute-done.18
  240.9 2.5 collective-permute-done.22
  254.6 6.5 collective-permute-done.19
  261.2 10.8 %collective-permute-done.25 = bf16[256,1152]{1,0:T(8,128)(2,1)S(1)} collective-permute-done((bf16[256,1152]{1,0:T(8,128)(2,1)S(1)}, bf16[256,1152]{1,0:T(8,128)(2,1)S(1)}, u32[]{:S(2)}, u32[]{:S(2)}) %collective-permute-start.25) | collective-permute-done | bytes 589856 | tf_op jit(solution)/shard_map/ppermute | solution.py:77
  279.7 16.4 %shard_map.230 = (bf16[1024,3584]{1,0:T(8,128)(2,1)}, bf16[1024,1792]{1,0:T(8,128)(2,1)}) custom-call(bf16[1024,1152]{1,0:T(8,128)(2,1)} %shard_map.229.x_ref.refs_0_, bf16[1152,1792]{1,0:T(8,128)(2,1)} %all-gather.4.cloned.1.call-done.other_ref.own_ref, bf16[1152,1792]{1,0:T(8,128)(2,1)} %collective-permute-done.24.other_ref), custom_call_target="tpu_custom_call" | custom-call | tf_op jit(solution)/shard_map/pallas_call | solution.py:445
  296.1 16.2 %shard_map.232 = (bf16[1024,3584]{1,0:T(8,128)(2,1)}, bf16[1024,1792]{1,0:T(8,128)(2,1)}) custom-call(bf16[1024,1152]{1,0:T(8,128)(2,1)} %shard_map.231.x_ref.other_ref.refs_1_, bf16[1152,1792]{1,0:T(8,128)(2,1)} %all-gather.4.cloned.1.call-done.other_ref.own_ref, bf16[1152,1792]{1,0:T(8,128)(2,1)} %collective-permute-done.24.other_ref), custom_call_target="tpu_custom_call" | custom-call | tf_op jit(solution)/shard_map/pallas_call | solution.py:445
  313.6 9.5 %shard_map.235 = bf16[1024,1152]{1,0:T(8,128)(2,1)} custom-call(bf16[1024,1792]{1,0:T(8,128)(2,1)} %shard_map.233.hidden_ref.value_ref, bf16[1152,896]{1,0:T(8,128)(2,1)} %shard_map.234.own_ref.own_down_ref, bf16[1152,896]{1,0:T(8,128)(2,1)} %copy-done.11), custom_call_target="tpu_custom_call" | custom-call | tf_op jit(solution)/shard_map/pallas_call | solution.py:463
  329.6 10.3 %shard_map.238 = bf16[1024,1152]{1,0:T(8,128)(2,1)} custom-call(bf16[1024,1792]{1,0:T(8,128)(2,1)} %shard_map.237.hidden_ref.value_ref, bf16[1152,896]{1,0:T(8,128)(2,1)} %shard_map.234.own_ref.own_down_ref, bf16[1152,896]{1,0:T(8,128)(2,1)} %copy-done.11), custom_call_target="tpu_custom_call" | custom-call | tf_op jit(solution)/shard_map/pallas_call | solution.py:463
  347.9 5.6 collective-permute-done.31
  353.6 12.6 %collective-permute-done.29 = bf16[128,1152]{1,0:T(8,128)(2,1)S(1)} collective-permute-done((bf16[128,1152]{1,0:T(8,128)(2,1)S(1)}, bf16[128,1152]{1,0:T(8,128)(2,1)S(1)}, u32[]{:S(2)}, u32[]{:S(2)}) %collective-permute-start.29) | collective-permute-done | bytes 294944 | tf_op jit(solution)/shard_map/ppermute | solution.py:77
  372.6 2.6 collective-permute-done.33
  383.1 12.8 %collective-permute-done.36 = bf16[128,1152]{1,0:T(8,128)(2,1)} collective-permute-done((bf16[128,1152]{1,0:T(8,128)(2,1)}, bf16[128,1152]{1,0:T(8,128)(2,1)}, u32[]{:S(2)}, u32[]{:S(2)}) %collective-permute-start.36) | collective-permute-done | bytes 294944 | tf_op jit(solution)/shard_map/ppermute | solution.py:77
  403.5 3.6 collective-permute-done.41
  414.3 27.2 %shard_map.245 = (bf16[1024,1152]{1,0:T(8,128)(2,1)}, bf16[1024,3584]{1,0:T(8,128)(2,1)}) custom-call(bf16[1024,1152]{1,0:T(8,128)(2,1)} %shard_map.244.grad_ref.refs_0_, bf16[1024,3584]{1,0:T(8,128)(2,1)} %get-tuple-element.58.gate_up_ref, bf16[1152,1792]{1,0:T(8,128)(2,1)} %all-gather.4.cloned.1.call-done.other_ref.own_ref, ...), custom_call_target="tpu_custom_call" | custom-call | tf_op jit(solution)/shard_map/pallas_call | solution.py:511
  444.9 4.9 pad_maximum_fusion.2.refs_1_.grad_ref
  449.9 17.7 %shard_map.250 = (bf16[1152,896]{1,0:T(8,128)(2,1)}, bf16[1152,896]{1,0:T(8,128)(2,1)}) custom-call(bf16[1024,1152]{1,0:T(8,128)(2,1)} %shard_map.244.grad_ref.refs_0_, bf16[1024,1152]{1,0:T(8,128)(2,1)} %pad_maximum_fusion.2.refs_1_.grad_ref, bf16[1024,1792]{1,0:T(8,128)(2,1)} %shard_map.247.refs_2_, bf16[1024,1792]{1,0:T(8,128)(2,1)} %shard_map.249.refs_3_), custom_call_target="tpu_custom_call" | custom-call | tf_op jit(solution)/shard_map/pallas_call | solution.py:552
  469.8 27.0 %shard_map.252 = (bf16[1024,1152]{1,0:T(8,128)(2,1)}, bf16[1024,3584]{1,0:T(8,128)(2,1)}) custom-call(bf16[1024,1152]{1,0:T(8,128)(2,1)} %pad_maximum_fusion.2.refs_1_.grad_ref, bf16[1024,3584]{1,0:T(8,128)(2,1)} %shard_map.251.gate_up_ref, bf16[1152,1792]{1,0:T(8,128)(2,1)} %all-gather.4.cloned.1.call-done.other_ref.own_ref, ...), custom_call_target="tpu_custom_call" | custom-call | tf_op jit(solution)/shard_map/pallas_call | solution.py:511
  496.7 2.5 fusion.85
  504.3 4.0 add_convert_fusion.2
  511.5 10.4 %collective-permute-done.49 = bf16[128,1152]{1,0:T(8,128)(2,1)} collective-permute-done((bf16[128,1152]{1,0:T(8,128)(2,1)}, bf16[128,1152]{1,0:T(8,128)(2,1)}, u32[]{:S(2)}, u32[]{:S(2)}) %collective-permute-start.49) | collective-permute-done | bytes 294944 | tf_op jit(solution)/shard_map/ppermute | solution.py:77
  526.9 17.9 %shard_map.257 = (bf16[1152,896]{1,0:T(8,128)(2,1)}, bf16[1152,896]{1,0:T(8,128)(2,1)}) custom-call(bf16[1024,1152]{1,0:T(8,128)(2,1)} %shard_map.229.x_ref.refs_0_, bf16[1024,1152]{1,0:T(8,128)(2,1)} %shard_map.231.x_ref.other_ref.refs_1_, bf16[1024,3584]{1,0:T(8,128)(2,1)} %shard_map.254.refs_2_.value_ref, bf16[1024,3584]{1,0:T(8,128)(2,1)} %shard_map.256.refs_3_.value_ref), custom_call_target="tpu_custom_call" | custom-call | tf_op jit(solution)/shard_map/pallas_call | solution.py:552
  548.7 4.2 fusion.9.other_ref
  552.9 3.4 collective-permute-done.51
  561.5 3.4 add_convert_fusion.1
  566.8 3.0 multiply_reduce_fusion
  570.3 3.6 multiply_reduce_fusion.1
  576.4 2.5 convolution_convert_fusion.3.grad_ref
  578.9 19.1 %shard_map.264 = (f32[512,1024]{1,0:T(8,128)}, bf16[2048,512]{1,0:T(8,128)(2,1)}) custom-call(s32[2]{0:T(128)} %pad_add_fusion.2.info_ref, bf16[512,1024]{1,0:T(8,128)(2,1)} %bitcast.182, bf16[512,1024]{1,0:T(8,128)(2,1)} %convolution_convert_fusion.3.grad_ref, bf16[512,1024]{1,0:T(8,128)(2,1)} %get-tuple-element.54.mixed_ref, ...), custom_call_target="tpu_custom_call" | custom-call | tf_op jit(solution)/shard_map/pallas_call | solution.py:397
  601.0 3.2 mul.793
  604.2 2.4 multiply_add_fusion.2
  606.6 2.8 multiply_reduce_fusion.9
  611.4 3.0 convolution_convert_fusion
  623.0 18.2 %shard_map.268 = (bf16[1152,896]{1,0:T(8,128)(2,1)}, bf16[1152,896]{1,0:T(8,128)(2,1)}) custom-call(bf16[1024,1152]{1,0:T(8,128)(2,1)} %shard_map.229.x_ref.refs_0_, bf16[1024,1152]{1,0:T(8,128)(2,1)} %shard_map.231.x_ref.other_ref.refs_1_, bf16[1024,3584]{1,0:T(8,128)(2,1)} %shard_map.266.refs_2_, bf16[1024,3584]{1,0:T(8,128)(2,1)} %shard_map.267.refs_3_), custom_call_target="tpu_custom_call" | custom-call | tf_op jit(solution)/shard_map/pallas_call | solution.py:552
  647.8 12.3 %collective-permute-done.59 = bf16[1152,256]{1,0:T(8,128)(2,1)S(1)} collective-permute-done((bf16[1152,256]{1,0:T(8,128)(2,1)S(1)}, bf16[1152,256]{1,0:T(8,128)(2,1)S(1)}, u32[]{:S(2)}, u32[]{:S(2)}) %collective-permute-start.59) | collective-permute-done | bytes 589856 | tf_op jit(solution)/shard_map/ppermute | solution.py:77
  663.1 2.5 collective-permute-start.57
  684.5 4.8 multiply_reduce_fusion.2
  692.2 2.6 collective-permute-done.68
  695.3 6.5 fusion.10
  702.4 3.8 collective-permute-start.70
  713.4 3.9 all-to-all-start.1
  721.0 24.3 %collective-permute-done.63 = bf16[1152,128]{1,0:T(8,128)(2,1)S(1)} collective-permute-done((bf16[1152,128]{1,0:T(8,128)(2,1)S(1)}, bf16[1152,128]{1,0:T(8,128)(2,1)S(1)}, u32[]{:S(2)}, u32[]{:S(2)}) %collective-permute-start.63) | collective-permute-done | bytes 294944 | tf_op jit(solution)/shard_map/ppermute | solution.py:77
  750.3 2.8 collective-permute-start.64
  760.0 3.4 all-to-all-start.2
  764.1 5.9 all-to-all-done.2
  774.8 9.2 %fusion.79 = (bf16[36,23296]{1,0:T(8,128)(2,1)}, f32[36,23296]{1,0:T(8,128)}, f32[36,23296]{1,0:T(8,128)}, f32[36,23296]{1,0:T(8,128)}) fusion(f32[36,23296]{1,0:T(8,128)} %param.20, bf16[36,23296]{1,0:T(8,128)(2,1)} %slice_dynamic-update-slice_fusion, f32[36,23296]{1,0:T(8,128)} %param.23, f32[36,23296]{1,0:T(8,128)} %param.26), kind=kLoop, calls=%fused_computation.340 | loop fusion | flops 14257152 | bytes 23482368 | tf_op jit(solution)/shard_map/convert_element_type | solution.py:818
  (728 shorter events, 249.9 us)
Async XLA Ops:
  11.7 28.2 %all-to-all-start = ((bf16[8,36,2688]{2,1,0:T(8,128)(2,1)}), bf16[8,36,2688]{2,1,0:T(8,128)(2,1)}, u32[]{:S(2)}, u32[]{:S(2)}) async-start(bf16[8,36,2688]{2,1,0:T(8,128)(2,1)} %pad_maximum_fusion.5), calls=%async_computation | async-start | bytes 3440640 | tf_op jit(solution)/shard_map/all_to_all | solution.py:598
  17.1 147.8 %all-gather.4.cloned.1.call-start = ((), (), s32[]{:S(2)}) async-start(), calls=%async_computation.8 | async-start | bytes 5160960 | tf_op jit(solution)/shard_map/all_gather | solution.py:601
  24.7 12.9 %collective-permute-start.2 = (bf16[72,896]{1,0:T(8,128)(2,1)S(1)}, bf16[72,896]{1,0:T(8,128)(2,1)S(1)}, u32[]{:S(2)}, u32[]{:S(2)}) collective-permute-start(bf16[72,896]{1,0:T(8,128)(2,1)S(1)} %pad_maximum_fusion.33), channel_id=1, source_target_pairs={{2,0},{3,1},{0,2},{1,3},{6,4},{7,5},{4,6},{5,7},{10,8},{11,9},{8,1... | collective-permute-start | bytes 387080 | tf_op jit(solution)/shard_map/ppermute | solution.py:73
  27.8 9.8 %collective-permute-start.3 = (bf16[72,896]{1,0:T(8,128)(2,1)S(1)}, bf16[72,896]{1,0:T(8,128)(2,1)S(1)}, u32[]{:S(2)}, u32[]{:S(2)}) collective-permute-start(bf16[72,896]{1,0:T(8,128)(2,1)S(1)} %pad_maximum_fusion.33), channel_id=1, source_target_pairs={{3,0},{0,1},{1,2},{2,3},{7,4},{4,5},{5,6},{6,7},{11,8},{8,9},{9,10... | collective-permute-start | bytes 387080 | tf_op jit(solution)/shard_map/ppermute | solution.py:73
  29.4 9.5 %collective-permute-start.1 = (bf16[72,896]{1,0:T(8,128)(2,1)S(1)}, bf16[72,896]{1,0:T(8,128)(2,1)S(1)}, u32[]{:S(2)}, u32[]{:S(2)}) collective-permute-start(bf16[72,896]{1,0:T(8,128)(2,1)S(1)} %pad_maximum_fusion.33), channel_id=1, source_target_pairs={{1,0},{2,1},{3,2},{0,3},{5,4},{6,5},{7,6},{4,7},{9,8},{10,9},{11,1... | collective-permute-start | bytes 387080 | tf_op jit(solution)/shard_map/ppermute | solution.py:73
  46.8 9.6 %collective-permute-start.6 = (bf16[4,72,512]{2,1,0:T(8,128)(2,1)S(1)}, bf16[4,72,512]{2,1,0:T(8,128)(2,1)S(1)}, u32[]{:S(2)}, u32[]{:S(2)}) collective-permute-start(bf16[4,72,512]{2,1,0:T(8,128)(2,1)S(1)} %slice.357), channel_id=1, source_target_pairs={{16,0},{20,4},{24,8},{28,12},{0,16},{4,20},{8,24},{12,28},{17,1},{... | collective-permute-start | bytes 884744 | tf_op jit(solution)/shard_map/ppermute | solution.py:77
  51.8 12.3 %collective-permute-start.5 = (bf16[4,2,72,384]{3,2,0,1:T(8,128)(2,1)S(1)}, bf16[4,2,72,384]{3,2,0,1:T(8,128)(2,1)S(1)}, u32[]{:S(2)}, u32[]{:S(2)}) collective-permute-start(bf16[4,2,72,384]{3,2,0,1:T(8,128)(2,1)S(1)} %pad_maximum_fusion.28), channel_id=1, source_target_pairs={{16,0},{20,4},{24,8},{28,12},{0,16},{4,20},{8,24},{12,28},{17,1},{... | collective-permute-start | bytes 1327112 | tf_op jit(solution)/shard_map/ppermute | solution.py:77
  56.5 11.5 %collective-permute-start.7 = (bf16[4,2,72,512]{3,2,0,1:T(8,128)(2,1)S(1)}, bf16[4,2,72,512]{3,2,0,1:T(8,128)(2,1)S(1)}, u32[]{:S(2)}, u32[]{:S(2)}) collective-permute-start(bf16[4,2,72,512]{3,2,0,1:T(8,128)(2,1)S(1)} %pad_maximum_fusion.13), channel_id=1, source_target_pairs={{8,0},{12,4},{0,8},{4,12},{24,16},{28,20},{16,24},{20,28},{9,1},{1... | collective-permute-start | bytes 1769480 | tf_op jit(solution)/shard_map/ppermute | solution.py:77
  76.4 135.0 %all-gather.6.cloned.1.call-start = ((), (), s32[]{:S(2)}) async-start(), calls=%async_computation.9 | async-start | bytes 2621440 | tf_op jit(solution)/shard_map/all_gather | solution.py:639
  96.6 15.5 %collective-permute-start.11 = (bf16[72,512]{1,0:T(8,128)(2,1)S(1)}, bf16[72,512]{1,0:T(8,128)(2,1)S(1)}, u32[]{:S(2)}, u32[]{:S(2)}) collective-permute-start(bf16[72,512]{1,0:T(8,128)(2,1)S(1)} %pad_maximum_fusion.34), channel_id=1, source_target_pairs={{2,0},{3,1},{0,2},{1,3},{6,4},{7,5},{4,6},{5,7},{10,8},{11,9},{8,1... | collective-permute-start | bytes 221192 | tf_op jit(solution)/shard_map/ppermute | solution.py:73
  102.7 11.7 %collective-permute-start.10 = (bf16[72,512]{1,0:T(8,128)(2,1)S(1)}, bf16[72,512]{1,0:T(8,128)(2,1)S(1)}, u32[]{:S(2)}, u32[]{:S(2)}) collective-permute-start(bf16[72,512]{1,0:T(8,128)(2,1)S(1)} %pad_maximum_fusion.34), channel_id=1, source_target_pairs={{1,0},{2,1},{3,2},{0,3},{5,4},{6,5},{7,6},{4,7},{9,8},{10,9},{11,1... | collective-permute-start | bytes 221192 | tf_op jit(solution)/shard_map/ppermute | solution.py:73
  164.9 114.9 %all-gather.8.cloned.1.call-start = ((), (), s32[]{:S(2)}) async-start(), calls=%async_computation.10 | async-start | bytes 2580480 | tf_op jit(solution)/shard_map/all_gather | solution.py:640
  166.2 113.6 %collective-permute-start.24 = (bf16[1152,1792]{1,0:T(8,128)(2,1)}, bf16[1152,1792]{1,0:T(8,128)(2,1)}, u32[]{:S(2)}, u32[]{:S(2)}) collective-permute-start(bf16[1152,1792]{1,0:T(8,128)(2,1)} %all-gather.4.cloned.1.call-done.other_ref.own_ref), channel_id=1, source_target_pairs={{4,0},{0,4},{12,8},{8,12},{20,16},{16,20},{28,24},{24,28},{5,1},{1... | collective-permute-start | bytes 12386312 | tf_op jit(solution)/shard_map/ppermute | solution.py:77
  228.1 10.2 %collective-permute-start.18 = (bf16[128,1152]{1,0:T(8,128)(2,1)}, bf16[128,1152]{1,0:T(8,128)(2,1)}, u32[]{:S(2)}, u32[]{:S(2)}) collective-permute-start(bf16[128,1152]{1,0:T(8,128)(2,1)} %get-tuple-element.141), channel_id=1, source_target_pairs={{8,0},{12,4},{0,8},{4,12},{24,16},{28,20},{16,24},{20,28},{9,1},{1... | collective-permute-start | bytes 884744 | tf_op jit(solution)/shard_map/ppermute | solution.py:77
  229.5 13.9 %collective-permute-start.22 = (bf16[128,1152]{1,0:T(8,128)(2,1)}, bf16[128,1152]{1,0:T(8,128)(2,1)}, u32[]{:S(2)}, u32[]{:S(2)}) collective-permute-start(bf16[128,1152]{1,0:T(8,128)(2,1)} %get-tuple-element.140), channel_id=1, source_target_pairs={{8,0},{12,4},{0,8},{4,12},{24,16},{28,20},{16,24},{20,28},{9,1},{1... | collective-permute-start | bytes 884744 | tf_op jit(solution)/shard_map/ppermute | solution.py:77
  232.0 14.1 %collective-permute-start.20 = (bf16[128,1152]{1,0:T(8,128)(2,1)}, bf16[128,1152]{1,0:T(8,128)(2,1)}, u32[]{:S(2)}, u32[]{:S(2)}) collective-permute-start(bf16[128,1152]{1,0:T(8,128)(2,1)} %get-tuple-element.136), channel_id=1, source_target_pairs={{16,0},{20,4},{24,8},{28,12},{0,16},{4,20},{8,24},{12,28},{17,1},{... | collective-permute-start | bytes 884744 | tf_op jit(solution)/shard_map/ppermute | solution.py:77
  233.4 15.3 %collective-permute-start.23 = (bf16[128,1152]{1,0:T(8,128)(2,1)}, bf16[128,1152]{1,0:T(8,128)(2,1)}, u32[]{:S(2)}, u32[]{:S(2)}) collective-permute-start(bf16[128,1152]{1,0:T(8,128)(2,1)} %get-tuple-element.139), channel_id=1, source_target_pairs={{16,0},{20,4},{24,8},{28,12},{0,16},{4,20},{8,24},{12,28},{17,1},{... | collective-permute-start | bytes 884744 | tf_op jit(solution)/shard_map/ppermute | solution.py:77
  234.0 331.0 %reduce-scatter.6.cloned.1.call-start = ((), (), s32[]{:S(2)}) async-start(), calls=%async_computation.11 | async-start | bytes 2580480 | tf_op jit(solution)/shard_map/reduce_scatter | solution.py:692
  239.4 21.7 %collective-permute-start.19 = (bf16[256,1152]{1,0:T(8,128)(2,1)S(1)}, bf16[256,1152]{1,0:T(8,128)(2,1)S(1)}, u32[]{:S(2)}, u32[]{:S(2)}) collective-permute-start(bf16[256,1152]{1,0:T(8,128)(2,1)S(1)} %pad_maximum_fusion.16), channel_id=1, source_target_pairs={{16,0},{20,4},{24,8},{28,12},{0,16},{4,20},{8,24},{12,28},{17,1},{... | collective-permute-start | bytes 1769480 | tf_op jit(solution)/shard_map/ppermute | solution.py:77
  244.6 27.4 %collective-permute-start.25 = (bf16[256,1152]{1,0:T(8,128)(2,1)S(1)}, bf16[256,1152]{1,0:T(8,128)(2,1)S(1)}, u32[]{:S(2)}, u32[]{:S(2)}) collective-permute-start(bf16[256,1152]{1,0:T(8,128)(2,1)S(1)} %pad_maximum_fusion.18.other_ref), channel_id=1, source_target_pairs={{16,0},{20,4},{24,8},{28,12},{0,16},{4,20},{8,24},{12,28},{17,1},{... | collective-permute-start | bytes 1769480 | tf_op jit(solution)/shard_map/ppermute | solution.py:77
  247.2 27.4 %collective-permute-start.21 = (bf16[256,1152]{1,0:T(8,128)(2,1)S(1)}, bf16[256,1152]{1,0:T(8,128)(2,1)S(1)}, u32[]{:S(2)}, u32[]{:S(2)}) collective-permute-start(bf16[256,1152]{1,0:T(8,128)(2,1)S(1)} %pad_maximum_fusion.17), channel_id=1, source_target_pairs={{8,0},{12,4},{0,8},{4,12},{24,16},{28,20},{16,24},{20,28},{9,1},{1... | collective-permute-start | bytes 1769480 | tf_op jit(solution)/shard_map/ppermute | solution.py:77
  250.7 27.1 %collective-permute-start.26 = (bf16[256,1152]{1,0:T(8,128)(2,1)}, bf16[256,1152]{1,0:T(8,128)(2,1)}, u32[]{:S(2)}, u32[]{:S(2)}) collective-permute-start(bf16[256,1152]{1,0:T(8,128)(2,1)} %pad_maximum_fusion.19.other_ref), channel_id=1, source_target_pairs={{8,0},{12,4},{0,8},{4,12},{24,16},{28,20},{16,24},{20,28},{9,1},{1... | collective-permute-start | bytes 1769480 | tf_op jit(solution)/shard_map/ppermute | solution.py:77
  296.1 16.2 %collective-permute-start.27 = (bf16[1152,896]{1,0:T(8,128)(2,1)}, bf16[1152,896]{1,0:T(8,128)(2,1)S(1)}, u32[]{:S(2)}, u32[]{:S(2)}) collective-permute-start(bf16[1152,896]{1,0:T(8,128)(2,1)} %shard_map.234.own_ref.own_down_ref), channel_id=1, source_target_pairs={{4,0},{0,4},{12,8},{8,12},{20,16},{16,20},{28,24},{24,28},{5,1},{1... | collective-permute-start | bytes 6193160 | tf_op jit(solution)/shard_map/ppermute | solution.py:77
  324.6 15.9 %collective-permute-start.28 = (bf16[256,1152]{1,0:T(8,128)(2,1)S(1)}, bf16[256,1152]{1,0:T(8,128)(2,1)}, u32[]{:S(2)}, u32[]{:S(2)}) collective-permute-start(bf16[256,1152]{1,0:T(8,128)(2,1)S(1)} %get-tuple-element.126.other_ref), channel_id=1, source_target_pairs={{16,0},{20,4},{24,8},{28,12},{0,16},{4,20},{8,24},{12,28},{17,1},{... | collective-permute-start | bytes 1769480 | tf_op jit(solution)/shard_map/ppermute | solution.py:77
  326.1 15.5 %collective-permute-start.30 = (bf16[256,1152]{1,0:T(8,128)(2,1)S(1)}, bf16[256,1152]{1,0:T(8,128)(2,1)}, u32[]{:S(2)}, u32[]{:S(2)}) collective-permute-start(bf16[256,1152]{1,0:T(8,128)(2,1)S(1)} %get-tuple-element.125.other_ref), channel_id=1, source_target_pairs={{8,0},{12,4},{0,8},{4,12},{24,16},{28,20},{16,24},{20,28},{9,1},{1... | collective-permute-start | bytes 1769480 | tf_op jit(solution)/shard_map/ppermute | solution.py:77
  343.5 10.0 %collective-permute-start.31 = (bf16[128,1152]{1,0:T(8,128)(2,1)S(1)}, bf16[128,1152]{1,0:T(8,128)(2,1)S(1)}, u32[]{:S(2)}, u32[]{:S(2)}) collective-permute-start(bf16[128,1152]{1,0:T(8,128)(2,1)S(1)} %slice.626), channel_id=1, source_target_pairs={{16,0},{20,4},{24,8},{28,12},{0,16},{4,20},{8,24},{12,28},{17,1},{... | collective-permute-start | bytes 884744 | tf_op jit(solution)/shard_map/ppermute | solution.py:77
  344.2 26.3 %collective-permute-start.32 = (bf16[256,1152]{1,0:T(8,128)(2,1)S(1)}, bf16[256,1152]{1,0:T(8,128)(2,1)S(1)}, u32[]{:S(2)}, u32[]{:S(2)}) collective-permute-start(bf16[256,1152]{1,0:T(8,128)(2,1)S(1)} %get-tuple-element.121), channel_id=1, source_target_pairs={{16,0},{20,4},{24,8},{28,12},{0,16},{4,20},{8,24},{12,28},{17,1},{... | collective-permute-start | bytes 1769480 | tf_op jit(solution)/shard_map/ppermute | solution.py:77
  345.8 24.7 %collective-permute-start.35 = (bf16[256,1152]{1,0:T(8,128)(2,1)S(1)}, bf16[256,1152]{1,0:T(8,128)(2,1)S(1)}, u32[]{:S(2)}, u32[]{:S(2)}) collective-permute-start(bf16[256,1152]{1,0:T(8,128)(2,1)S(1)} %get-tuple-element.122), channel_id=1, source_target_pairs={{8,0},{12,4},{0,8},{4,12},{24,16},{28,20},{16,24},{20,28},{9,1},{1... | collective-permute-start | bytes 1769480 | tf_op jit(solution)/shard_map/ppermute | solution.py:77
  347.3 18.9 %collective-permute-start.29 = (bf16[128,1152]{1,0:T(8,128)(2,1)S(1)}, bf16[128,1152]{1,0:T(8,128)(2,1)S(1)}, u32[]{:S(2)}, u32[]{:S(2)}) collective-permute-start(bf16[128,1152]{1,0:T(8,128)(2,1)S(1)} %slice.627), channel_id=1, source_target_pairs={{8,0},{12,4},{0,8},{4,12},{24,16},{28,20},{16,24},{20,28},{9,1},{1... | collective-permute-start | bytes 884744 | tf_op jit(solution)/shard_map/ppermute | solution.py:77
  369.9 10.4 %collective-permute-start.38 = (bf16[128,1152]{1,0:T(8,128)(2,1)}, bf16[128,1152]{1,0:T(8,128)(2,1)}, u32[]{:S(2)}, u32[]{:S(2)}) collective-permute-start(bf16[128,1152]{1,0:T(8,128)(2,1)} %get-tuple-element.154), channel_id=1, source_target_pairs={{16,0},{20,4},{24,8},{28,12},{0,16},{4,20},{8,24},{12,28},{17,1},{... | collective-permute-start | bytes 884744 | tf_op jit(solution)/shard_map/ppermute | solution.py:77
  376.8 25.5 %collective-permute-start.37 = (bf16[256,1152]{1,0:T(8,128)(2,1)}, bf16[256,1152]{1,0:T(8,128)(2,1)}, u32[]{:S(2)}, u32[]{:S(2)}) collective-permute-start(bf16[256,1152]{1,0:T(8,128)(2,1)} %pad_maximum_fusion.20.other_ref), channel_id=1, source_target_pairs={{16,0},{20,4},{24,8},{28,12},{0,16},{4,20},{8,24},{12,28},{17,1},{... | collective-permute-start | bytes 1769480 | tf_op jit(solution)/shard_map/ppermute | solution.py:77
  377.5 18.4 %collective-permute-start.36 = (bf16[128,1152]{1,0:T(8,128)(2,1)}, bf16[128,1152]{1,0:T(8,128)(2,1)}, u32[]{:S(2)}, u32[]{:S(2)}) collective-permute-start(bf16[128,1152]{1,0:T(8,128)(2,1)} %shard_map.240), channel_id=1, source_target_pairs={{16,0},{20,4},{24,8},{28,12},{0,16},{4,20},{8,24},{12,28},{17,1},{... | collective-permute-start | bytes 884744 | tf_op jit(solution)/shard_map/ppermute | solution.py:77
  378.9 18.2 %collective-permute-start.34 = (bf16[128,1152]{1,0:T(8,128)(2,1)}, bf16[128,1152]{1,0:T(8,128)(2,1)S(1)}, u32[]{:S(2)}, u32[]{:S(2)}) collective-permute-start(bf16[128,1152]{1,0:T(8,128)(2,1)} %shard_map.239), channel_id=1, source_target_pairs={{8,0},{12,4},{0,8},{4,12},{24,16},{28,20},{16,24},{20,28},{9,1},{1... | collective-permute-start | bytes 884744 | tf_op jit(solution)/shard_map/ppermute | solution.py:77
  381.4 27.6 %collective-permute-start.39 = (bf16[256,1152]{1,0:T(8,128)(2,1)S(1)}, bf16[256,1152]{1,0:T(8,128)(2,1)S(1)}, u32[]{:S(2)}, u32[]{:S(2)}) collective-permute-start(bf16[256,1152]{1,0:T(8,128)(2,1)S(1)} %pad_maximum_fusion.21), channel_id=1, source_target_pairs={{8,0},{12,4},{0,8},{4,12},{24,16},{28,20},{16,24},{20,28},{9,1},{1... | collective-permute-start | bytes 1769480 | tf_op jit(solution)/shard_map/ppermute | solution.py:77
  401.1 9.5 %collective-permute-start.40 = (bf16[128,1152]{1,0:T(8,128)(2,1)S(1)}, bf16[128,1152]{1,0:T(8,128)(2,1)}, u32[]{:S(2)}, u32[]{:S(2)}) collective-permute-start(bf16[128,1152]{1,0:T(8,128)(2,1)S(1)} %get-tuple-element.153), channel_id=1, source_target_pairs={{8,0},{12,4},{0,8},{4,12},{24,16},{28,20},{16,24},{20,28},{9,1},{1... | collective-permute-start | bytes 884744 | tf_op jit(solution)/shard_map/ppermute | solution.py:77
  412.4 31.4 %collective-permute-start.43 = (bf16[256,1152]{1,0:T(8,128)(2,1)}, bf16[256,1152]{1,0:T(8,128)(2,1)S(1)}, u32[]{:S(2)}, u32[]{:S(2)}) collective-permute-start(bf16[256,1152]{1,0:T(8,128)(2,1)} %shard_map.243.other_ref), channel_id=1, source_target_pairs={{8,0},{12,4},{0,8},{4,12},{24,16},{28,20},{16,24},{20,28},{9,1},{1... | collective-permute-start | bytes 1769480 | tf_op jit(solution)/shard_map/ppermute | solution.py:77
  413.7 30.2 %collective-permute-start.42 = (bf16[256,1152]{1,0:T(8,128)(2,1)}, bf16[256,1152]{1,0:T(8,128)(2,1)S(1)}, u32[]{:S(2)}, u32[]{:S(2)}) collective-permute-start(bf16[256,1152]{1,0:T(8,128)(2,1)} %shard_map.241.other_ref), channel_id=1, source_target_pairs={{16,0},{20,4},{24,8},{28,12},{0,16},{4,20},{8,24},{12,28},{17,1},{... | collective-permute-start | bytes 1769480 | tf_op jit(solution)/shard_map/ppermute | solution.py:77
  467.5 36.8 %collective-permute-start.52 = (bf16[1152,896]{1,0:T(8,128)(2,1)}, bf16[1152,896]{1,0:T(8,128)(2,1)}, u32[]{:S(2)}, u32[]{:S(2)}) collective-permute-start(bf16[1152,896]{1,0:T(8,128)(2,1)} %get-tuple-element.65), channel_id=1, source_target_pairs={{4,0},{0,4},{12,8},{8,12},{20,16},{16,20},{28,24},{24,28},{5,1},{1... | collective-permute-start | bytes 6193160 | tf_op jit(solution)/shard_map/ppermute | solution.py:77
  467.5 33.6 %collective-permute-start.46 = (bf16[256,1152]{1,0:T(8,128)(2,1)S(1)}, bf16[256,1152]{1,0:T(8,128)(2,1)S(1)}, u32[]{:S(2)}, u32[]{:S(2)}) collective-permute-start(bf16[256,1152]{1,0:T(8,128)(2,1)S(1)} %copy-done.41), channel_id=1, source_target_pairs={{16,0},{20,4},{24,8},{28,12},{0,16},{4,20},{8,24},{12,28},{17,1},{... | collective-permute-start | bytes 1769480 | tf_op jit(solution)/shard_map/ppermute | solution.py:77
  469.0 32.2 %collective-permute-start.48 = (bf16[256,1152]{1,0:T(8,128)(2,1)S(1)}, bf16[256,1152]{1,0:T(8,128)(2,1)S(1)}, u32[]{:S(2)}, u32[]{:S(2)}) collective-permute-start(bf16[256,1152]{1,0:T(8,128)(2,1)S(1)} %copy-done.40), channel_id=1, source_target_pairs={{8,0},{12,4},{0,8},{4,12},{24,16},{28,20},{16,24},{20,28},{9,1},{1... | collective-permute-start | bytes 1769480 | tf_op jit(solution)/shard_map/ppermute | solution.py:77
  499.2 24.6 %collective-permute-start.45 = (bf16[256,1152]{1,0:T(8,128)(2,1)}, bf16[256,1152]{1,0:T(8,128)(2,1)}, u32[]{:S(2)}, u32[]{:S(2)}) collective-permute-start(bf16[256,1152]{1,0:T(8,128)(2,1)} %get-tuple-element.115), channel_id=1, source_target_pairs={{8,0},{12,4},{0,8},{4,12},{24,16},{28,20},{16,24},{20,28},{9,1},{1... | collective-permute-start | bytes 1769480 | tf_op jit(solution)/shard_map/ppermute | solution.py:77
  500.5 23.3 %collective-permute-start.44 = (bf16[256,1152]{1,0:T(8,128)(2,1)}, bf16[256,1152]{1,0:T(8,128)(2,1)}, u32[]{:S(2)}, u32[]{:S(2)}) collective-permute-start(bf16[256,1152]{1,0:T(8,128)(2,1)} %get-tuple-element.116), channel_id=1, source_target_pairs={{16,0},{20,4},{24,8},{28,12},{0,16},{4,20},{8,24},{12,28},{17,1},{... | collective-permute-start | bytes 1769480 | tf_op jit(solution)/shard_map/ppermute | solution.py:77
  502.2 19.7 %collective-permute-start.49 = (bf16[128,1152]{1,0:T(8,128)(2,1)}, bf16[128,1152]{1,0:T(8,128)(2,1)}, u32[]{:S(2)}, u32[]{:S(2)}) collective-permute-start(bf16[128,1152]{1,0:T(8,128)(2,1)} %slice.620.other_ref), channel_id=1, source_target_pairs={{16,0},{20,4},{24,8},{28,12},{0,16},{4,20},{8,24},{12,28},{17,1},{... | collective-permute-start | bytes 884744 | tf_op jit(solution)/shard_map/ppermute | solution.py:77
  508.4 112.7 %reduce-scatter.8.cloned.1.call-start = ((), (), s32[]{:S(2)}) async-start(), calls=%async_computation.12 | async-start | bytes 2580480 | tf_op jit(solution)/shard_map/reduce_scatter | solution.py:692
  510.7 34.1 %collective-permute-start.47 = (bf16[128,1152]{1,0:T(8,128)(2,1)}, bf16[128,1152]{1,0:T(8,128)(2,1)}, u32[]{:S(2)}, u32[]{:S(2)}) collective-permute-start(bf16[128,1152]{1,0:T(8,128)(2,1)} %slice.621.other_ref), channel_id=1, source_target_pairs={{8,0},{12,4},{0,8},{4,12},{24,16},{28,20},{16,24},{20,28},{9,1},{1... | collective-permute-start | bytes 884744 | tf_op jit(solution)/shard_map/ppermute | solution.py:77
  544.8 15.2 %collective-permute-start.53 = (bf16[1152,896]{1,0:T(8,128)(2,1)}, bf16[1152,896]{1,0:T(8,128)(2,1)}, u32[]{:S(2)}, u32[]{:S(2)}) collective-permute-start(bf16[1152,896]{1,0:T(8,128)(2,1)} %get-tuple-element.69), channel_id=1, source_target_pairs={{4,0},{0,4},{12,8},{8,12},{20,16},{16,20},{28,24},{24,28},{5,1},{1... | collective-permute-start | bytes 6193160 | tf_op jit(solution)/shard_map/ppermute | solution.py:77
  546.6 9.7 %collective-permute-start.51 = (bf16[128,1152]{1,0:T(8,128)(2,1)}, bf16[128,1152]{1,0:T(8,128)(2,1)}, u32[]{:S(2)}, u32[]{:S(2)}) collective-permute-start(bf16[128,1152]{1,0:T(8,128)(2,1)} %slice.622.other_ref), channel_id=1, source_target_pairs={{16,0},{20,4},{24,8},{28,12},{0,16},{4,20},{8,24},{12,28},{17,1},{... | collective-permute-start | bytes 884744 | tf_op jit(solution)/shard_map/ppermute | solution.py:77
  547.2 10.1 %collective-permute-start.50 = (bf16[128,1152]{1,0:T(8,128)(2,1)}, bf16[128,1152]{1,0:T(8,128)(2,1)}, u32[]{:S(2)}, u32[]{:S(2)}) collective-permute-start(bf16[128,1152]{1,0:T(8,128)(2,1)} %slice.623.other_ref), channel_id=1, source_target_pairs={{8,0},{12,4},{0,8},{4,12},{24,16},{28,20},{16,24},{20,28},{9,1},{1... | collective-permute-start | bytes 884744 | tf_op jit(solution)/shard_map/ppermute | solution.py:77
  565.0 102.5 %reduce-scatter.10.cloned.1.call-start = ((), (), s32[]{:S(2)}) async-start(), calls=%async_computation.13 | async-start | bytes 2621440 | tf_op jit(solution)/shard_map/reduce_scatter | solution.py:726
  615.6 27.1 %collective-permute-start.58 = (bf16[1152,512]{1,0:T(8,128)(2,1)}, bf16[1152,512]{1,0:T(8,128)(2,1)}, u32[]{:S(2)}, u32[]{:S(2)}) collective-permute-start(bf16[1152,512]{1,0:T(8,128)(2,1)} %constant_dynamic-slice_fusion.5), channel_id=1, source_target_pairs={{4,0},{0,4},{12,8},{8,12},{20,16},{16,20},{28,24},{24,28},{5,1},{1... | collective-permute-start | bytes 3538952 | tf_op jit(solution)/shard_map/ppermute | solution.py:77
  621.1 89.7 %reduce-scatter.14.cloned.1.call-start = ((), (), s32[]{:S(2)}) async-start(), calls=%async_computation.15 | async-start | bytes 2580480 | tf_op jit(solution)/shard_map/reduce_scatter | solution.py:692
  622.7 22.4 %collective-permute-start.55 = (bf16[1152,512]{1,0:T(8,128)(2,1)S(1)}, bf16[1152,512]{1,0:T(8,128)(2,1)}, u32[]{:S(2)}, u32[]{:S(2)}) collective-permute-start(bf16[1152,512]{1,0:T(8,128)(2,1)S(1)} %constant_dynamic-slice_fusion.8), channel_id=1, source_target_pairs={{4,0},{0,4},{12,8},{8,12},{20,16},{16,20},{28,24},{24,28},{5,1},{1... | collective-permute-start | bytes 3538952 | tf_op jit(solution)/shard_map/ppermute | solution.py:77
  641.2 24.4 %collective-permute-start.54 = (bf16[1152,896]{1,0:T(8,128)(2,1)}, bf16[1152,896]{1,0:T(8,128)(2,1)S(1)}, u32[]{:S(2)}, u32[]{:S(2)}) collective-permute-start(bf16[1152,896]{1,0:T(8,128)(2,1)} %get-tuple-element.71), channel_id=1, source_target_pairs={{4,0},{0,4},{12,8},{8,12},{20,16},{16,20},{28,24},{24,28},{5,1},{1... | collective-permute-start | bytes 6193160 | tf_op jit(solution)/shard_map/ppermute | solution.py:77
  644.6 15.5 %collective-permute-start.59 = (bf16[1152,256]{1,0:T(8,128)(2,1)S(1)}, bf16[1152,256]{1,0:T(8,128)(2,1)S(1)}, u32[]{:S(2)}, u32[]{:S(2)}) collective-permute-start(bf16[1152,256]{1,0:T(8,128)(2,1)S(1)} %constant_dynamic-slice_fusion.4), channel_id=1, source_target_pairs={{16,0},{20,4},{24,8},{28,12},{0,16},{4,20},{8,24},{12,28},{17,1},{... | collective-permute-start | bytes 1769480 | tf_op jit(solution)/shard_map/ppermute | solution.py:77
  646.9 15.2 %collective-permute-start.56 = (bf16[1152,256]{1,0:T(8,128)(2,1)S(1)}, bf16[1152,256]{1,0:T(8,128)(2,1)S(1)}, u32[]{:S(2)}, u32[]{:S(2)}) collective-permute-start(bf16[1152,256]{1,0:T(8,128)(2,1)S(1)} %constant_dynamic-slice_fusion.7), channel_id=1, source_target_pairs={{8,0},{12,4},{0,8},{4,12},{24,16},{28,20},{16,24},{20,28},{9,1},{1... | collective-permute-start | bytes 1769480 | tf_op jit(solution)/shard_map/ppermute | solution.py:77
  669.7 77.6 %reduce-scatter.12.cloned.1.call-start = ((), (), s32[]{:S(2)}) async-start(), calls=%async_computation.14 | async-start | bytes 737280 | tf_op jit(solution)/shard_map/reduce_scatter | solution.py:692
  690.3 15.9 %collective-permute-start.61 = (bf16[1152,256]{1,0:T(8,128)(2,1)S(1)}, bf16[1152,256]{1,0:T(8,128)(2,1)S(1)}, u32[]{:S(2)}, u32[]{:S(2)}) collective-permute-start(bf16[1152,256]{1,0:T(8,128)(2,1)S(1)} %copy-done.58), channel_id=1, source_target_pairs={{4,0},{0,4},{12,8},{8,12},{20,16},{16,20},{28,24},{24,28},{5,1},{1... | collective-permute-start | bytes 1769480 | tf_op jit(solution)/shard_map/ppermute | solution.py:77
  702.4 17.0 %collective-permute-start.72 = (f32[40,128]{1,0:T(8,128)}, f32[40,128]{1,0:T(8,128)}, u32[]{:S(2)}, u32[]{:S(2)}) collective-permute-start(f32[40,128]{1,0:T(8,128)} %add.602), channel_id=1, source_target_pairs={{3,0},{0,1},{1,2},{2,3},{7,4},{4,5},{5,6},{6,7},{11,8},{8,9},{9,10... | collective-permute-start | bytes 61448 | tf_op jit(solution)/shard_map/ppermute | solution.py:73
  702.4 17.0 %collective-permute-start.70 = (f32[40,128]{1,0:T(8,128)}, f32[40,128]{1,0:T(8,128)}, u32[]{:S(2)}, u32[]{:S(2)}) collective-permute-start(f32[40,128]{1,0:T(8,128)} %add.602), channel_id=1, source_target_pairs={{1,0},{2,1},{3,2},{0,3},{5,4},{6,5},{7,6},{4,7},{9,8},{10,9},{11,1... | collective-permute-start | bytes 61448 | tf_op jit(solution)/shard_map/ppermute | solution.py:73
  706.2 13.2 %collective-permute-start.71 = (f32[40,128]{1,0:T(8,128)}, f32[40,128]{1,0:T(8,128)}, u32[]{:S(2)}, u32[]{:S(2)}) collective-permute-start(f32[40,128]{1,0:T(8,128)} %add.602), channel_id=1, source_target_pairs={{2,0},{3,1},{0,2},{1,3},{6,4},{7,5},{4,6},{5,7},{10,8},{11,9},{8,1... | collective-permute-start | bytes 61448 | tf_op jit(solution)/shard_map/ppermute | solution.py:73
  707.1 10.1 %collective-permute-start.62 = (bf16[1152,128]{1,0:T(8,128)(2,1)}, bf16[1152,128]{1,0:T(8,128)(2,1)S(1)}, u32[]{:S(2)}, u32[]{:S(2)}) collective-permute-start(bf16[1152,128]{1,0:T(8,128)(2,1)} %constant_dynamic-slice_fusion.2), channel_id=1, source_target_pairs={{16,0},{20,4},{24,8},{28,12},{0,16},{4,20},{8,24},{12,28},{17,1},{... | collective-permute-start | bytes 884744 | tf_op jit(solution)/shard_map/ppermute | solution.py:77
  713.4 32.7 %all-to-all-start.1 = ((bf16[8,36,2688]{2,1,0:T(8,128)(2,1)}), bf16[8,36,2688]{2,1,0:T(8,128)(2,1)S(1)}, u32[]{:S(2)}, u32[]{:S(2)}) async-start(bf16[8,36,2688]{2,1,0:T(8,128)(2,1)} %reshape.526), calls=%async_computation.6 | async-start | bytes 3440640 | tf_op jit(solution)/shard_map/all_to_all | solution.py:695
  717.4 27.9 %collective-permute-start.63 = (bf16[1152,128]{1,0:T(8,128)(2,1)S(1)}, bf16[1152,128]{1,0:T(8,128)(2,1)S(1)}, u32[]{:S(2)}, u32[]{:S(2)}) collective-permute-start(bf16[1152,128]{1,0:T(8,128)(2,1)S(1)} %add_convert_fusion.9), channel_id=1, source_target_pairs={{8,0},{12,4},{0,8},{4,12},{24,16},{28,20},{16,24},{20,28},{9,1},{1... | collective-permute-start | bytes 884744 | tf_op jit(solution)/shard_map/ppermute | solution.py:77
  760.0 10.1 %all-to-all-start.2 = ((bf16[8,36,384]{2,1,0:T(8,128)(2,1)}), bf16[8,36,384]{2,1,0:T(8,128)(2,1)S(1)}, u32[]{:S(2)}, u32[]{:S(2)}) async-start(bf16[8,36,384]{2,1,0:T(8,128)(2,1)} %reshape.528), calls=%async_computation.7 | async-start | bytes 491520 | tf_op jit(solution)/shard_map/all_to_all | solution.py:695
  (165 other events, 1210.4 us)
Sparse Core Ops, SparseCore 0:
  76.5 88.2 all-gather.3
  167.0 44.3 all-gather.5
  234.1 43.9 all-gather.7
  508.5 40.5 reduce-scatter.5
  565.1 40.6 reduce-scatter.7
  621.3 40.9 reduce-scatter.9
  669.8 40.9 reduce-scatter.13
  713.2 21.3 reduce-scatter.11

commit v4 on v3

--- a/solution.py
+++ b/solution.py
@@ -742,19 +742,20 @@
     raw_key, grad_head_key = pull_key(key_value_grad[:, :HD])
     key_value_low = jnp.concatenate([raw_key, key_value_grad[:, HD:]], axis=1).astype(BF)
     late_bits, same_bits = bits_out[:2], bits_out[2:]
-    late_share, sent = scatter_cols_sent(dot(normed_low, key_value_low, TN), late_bits)
+    late_share, sent = scatter_cols_sent(dot(normed_low, key_value_low, TN), late_bits[:1])
     in_part = dot(query_grad_low, w_qkv[:, :Q_COLS], NT)
     in_part = in_part + dot(tie(key_value_low, sent), w_qkv[:, Q_COLS:], NT)
     input_part, grad_zero = pull_in(in_part)
     grad_input_low = (residual_grad + input_part).astype(BF)
 
-    for bit in same_bits:
-        late_share = (late_share.astype(F32) + flip(late_share, bit).astype(F32)).astype(BF)
     back = to_rows(jnp.concatenate([summed_gate, summed_up, summed_down], axis=1))
     early = shard_sum(jnp.concatenate([query_share, out_share], axis=1))
-    late_share = tie(tie(late_share, back), early)
     slices = scatter_parts(late_share.reshape(z_count, -1, late_share.shape[1]), "ctx")
-    back_attn = jnp.concatenate([early, scatter_direct(slices, "ctx").astype(BF)], axis=1)
+    late_rows = tie(tie(scatter_direct(slices, "ctx").astype(BF), back), early)
+    late_rows = scatter_cols(late_rows, late_bits[1:])
+    for bit in same_bits:
+        late_rows = (late_rows.astype(F32) + flip(late_rows, bit).astype(F32)).astype(BF)
+    back_attn = jnp.concatenate([early, late_rows], axis=1)
     back_attn = to_rows(back_attn)
     share = Q_COLS // dp_count
     sum_query = columns_back(back_attn[:, :, :share], bits_query)

time: 800 us -> 797 us (level)
    ppermute x61, waiting for transfers between devices: 143 us -> 122 us  [flip(): lax.ppermute(values, 'dp', [(i ^ bit, i) for i in range(lax.axis_size('dp...]
    reduce_scatter x4, waiting for transfers between devices: 2.38 us -> 12.9 us  [shard_sum(): return lax.psum_scatter(grad, 'ctx', scatter_dimension=0, tiled=True)]
    unnamed x319 -> x317, local copies, waits for them, and re-layouts: 43.9 us -> 43.9 us
  transfers between devices with their start and end apart: 84 -> 84, of which waited for: 37 -> 38; matrix products, arithmetic and copies ran while one was open for 23% -> 23% of each run, Pallas kernels for 18% -> 18%
where the time goes in v4:
time: 797 us; the launch traced here: 788 us
  waiting for transfers between devices  237 us (30%)
  Pallas kernels  189 us (24%)
  other arithmetic  116 us (15%)
  starting transfers between devices  97.2 us (12%)
  local copies, waits for them, and re-layouts  93.8 us (12%)
  matrix products  37.9 us (5%)
  between operations  17.8 us (2%)
    ppermute x61, waiting for transfers between devices, flip(): lax.ppermute(values, 'dp', [(i ^ bit, i) for i in range(lax.axis_size('dp...  122 us
    ppermute x61, starting transfers between devices, flip(): lax.ppermute(values, 'dp', [(i ^ bit, i) for i in range(lax.axis_size('dp...  56.9 us
    pallas_call x2, Pallas kernels, mlp_backward(): pl.pallas_call(mlp_back_kernel, grid=(rows // tile,), in_specs=[spec(widt...  54.1 us
    pallas_call x3, Pallas kernels, products(): pl.pallas_call(kernel, grid=(2,), in_specs=[left, left, right, right], ou...  53.7 us
    all_gather x1, waiting for transfers between devices, body(): key_value = lax.all_gather(key_value, 'ctx', axis=0, tiled=True)  45.3 us
    unnamed x317, local copies, waits for them, and re-layouts  43.9 us
    pallas_call x2, Pallas kernels, mlp_up(): pl.pallas_call(mlp_up_kernel, grid=(rows // tile,), in_specs=[spec(width)...  32.5 us
    all_gather x1, waiting for transfers between devices, body(): gate_up_own = lax.all_gather(gate_up_block, 'ctx', axis=0, tiled=True)  27.9 us
  transfers between devices with their start and end apart: 84, of which 38 were waited for; matrix products, arithmetic and copies ran while one was open for 23% of the time, Pallas kernels for 18%

profile of v4, /device:TPU:0, one launch (start us, length us, event | category | flops | bytes accessed | tf_op | source)
XLA Modules:
  0.0 788.4 jit_solution(6233905254321200941)
XLA Ops:
  11.7 5.3 all-to-all-start
  24.7 3.1 collective-permute-start.2
  31.7 6.0 collective-permute-done.2
  53.5 3.0 collective-permute-done.6
  56.6 7.5 collective-permute-done.5
  64.5 3.6 collective-permute-done.7
  71.3 3.3 multiply_reduce_fusion.8
  76.7 3.9 broadcast_select_fusion
  86.3 2.8 fusion.76
  96.7 6.1 collective-permute-start.11
  102.8 3.8 collective-permute-start.10
  107.3 4.8 collective-permute-done.11
  117.2 2.7 collective-permute-done.13
  124.5 3.0 collective-permute-done.16
  136.9 27.9 %all-gather.4.cloned.1.call-done.other_ref.own_ref = bf16[1152,1792]{1,0:T(8,128)(2,1)} async-done(((bf16[288,1792]{1,0:T(8,128)(2,1)}), bf16[1152,1792]{1,0:T(8,128)(2,1)}) %all-gather.4.cloned.1.call-update) | async-done | bytes 4128784 | tf_op jit(solution)/shard_map/all_gather | solution.py:601
  166.2 45.3 %all-gather.6.cloned.1.call-done.kv_ref.other_ref = bf16[2048,512]{1,0:T(8,128)(2,1)} async-done(((bf16[512,512]{1,0:T(8,128)(2,1)}), bf16[2048,512]{1,0:T(8,128)(2,1)}) %all-gather.6.cloned.1.call-update) | async-done | bytes 2097168 | tf_op jit(solution)/shard_map/all_gather | solution.py:639
  211.4 10.1 %shard_map.225 = (bf16[512,1024]{1,0:T(8,128)(2,1)}, f32[512,512]{1,0:T(8,128)}) custom-call(s32[2]{0:T(128)} %pad_add_fusion.2.info_ref, bf16[512,1024]{1,0:T(8,128)(2,1)} %bitcast.181, bf16[2048,512]{1,0:T(8,128)(2,1)} %all-gather.6.cloned.1.call-done.kv_ref.other_ref), custom_call_target="tpu_custom_call" | custom-call | tf_op jit(solution)/shard_map/pallas_call | solution.py:315
  221.5 3.1 multiply_reduce_fusion.7
  234.1 4.2 collective-permute-done.18
  241.0 2.5 collective-permute-done.22
  254.7 6.5 collective-permute-done.19
  261.2 10.8 %collective-permute-done.25 = bf16[256,1152]{1,0:T(8,128)(2,1)S(1)} collective-permute-done((bf16[256,1152]{1,0:T(8,128)(2,1)S(1)}, bf16[256,1152]{1,0:T(8,128)(2,1)S(1)}, u32[]{:S(2)}, u32[]{:S(2)}) %collective-permute-start.25) | collective-permute-done | bytes 589856 | tf_op jit(solution)/shard_map/ppermute | solution.py:77
  279.8 16.4 %shard_map.230 = (bf16[1024,3584]{1,0:T(8,128)(2,1)}, bf16[1024,1792]{1,0:T(8,128)(2,1)}) custom-call(bf16[1024,1152]{1,0:T(8,128)(2,1)} %shard_map.229.x_ref.refs_0_, bf16[1152,1792]{1,0:T(8,128)(2,1)} %all-gather.4.cloned.1.call-done.other_ref.own_ref, bf16[1152,1792]{1,0:T(8,128)(2,1)} %collective-permute-done.24.other_ref), custom_call_target="tpu_custom_call" | custom-call | tf_op jit(solution)/shard_map/pallas_call | solution.py:445
  296.1 16.2 %shard_map.232 = (bf16[1024,3584]{1,0:T(8,128)(2,1)}, bf16[1024,1792]{1,0:T(8,128)(2,1)}) custom-call(bf16[1024,1152]{1,0:T(8,128)(2,1)} %shard_map.231.x_ref.other_ref.refs_1_, bf16[1152,1792]{1,0:T(8,128)(2,1)} %all-gather.4.cloned.1.call-done.other_ref.own_ref, bf16[1152,1792]{1,0:T(8,128)(2,1)} %collective-permute-done.24.other_ref), custom_call_target="tpu_custom_call" | custom-call | tf_op jit(solution)/shard_map/pallas_call | solution.py:445
  313.6 9.5 %shard_map.235 = bf16[1024,1152]{1,0:T(8,128)(2,1)} custom-call(bf16[1024,1792]{1,0:T(8,128)(2,1)} %shard_map.233.hidden_ref.value_ref, bf16[1152,896]{1,0:T(8,128)(2,1)} %shard_map.234.own_ref.own_down_ref, bf16[1152,896]{1,0:T(8,128)(2,1)} %copy-done.11), custom_call_target="tpu_custom_call" | custom-call | tf_op jit(solution)/shard_map/pallas_call | solution.py:463
  329.6 10.3 %shard_map.238 = bf16[1024,1152]{1,0:T(8,128)(2,1)} custom-call(bf16[1024,1792]{1,0:T(8,128)(2,1)} %shard_map.237.hidden_ref.value_ref, bf16[1152,896]{1,0:T(8,128)(2,1)} %shard_map.234.own_ref.own_down_ref, bf16[1152,896]{1,0:T(8,128)(2,1)} %copy-done.11), custom_call_target="tpu_custom_call" | custom-call | tf_op jit(solution)/shard_map/pallas_call | solution.py:463
  348.0 5.6 collective-permute-done.31
  353.7 12.6 %collective-permute-done.29 = bf16[128,1152]{1,0:T(8,128)(2,1)S(1)} collective-permute-done((bf16[128,1152]{1,0:T(8,128)(2,1)S(1)}, bf16[128,1152]{1,0:T(8,128)(2,1)S(1)}, u32[]{:S(2)}, u32[]{:S(2)}) %collective-permute-start.29) | collective-permute-done | bytes 294944 | tf_op jit(solution)/shard_map/ppermute | solution.py:77
  372.7 2.6 collective-permute-done.33
  383.1 12.8 %collective-permute-done.36 = bf16[128,1152]{1,0:T(8,128)(2,1)} collective-permute-done((bf16[128,1152]{1,0:T(8,128)(2,1)}, bf16[128,1152]{1,0:T(8,128)(2,1)}, u32[]{:S(2)}, u32[]{:S(2)}) %collective-permute-start.36) | collective-permute-done | bytes 294944 | tf_op jit(solution)/shard_map/ppermute | solution.py:77
  403.6 3.6 collective-permute-done.41
  414.4 27.2 %shard_map.245 = (bf16[1024,1152]{1,0:T(8,128)(2,1)}, bf16[1024,3584]{1,0:T(8,128)(2,1)}) custom-call(bf16[1024,1152]{1,0:T(8,128)(2,1)} %shard_map.244.grad_ref.refs_0_, bf16[1024,3584]{1,0:T(8,128)(2,1)} %get-tuple-element.58.gate_up_ref, bf16[1152,1792]{1,0:T(8,128)(2,1)} %all-gather.4.cloned.1.call-done.other_ref.own_ref, ...), custom_call_target="tpu_custom_call" | custom-call | tf_op jit(solution)/shard_map/pallas_call | solution.py:511
  445.0 4.9 pad_maximum_fusion.2.refs_1_.grad_ref
  450.0 17.7 %shard_map.250 = (bf16[1152,896]{1,0:T(8,128)(2,1)}, bf16[1152,896]{1,0:T(8,128)(2,1)}) custom-call(bf16[1024,1152]{1,0:T(8,128)(2,1)} %shard_map.244.grad_ref.refs_0_, bf16[1024,1152]{1,0:T(8,128)(2,1)} %pad_maximum_fusion.2.refs_1_.grad_ref, bf16[1024,1792]{1,0:T(8,128)(2,1)} %shard_map.247.refs_2_, bf16[1024,1792]{1,0:T(8,128)(2,1)} %shard_map.249.refs_3_), custom_call_target="tpu_custom_call" | custom-call | tf_op jit(solution)/shard_map/pallas_call | solution.py:552
  469.9 27.0 %shard_map.252 = (bf16[1024,1152]{1,0:T(8,128)(2,1)}, bf16[1024,3584]{1,0:T(8,128)(2,1)}) custom-call(bf16[1024,1152]{1,0:T(8,128)(2,1)} %pad_maximum_fusion.2.refs_1_.grad_ref, bf16[1024,3584]{1,0:T(8,128)(2,1)} %shard_map.251.gate_up_ref, bf16[1152,1792]{1,0:T(8,128)(2,1)} %all-gather.4.cloned.1.call-done.other_ref.own_ref, ...), custom_call_target="tpu_custom_call" | custom-call | tf_op jit(solution)/shard_map/pallas_call | solution.py:511
  496.8 2.5 fusion.85
  504.4 4.0 add_convert_fusion.2
  511.6 10.5 %collective-permute-done.49 = bf16[128,1152]{1,0:T(8,128)(2,1)} collective-permute-done((bf16[128,1152]{1,0:T(8,128)(2,1)}, bf16[128,1152]{1,0:T(8,128)(2,1)}, u32[]{:S(2)}, u32[]{:S(2)}) %collective-permute-start.49) | collective-permute-done | bytes 294944 | tf_op jit(solution)/shard_map/ppermute | solution.py:77
  527.0 17.9 %shard_map.257 = (bf16[1152,896]{1,0:T(8,128)(2,1)}, bf16[1152,896]{1,0:T(8,128)(2,1)}) custom-call(bf16[1024,1152]{1,0:T(8,128)(2,1)} %shard_map.229.x_ref.refs_0_, bf16[1024,1152]{1,0:T(8,128)(2,1)} %shard_map.231.x_ref.other_ref.refs_1_, bf16[1024,3584]{1,0:T(8,128)(2,1)} %shard_map.254.refs_2_.value_ref, bf16[1024,3584]{1,0:T(8,128)(2,1)} %shard_map.256.refs_3_.value_ref), custom_call_target="tpu_custom_call" | custom-call | tf_op jit(solution)/shard_map/pallas_call | solution.py:552
  548.8 4.2 fusion.9.other_ref
  553.0 3.5 collective-permute-done.51
  561.6 3.5 add_convert_fusion.1
  566.9 3.0 multiply_reduce_fusion
  570.4 3.6 multiply_reduce_fusion.1
  576.5 2.5 convolution_convert_fusion.3.grad_ref
  579.0 19.1 %shard_map.264 = (f32[512,1024]{1,0:T(8,128)}, bf16[2048,512]{1,0:T(8,128)(2,1)}) custom-call(s32[2]{0:T(128)} %pad_add_fusion.2.info_ref, bf16[512,1024]{1,0:T(8,128)(2,1)} %bitcast.182, bf16[512,1024]{1,0:T(8,128)(2,1)} %convolution_convert_fusion.3.grad_ref, bf16[512,1024]{1,0:T(8,128)(2,1)} %get-tuple-element.54.mixed_ref, ...), custom_call_target="tpu_custom_call" | custom-call | tf_op jit(solution)/shard_map/pallas_call | solution.py:397
  601.1 3.2 mul.793
  606.7 2.8 multiply_reduce_fusion.9
  611.5 3.0 convolution_convert_fusion
  623.1 18.2 %shard_map.268 = (bf16[1152,896]{1,0:T(8,128)(2,1)}, bf16[1152,896]{1,0:T(8,128)(2,1)}) custom-call(bf16[1024,1152]{1,0:T(8,128)(2,1)} %shard_map.229.x_ref.refs_0_, bf16[1024,1152]{1,0:T(8,128)(2,1)} %shard_map.231.x_ref.other_ref.refs_1_, bf16[1024,3584]{1,0:T(8,128)(2,1)} %shard_map.266.refs_2_, bf16[1024,3584]{1,0:T(8,128)(2,1)} %shard_map.267.refs_3_), custom_call_target="tpu_custom_call" | custom-call | tf_op jit(solution)/shard_map/pallas_call | solution.py:552
  647.9 12.3 %collective-permute-done.59 = bf16[1152,256]{1,0:T(8,128)(2,1)S(1)} collective-permute-done((bf16[1152,256]{1,0:T(8,128)(2,1)S(1)}, bf16[1152,256]{1,0:T(8,128)(2,1)S(1)}, u32[]{:S(2)}, u32[]{:S(2)}) %collective-permute-start.59) | collective-permute-done | bytes 589856 | tf_op jit(solution)/shard_map/ppermute | solution.py:77
  663.2 2.5 collective-permute-start.57
  684.5 5.3 multiply_reduce_fusion.2
  696.9 12.9 %reduce-scatter.14.cloned.1.call-done = bf16[288,896]{1,0:T(8,128)(2,1)} async-done(((bf16[1152,896]{1,0:T(8,128)(2,1)}), bf16[288,896]{1,0:T(8,128)(2,1)}) %reduce-scatter.14.cloned.1.call-update) | async-done | bytes 516112 | tf_op jit(solution)/shard_map/reduce_scatter | solution.py:692
  712.3 3.8 all-to-all-start.1
  716.1 6.6 fusion.10
  723.3 3.3 collective-permute-start.70
  728.6 2.4 collective-permute-start.63
  731.0 2.8 collective-permute-start.62
  733.9 2.6 collective-permute-done.64
  736.5 5.6 collective-permute-done.63
  756.4 4.0 all-to-all-start.2
  761.2 6.0 all-to-all-done.2
  772.0 9.2 %fusion.79 = (bf16[36,23296]{1,0:T(8,128)(2,1)}, f32[36,23296]{1,0:T(8,128)}, f32[36,23296]{1,0:T(8,128)}, f32[36,23296]{1,0:T(8,128)}) fusion(f32[36,23296]{1,0:T(8,128)} %param.20, bf16[36,23296]{1,0:T(8,128)(2,1)} %slice_dynamic-update-slice_fusion, f32[36,23296]{1,0:T(8,128)} %param.23, f32[36,23296]{1,0:T(8,128)} %param.26), kind=kLoop, calls=%fused_computation.340 | loop fusion | flops 14257152 | bytes 23482368 | tf_op jit(solution)/shard_map/convert_element_type | solution.py:819
  (726 shorter events, 254.3 us)
Async XLA Ops:
  11.7 28.2 %all-to-all-start = ((bf16[8,36,2688]{2,1,0:T(8,128)(2,1)}), bf16[8,36,2688]{2,1,0:T(8,128)(2,1)}, u32[]{:S(2)}, u32[]{:S(2)}) async-start(bf16[8,36,2688]{2,1,0:T(8,128)(2,1)} %pad_maximum_fusion.5), calls=%async_computation | async-start | bytes 3440640 | tf_op jit(solution)/shard_map/all_to_all | solution.py:598
  17.1 147.8 %all-gather.4.cloned.1.call-start = ((), (), s32[]{:S(2)}) async-start(), calls=%async_computation.8 | async-start | bytes 5160960 | tf_op jit(solution)/shard_map/all_gather | solution.py:601
  24.7 12.9 %collective-permute-start.2 = (bf16[72,896]{1,0:T(8,128)(2,1)S(1)}, bf16[72,896]{1,0:T(8,128)(2,1)S(1)}, u32[]{:S(2)}, u32[]{:S(2)}) collective-permute-start(bf16[72,896]{1,0:T(8,128)(2,1)S(1)} %pad_maximum_fusion.33), channel_id=1, source_target_pairs={{2,0},{3,1},{0,2},{1,3},{6,4},{7,5},{4,6},{5,7},{10,8},{11,9},{8,1... | collective-permute-start | bytes 387080 | tf_op jit(solution)/shard_map/ppermute | solution.py:73
  27.8 9.8 %collective-permute-start.3 = (bf16[72,896]{1,0:T(8,128)(2,1)S(1)}, bf16[72,896]{1,0:T(8,128)(2,1)S(1)}, u32[]{:S(2)}, u32[]{:S(2)}) collective-permute-start(bf16[72,896]{1,0:T(8,128)(2,1)S(1)} %pad_maximum_fusion.33), channel_id=1, source_target_pairs={{3,0},{0,1},{1,2},{2,3},{7,4},{4,5},{5,6},{6,7},{11,8},{8,9},{9,10... | collective-permute-start | bytes 387080 | tf_op jit(solution)/shard_map/ppermute | solution.py:73
  29.4 9.5 %collective-permute-start.1 = (bf16[72,896]{1,0:T(8,128)(2,1)S(1)}, bf16[72,896]{1,0:T(8,128)(2,1)S(1)}, u32[]{:S(2)}, u32[]{:S(2)}) collective-permute-start(bf16[72,896]{1,0:T(8,128)(2,1)S(1)} %pad_maximum_fusion.33), channel_id=1, source_target_pairs={{1,0},{2,1},{3,2},{0,3},{5,4},{6,5},{7,6},{4,7},{9,8},{10,9},{11,1... | collective-permute-start | bytes 387080 | tf_op jit(solution)/shard_map/ppermute | solution.py:73
  46.8 9.6 %collective-permute-start.6 = (bf16[4,72,512]{2,1,0:T(8,128)(2,1)S(1)}, bf16[4,72,512]{2,1,0:T(8,128)(2,1)S(1)}, u32[]{:S(2)}, u32[]{:S(2)}) collective-permute-start(bf16[4,72,512]{2,1,0:T(8,128)(2,1)S(1)} %slice.357), channel_id=1, source_target_pairs={{16,0},{20,4},{24,8},{28,12},{0,16},{4,20},{8,24},{12,28},{17,1},{... | collective-permute-start | bytes 884744 | tf_op jit(solution)/shard_map/ppermute | solution.py:77
  51.8 12.3 %collective-permute-start.5 = (bf16[4,2,72,384]{3,2,0,1:T(8,128)(2,1)S(1)}, bf16[4,2,72,384]{3,2,0,1:T(8,128)(2,1)S(1)}, u32[]{:S(2)}, u32[]{:S(2)}) collective-permute-start(bf16[4,2,72,384]{3,2,0,1:T(8,128)(2,1)S(1)} %pad_maximum_fusion.28), channel_id=1, source_target_pairs={{16,0},{20,4},{24,8},{28,12},{0,16},{4,20},{8,24},{12,28},{17,1},{... | collective-permute-start | bytes 1327112 | tf_op jit(solution)/shard_map/ppermute | solution.py:77
  56.5 11.5 %collective-permute-start.7 = (bf16[4,2,72,512]{3,2,0,1:T(8,128)(2,1)S(1)}, bf16[4,2,72,512]{3,2,0,1:T(8,128)(2,1)S(1)}, u32[]{:S(2)}, u32[]{:S(2)}) collective-permute-start(bf16[4,2,72,512]{3,2,0,1:T(8,128)(2,1)S(1)} %pad_maximum_fusion.13), channel_id=1, source_target_pairs={{8,0},{12,4},{0,8},{4,12},{24,16},{28,20},{16,24},{20,28},{9,1},{1... | collective-permute-start | bytes 1769480 | tf_op jit(solution)/shard_map/ppermute | solution.py:77
  76.4 135.0 %all-gather.6.cloned.1.call-start = ((), (), s32[]{:S(2)}) async-start(), calls=%async_computation.9 | async-start | bytes 2621440 | tf_op jit(solution)/shard_map/all_gather | solution.py:639
  96.7 15.5 %collective-permute-start.11 = (bf16[72,512]{1,0:T(8,128)(2,1)S(1)}, bf16[72,512]{1,0:T(8,128)(2,1)S(1)}, u32[]{:S(2)}, u32[]{:S(2)}) collective-permute-start(bf16[72,512]{1,0:T(8,128)(2,1)S(1)} %pad_maximum_fusion.34), channel_id=1, source_target_pairs={{2,0},{3,1},{0,2},{1,3},{6,4},{7,5},{4,6},{5,7},{10,8},{11,9},{8,1... | collective-permute-start | bytes 221192 | tf_op jit(solution)/shard_map/ppermute | solution.py:73
  102.8 9.4 %collective-permute-start.12 = (bf16[72,512]{1,0:T(8,128)(2,1)S(1)}, bf16[72,512]{1,0:T(8,128)(2,1)S(1)}, u32[]{:S(2)}, u32[]{:S(2)}) collective-permute-start(bf16[72,512]{1,0:T(8,128)(2,1)S(1)} %pad_maximum_fusion.34), channel_id=1, source_target_pairs={{3,0},{0,1},{1,2},{2,3},{7,4},{4,5},{5,6},{6,7},{11,8},{8,9},{9,10... | collective-permute-start | bytes 221192 | tf_op jit(solution)/shard_map/ppermute | solution.py:73
  102.8 11.7 %collective-permute-start.10 = (bf16[72,512]{1,0:T(8,128)(2,1)S(1)}, bf16[72,512]{1,0:T(8,128)(2,1)S(1)}, u32[]{:S(2)}, u32[]{:S(2)}) collective-permute-start(bf16[72,512]{1,0:T(8,128)(2,1)S(1)} %pad_maximum_fusion.34), channel_id=1, source_target_pairs={{1,0},{2,1},{3,2},{0,3},{5,4},{6,5},{7,6},{4,7},{9,8},{10,9},{11,1... | collective-permute-start | bytes 221192 | tf_op jit(solution)/shard_map/ppermute | solution.py:73
  164.9 114.9 %all-gather.8.cloned.1.call-start = ((), (), s32[]{:S(2)}) async-start(), calls=%async_computation.10 | async-start | bytes 2580480 | tf_op jit(solution)/shard_map/all_gather | solution.py:640
  166.2 113.6 %collective-permute-start.24 = (bf16[1152,1792]{1,0:T(8,128)(2,1)}, bf16[1152,1792]{1,0:T(8,128)(2,1)}, u32[]{:S(2)}, u32[]{:S(2)}) collective-permute-start(bf16[1152,1792]{1,0:T(8,128)(2,1)} %all-gather.4.cloned.1.call-done.other_ref.own_ref), channel_id=1, source_target_pairs={{4,0},{0,4},{12,8},{8,12},{20,16},{16,20},{28,24},{24,28},{5,1},{1... | collective-permute-start | bytes 12386312 | tf_op jit(solution)/shard_map/ppermute | solution.py:77
  228.1 10.2 %collective-permute-start.18 = (bf16[128,1152]{1,0:T(8,128)(2,1)}, bf16[128,1152]{1,0:T(8,128)(2,1)}, u32[]{:S(2)}, u32[]{:S(2)}) collective-permute-start(bf16[128,1152]{1,0:T(8,128)(2,1)} %get-tuple-element.141), channel_id=1, source_target_pairs={{8,0},{12,4},{0,8},{4,12},{24,16},{28,20},{16,24},{20,28},{9,1},{1... | collective-permute-start | bytes 884744 | tf_op jit(solution)/shard_map/ppermute | solution.py:77
  229.6 13.9 %collective-permute-start.22 = (bf16[128,1152]{1,0:T(8,128)(2,1)}, bf16[128,1152]{1,0:T(8,128)(2,1)}, u32[]{:S(2)}, u32[]{:S(2)}) collective-permute-start(bf16[128,1152]{1,0:T(8,128)(2,1)} %get-tuple-element.140), channel_id=1, source_target_pairs={{8,0},{12,4},{0,8},{4,12},{24,16},{28,20},{16,24},{20,28},{9,1},{1... | collective-permute-start | bytes 884744 | tf_op jit(solution)/shard_map/ppermute | solution.py:77
  232.0 14.1 %collective-permute-start.20 = (bf16[128,1152]{1,0:T(8,128)(2,1)}, bf16[128,1152]{1,0:T(8,128)(2,1)}, u32[]{:S(2)}, u32[]{:S(2)}) collective-permute-start(bf16[128,1152]{1,0:T(8,128)(2,1)} %get-tuple-element.136), channel_id=1, source_target_pairs={{16,0},{20,4},{24,8},{28,12},{0,16},{4,20},{8,24},{12,28},{17,1},{... | collective-permute-start | bytes 884744 | tf_op jit(solution)/shard_map/ppermute | solution.py:77
  233.5 15.3 %collective-permute-start.23 = (bf16[128,1152]{1,0:T(8,128)(2,1)}, bf16[128,1152]{1,0:T(8,128)(2,1)}, u32[]{:S(2)}, u32[]{:S(2)}) collective-permute-start(bf16[128,1152]{1,0:T(8,128)(2,1)} %get-tuple-element.139), channel_id=1, source_target_pairs={{16,0},{20,4},{24,8},{28,12},{0,16},{4,20},{8,24},{12,28},{17,1},{... | collective-permute-start | bytes 884744 | tf_op jit(solution)/shard_map/ppermute | solution.py:77
  234.1 331.1 %reduce-scatter.6.cloned.1.call-start = ((), (), s32[]{:S(2)}) async-start(), calls=%async_computation.11 | async-start | bytes 2580480 | tf_op jit(solution)/shard_map/reduce_scatter | solution.py:692
  239.5 21.7 %collective-permute-start.19 = (bf16[256,1152]{1,0:T(8,128)(2,1)S(1)}, bf16[256,1152]{1,0:T(8,128)(2,1)S(1)}, u32[]{:S(2)}, u32[]{:S(2)}) collective-permute-start(bf16[256,1152]{1,0:T(8,128)(2,1)S(1)} %pad_maximum_fusion.16), channel_id=1, source_target_pairs={{16,0},{20,4},{24,8},{28,12},{0,16},{4,20},{8,24},{12,28},{17,1},{... | collective-permute-start | bytes 1769480 | tf_op jit(solution)/shard_map/ppermute | solution.py:77
  244.6 27.4 %collective-permute-start.25 = (bf16[256,1152]{1,0:T(8,128)(2,1)S(1)}, bf16[256,1152]{1,0:T(8,128)(2,1)S(1)}, u32[]{:S(2)}, u32[]{:S(2)}) collective-permute-start(bf16[256,1152]{1,0:T(8,128)(2,1)S(1)} %pad_maximum_fusion.18.other_ref), channel_id=1, source_target_pairs={{16,0},{20,4},{24,8},{28,12},{0,16},{4,20},{8,24},{12,28},{17,1},{... | collective-permute-start | bytes 1769480 | tf_op jit(solution)/shard_map/ppermute | solution.py:77
  247.3 27.4 %collective-permute-start.21 = (bf16[256,1152]{1,0:T(8,128)(2,1)S(1)}, bf16[256,1152]{1,0:T(8,128)(2,1)S(1)}, u32[]{:S(2)}, u32[]{:S(2)}) collective-permute-start(bf16[256,1152]{1,0:T(8,128)(2,1)S(1)} %pad_maximum_fusion.17), channel_id=1, source_target_pairs={{8,0},{12,4},{0,8},{4,12},{24,16},{28,20},{16,24},{20,28},{9,1},{1... | collective-permute-start | bytes 1769480 | tf_op jit(solution)/shard_map/ppermute | solution.py:77
  250.7 27.1 %collective-permute-start.26 = (bf16[256,1152]{1,0:T(8,128)(2,1)}, bf16[256,1152]{1,0:T(8,128)(2,1)}, u32[]{:S(2)}, u32[]{:S(2)}) collective-permute-start(bf16[256,1152]{1,0:T(8,128)(2,1)} %pad_maximum_fusion.19.other_ref), channel_id=1, source_target_pairs={{8,0},{12,4},{0,8},{4,12},{24,16},{28,20},{16,24},{20,28},{9,1},{1... | collective-permute-start | bytes 1769480 | tf_op jit(solution)/shard_map/ppermute | solution.py:77
  296.1 16.2 %collective-permute-start.27 = (bf16[1152,896]{1,0:T(8,128)(2,1)}, bf16[1152,896]{1,0:T(8,128)(2,1)S(1)}, u32[]{:S(2)}, u32[]{:S(2)}) collective-permute-start(bf16[1152,896]{1,0:T(8,128)(2,1)} %shard_map.234.own_ref.own_down_ref), channel_id=1, source_target_pairs={{4,0},{0,4},{12,8},{8,12},{20,16},{16,20},{28,24},{24,28},{5,1},{1... | collective-permute-start | bytes 6193160 | tf_op jit(solution)/shard_map/ppermute | solution.py:77
  324.6 15.9 %collective-permute-start.28 = (bf16[256,1152]{1,0:T(8,128)(2,1)S(1)}, bf16[256,1152]{1,0:T(8,128)(2,1)}, u32[]{:S(2)}, u32[]{:S(2)}) collective-permute-start(bf16[256,1152]{1,0:T(8,128)(2,1)S(1)} %get-tuple-element.126.other_ref), channel_id=1, source_target_pairs={{16,0},{20,4},{24,8},{28,12},{0,16},{4,20},{8,24},{12,28},{17,1},{... | collective-permute-start | bytes 1769480 | tf_op jit(solution)/shard_map/ppermute | solution.py:77
  326.2 15.5 %collective-permute-start.30 = (bf16[256,1152]{1,0:T(8,128)(2,1)S(1)}, bf16[256,1152]{1,0:T(8,128)(2,1)}, u32[]{:S(2)}, u32[]{:S(2)}) collective-permute-start(bf16[256,1152]{1,0:T(8,128)(2,1)S(1)} %get-tuple-element.125.other_ref), channel_id=1, source_target_pairs={{8,0},{12,4},{0,8},{4,12},{24,16},{28,20},{16,24},{20,28},{9,1},{1... | collective-permute-start | bytes 1769480 | tf_op jit(solution)/shard_map/ppermute | solution.py:77
  343.6 10.0 %collective-permute-start.31 = (bf16[128,1152]{1,0:T(8,128)(2,1)S(1)}, bf16[128,1152]{1,0:T(8,128)(2,1)S(1)}, u32[]{:S(2)}, u32[]{:S(2)}) collective-permute-start(bf16[128,1152]{1,0:T(8,128)(2,1)S(1)} %slice.626), channel_id=1, source_target_pairs={{16,0},{20,4},{24,8},{28,12},{0,16},{4,20},{8,24},{12,28},{17,1},{... | collective-permute-start | bytes 884744 | tf_op jit(solution)/shard_map/ppermute | solution.py:77
  344.3 26.3 %collective-permute-start.32 = (bf16[256,1152]{1,0:T(8,128)(2,1)S(1)}, bf16[256,1152]{1,0:T(8,128)(2,1)S(1)}, u32[]{:S(2)}, u32[]{:S(2)}) collective-permute-start(bf16[256,1152]{1,0:T(8,128)(2,1)S(1)} %get-tuple-element.121), channel_id=1, source_target_pairs={{16,0},{20,4},{24,8},{28,12},{0,16},{4,20},{8,24},{12,28},{17,1},{... | collective-permute-start | bytes 1769480 | tf_op jit(solution)/shard_map/ppermute | solution.py:77
  345.8 24.7 %collective-permute-start.35 = (bf16[256,1152]{1,0:T(8,128)(2,1)S(1)}, bf16[256,1152]{1,0:T(8,128)(2,1)S(1)}, u32[]{:S(2)}, u32[]{:S(2)}) collective-permute-start(bf16[256,1152]{1,0:T(8,128)(2,1)S(1)} %get-tuple-element.122), channel_id=1, source_target_pairs={{8,0},{12,4},{0,8},{4,12},{24,16},{28,20},{16,24},{20,28},{9,1},{1... | collective-permute-start | bytes 1769480 | tf_op jit(solution)/shard_map/ppermute | solution.py:77
  347.3 18.9 %collective-permute-start.29 = (bf16[128,1152]{1,0:T(8,128)(2,1)S(1)}, bf16[128,1152]{1,0:T(8,128)(2,1)S(1)}, u32[]{:S(2)}, u32[]{:S(2)}) collective-permute-start(bf16[128,1152]{1,0:T(8,128)(2,1)S(1)} %slice.627), channel_id=1, source_target_pairs={{8,0},{12,4},{0,8},{4,12},{24,16},{28,20},{16,24},{20,28},{9,1},{1... | collective-permute-start | bytes 884744 | tf_op jit(solution)/shard_map/ppermute | solution.py:77
  370.0 10.4 %collective-permute-start.38 = (bf16[128,1152]{1,0:T(8,128)(2,1)}, bf16[128,1152]{1,0:T(8,128)(2,1)}, u32[]{:S(2)}, u32[]{:S(2)}) collective-permute-start(bf16[128,1152]{1,0:T(8,128)(2,1)} %get-tuple-element.157), channel_id=1, source_target_pairs={{16,0},{20,4},{24,8},{28,12},{0,16},{4,20},{8,24},{12,28},{17,1},{... | collective-permute-start | bytes 884744 | tf_op jit(solution)/shard_map/ppermute | solution.py:77
  376.9 25.5 %collective-permute-start.37 = (bf16[256,1152]{1,0:T(8,128)(2,1)}, bf16[256,1152]{1,0:T(8,128)(2,1)}, u32[]{:S(2)}, u32[]{:S(2)}) collective-permute-start(bf16[256,1152]{1,0:T(8,128)(2,1)} %pad_maximum_fusion.20.other_ref), channel_id=1, source_target_pairs={{16,0},{20,4},{24,8},{28,12},{0,16},{4,20},{8,24},{12,28},{17,1},{... | collective-permute-start | bytes 1769480 | tf_op jit(solution)/shard_map/ppermute | solution.py:77
  377.6 18.4 %collective-permute-start.36 = (bf16[128,1152]{1,0:T(8,128)(2,1)}, bf16[128,1152]{1,0:T(8,128)(2,1)}, u32[]{:S(2)}, u32[]{:S(2)}) collective-permute-start(bf16[128,1152]{1,0:T(8,128)(2,1)} %shard_map.240), channel_id=1, source_target_pairs={{16,0},{20,4},{24,8},{28,12},{0,16},{4,20},{8,24},{12,28},{17,1},{... | collective-permute-start | bytes 884744 | tf_op jit(solution)/shard_map/ppermute | solution.py:77
  378.9 18.2 %collective-permute-start.34 = (bf16[128,1152]{1,0:T(8,128)(2,1)}, bf16[128,1152]{1,0:T(8,128)(2,1)S(1)}, u32[]{:S(2)}, u32[]{:S(2)}) collective-permute-start(bf16[128,1152]{1,0:T(8,128)(2,1)} %shard_map.239), channel_id=1, source_target_pairs={{8,0},{12,4},{0,8},{4,12},{24,16},{28,20},{16,24},{20,28},{9,1},{1... | collective-permute-start | bytes 884744 | tf_op jit(solution)/shard_map/ppermute | solution.py:77
  381.5 27.6 %collective-permute-start.39 = (bf16[256,1152]{1,0:T(8,128)(2,1)S(1)}, bf16[256,1152]{1,0:T(8,128)(2,1)S(1)}, u32[]{:S(2)}, u32[]{:S(2)}) collective-permute-start(bf16[256,1152]{1,0:T(8,128)(2,1)S(1)} %pad_maximum_fusion.21), channel_id=1, source_target_pairs={{8,0},{12,4},{0,8},{4,12},{24,16},{28,20},{16,24},{20,28},{9,1},{1... | collective-permute-start | bytes 1769480 | tf_op jit(solution)/shard_map/ppermute | solution.py:77
  401.1 9.5 %collective-permute-start.40 = (bf16[128,1152]{1,0:T(8,128)(2,1)S(1)}, bf16[128,1152]{1,0:T(8,128)(2,1)}, u32[]{:S(2)}, u32[]{:S(2)}) collective-permute-start(bf16[128,1152]{1,0:T(8,128)(2,1)S(1)} %get-tuple-element.156), channel_id=1, source_target_pairs={{8,0},{12,4},{0,8},{4,12},{24,16},{28,20},{16,24},{20,28},{9,1},{1... | collective-permute-start | bytes 884744 | tf_op jit(solution)/shard_map/ppermute | solution.py:77
  412.5 31.5 %collective-permute-start.43 = (bf16[256,1152]{1,0:T(8,128)(2,1)}, bf16[256,1152]{1,0:T(8,128)(2,1)S(1)}, u32[]{:S(2)}, u32[]{:S(2)}) collective-permute-start(bf16[256,1152]{1,0:T(8,128)(2,1)} %shard_map.243.other_ref), channel_id=1, source_target_pairs={{8,0},{12,4},{0,8},{4,12},{24,16},{28,20},{16,24},{20,28},{9,1},{1... | collective-permute-start | bytes 1769480 | tf_op jit(solution)/shard_map/ppermute | solution.py:77
  413.7 30.2 %collective-permute-start.42 = (bf16[256,1152]{1,0:T(8,128)(2,1)}, bf16[256,1152]{1,0:T(8,128)(2,1)S(1)}, u32[]{:S(2)}, u32[]{:S(2)}) collective-permute-start(bf16[256,1152]{1,0:T(8,128)(2,1)} %shard_map.241.other_ref), channel_id=1, source_target_pairs={{16,0},{20,4},{24,8},{28,12},{0,16},{4,20},{8,24},{12,28},{17,1},{... | collective-permute-start | bytes 1769480 | tf_op jit(solution)/shard_map/ppermute | solution.py:77
  467.6 36.8 %collective-permute-start.52 = (bf16[1152,896]{1,0:T(8,128)(2,1)}, bf16[1152,896]{1,0:T(8,128)(2,1)}, u32[]{:S(2)}, u32[]{:S(2)}) collective-permute-start(bf16[1152,896]{1,0:T(8,128)(2,1)} %get-tuple-element.65), channel_id=1, source_target_pairs={{4,0},{0,4},{12,8},{8,12},{20,16},{16,20},{28,24},{24,28},{5,1},{1... | collective-permute-start | bytes 6193160 | tf_op jit(solution)/shard_map/ppermute | solution.py:77
  467.6 33.6 %collective-permute-start.46 = (bf16[256,1152]{1,0:T(8,128)(2,1)S(1)}, bf16[256,1152]{1,0:T(8,128)(2,1)S(1)}, u32[]{:S(2)}, u32[]{:S(2)}) collective-permute-start(bf16[256,1152]{1,0:T(8,128)(2,1)S(1)} %copy-done.41), channel_id=1, source_target_pairs={{16,0},{20,4},{24,8},{28,12},{0,16},{4,20},{8,24},{12,28},{17,1},{... | collective-permute-start | bytes 1769480 | tf_op jit(solution)/shard_map/ppermute | solution.py:77
  469.1 32.2 %collective-permute-start.48 = (bf16[256,1152]{1,0:T(8,128)(2,1)S(1)}, bf16[256,1152]{1,0:T(8,128)(2,1)S(1)}, u32[]{:S(2)}, u32[]{:S(2)}) collective-permute-start(bf16[256,1152]{1,0:T(8,128)(2,1)S(1)} %copy-done.40), channel_id=1, source_target_pairs={{8,0},{12,4},{0,8},{4,12},{24,16},{28,20},{16,24},{20,28},{9,1},{1... | collective-permute-start | bytes 1769480 | tf_op jit(solution)/shard_map/ppermute | solution.py:77
  499.3 24.5 %collective-permute-start.45 = (bf16[256,1152]{1,0:T(8,128)(2,1)}, bf16[256,1152]{1,0:T(8,128)(2,1)}, u32[]{:S(2)}, u32[]{:S(2)}) collective-permute-start(bf16[256,1152]{1,0:T(8,128)(2,1)} %get-tuple-element.115), channel_id=1, source_target_pairs={{8,0},{12,4},{0,8},{4,12},{24,16},{28,20},{16,24},{20,28},{9,1},{1... | collective-permute-start | bytes 1769480 | tf_op jit(solution)/shard_map/ppermute | solution.py:77
  500.5 23.3 %collective-permute-start.44 = (bf16[256,1152]{1,0:T(8,128)(2,1)}, bf16[256,1152]{1,0:T(8,128)(2,1)}, u32[]{:S(2)}, u32[]{:S(2)}) collective-permute-start(bf16[256,1152]{1,0:T(8,128)(2,1)} %get-tuple-element.116), channel_id=1, source_target_pairs={{16,0},{20,4},{24,8},{28,12},{0,16},{4,20},{8,24},{12,28},{17,1},{... | collective-permute-start | bytes 1769480 | tf_op jit(solution)/shard_map/ppermute | solution.py:77
  502.3 19.7 %collective-permute-start.49 = (bf16[128,1152]{1,0:T(8,128)(2,1)}, bf16[128,1152]{1,0:T(8,128)(2,1)}, u32[]{:S(2)}, u32[]{:S(2)}) collective-permute-start(bf16[128,1152]{1,0:T(8,128)(2,1)} %slice.620.other_ref), channel_id=1, source_target_pairs={{16,0},{20,4},{24,8},{28,12},{0,16},{4,20},{8,24},{12,28},{17,1},{... | collective-permute-start | bytes 884744 | tf_op jit(solution)/shard_map/ppermute | solution.py:77
  508.4 112.7 %reduce-scatter.8.cloned.1.call-start = ((), (), s32[]{:S(2)}) async-start(), calls=%async_computation.12 | async-start | bytes 2580480 | tf_op jit(solution)/shard_map/reduce_scatter | solution.py:692
  510.8 34.1 %collective-permute-start.47 = (bf16[128,1152]{1,0:T(8,128)(2,1)}, bf16[128,1152]{1,0:T(8,128)(2,1)}, u32[]{:S(2)}, u32[]{:S(2)}) collective-permute-start(bf16[128,1152]{1,0:T(8,128)(2,1)} %slice.621.other_ref), channel_id=1, source_target_pairs={{8,0},{12,4},{0,8},{4,12},{24,16},{28,20},{16,24},{20,28},{9,1},{1... | collective-permute-start | bytes 884744 | tf_op jit(solution)/shard_map/ppermute | solution.py:77
  544.8 15.2 %collective-permute-start.53 = (bf16[1152,896]{1,0:T(8,128)(2,1)}, bf16[1152,896]{1,0:T(8,128)(2,1)}, u32[]{:S(2)}, u32[]{:S(2)}) collective-permute-start(bf16[1152,896]{1,0:T(8,128)(2,1)} %get-tuple-element.69), channel_id=1, source_target_pairs={{4,0},{0,4},{12,8},{8,12},{20,16},{16,20},{28,24},{24,28},{5,1},{1... | collective-permute-start | bytes 6193160 | tf_op jit(solution)/shard_map/ppermute | solution.py:77
  546.7 9.7 %collective-permute-start.51 = (bf16[128,1152]{1,0:T(8,128)(2,1)}, bf16[128,1152]{1,0:T(8,128)(2,1)}, u32[]{:S(2)}, u32[]{:S(2)}) collective-permute-start(bf16[128,1152]{1,0:T(8,128)(2,1)} %slice.622.other_ref), channel_id=1, source_target_pairs={{16,0},{20,4},{24,8},{28,12},{0,16},{4,20},{8,24},{12,28},{17,1},{... | collective-permute-start | bytes 884744 | tf_op jit(solution)/shard_map/ppermute | solution.py:77
  547.3 10.1 %collective-permute-start.50 = (bf16[128,1152]{1,0:T(8,128)(2,1)}, bf16[128,1152]{1,0:T(8,128)(2,1)}, u32[]{:S(2)}, u32[]{:S(2)}) collective-permute-start(bf16[128,1152]{1,0:T(8,128)(2,1)} %slice.623.other_ref), channel_id=1, source_target_pairs={{8,0},{12,4},{0,8},{4,12},{24,16},{28,20},{16,24},{20,28},{9,1},{1... | collective-permute-start | bytes 884744 | tf_op jit(solution)/shard_map/ppermute | solution.py:77
  565.1 102.5 %reduce-scatter.10.cloned.1.call-start = ((), (), s32[]{:S(2)}) async-start(), calls=%async_computation.13 | async-start | bytes 2621440 | tf_op jit(solution)/shard_map/reduce_scatter | solution.py:726
  615.7 27.1 %collective-permute-start.58 = (bf16[1152,512]{1,0:T(8,128)(2,1)}, bf16[1152,512]{1,0:T(8,128)(2,1)}, u32[]{:S(2)}, u32[]{:S(2)}) collective-permute-start(bf16[1152,512]{1,0:T(8,128)(2,1)} %constant_dynamic-slice_fusion.5), channel_id=1, source_target_pairs={{4,0},{0,4},{12,8},{8,12},{20,16},{16,20},{28,24},{24,28},{5,1},{1... | collective-permute-start | bytes 3538952 | tf_op jit(solution)/shard_map/ppermute | solution.py:77
  621.2 88.5 %reduce-scatter.14.cloned.1.call-start = ((), (), s32[]{:S(2)}) async-start(), calls=%async_computation.15 | async-start | bytes 2580480 | tf_op jit(solution)/shard_map/reduce_scatter | solution.py:692
  622.8 22.4 %collective-permute-start.55 = (bf16[1152,512]{1,0:T(8,128)(2,1)S(1)}, bf16[1152,512]{1,0:T(8,128)(2,1)}, u32[]{:S(2)}, u32[]{:S(2)}) collective-permute-start(bf16[1152,512]{1,0:T(8,128)(2,1)S(1)} %constant_dynamic-slice_fusion.8), channel_id=1, source_target_pairs={{4,0},{0,4},{12,8},{8,12},{20,16},{16,20},{28,24},{24,28},{5,1},{1... | collective-permute-start | bytes 3538952 | tf_op jit(solution)/shard_map/ppermute | solution.py:77
  641.3 24.4 %collective-permute-start.54 = (bf16[1152,896]{1,0:T(8,128)(2,1)}, bf16[1152,896]{1,0:T(8,128)(2,1)S(1)}, u32[]{:S(2)}, u32[]{:S(2)}) collective-permute-start(bf16[1152,896]{1,0:T(8,128)(2,1)} %get-tuple-element.71), channel_id=1, source_target_pairs={{4,0},{0,4},{12,8},{8,12},{20,16},{16,20},{28,24},{24,28},{5,1},{1... | collective-permute-start | bytes 6193160 | tf_op jit(solution)/shard_map/ppermute | solution.py:77
  644.7 15.5 %collective-permute-start.59 = (bf16[1152,256]{1,0:T(8,128)(2,1)S(1)}, bf16[1152,256]{1,0:T(8,128)(2,1)S(1)}, u32[]{:S(2)}, u32[]{:S(2)}) collective-permute-start(bf16[1152,256]{1,0:T(8,128)(2,1)S(1)} %constant_dynamic-slice_fusion.4), channel_id=1, source_target_pairs={{16,0},{20,4},{24,8},{28,12},{0,16},{4,20},{8,24},{12,28},{17,1},{... | collective-permute-start | bytes 1769480 | tf_op jit(solution)/shard_map/ppermute | solution.py:77
  647.0 15.2 %collective-permute-start.56 = (bf16[1152,256]{1,0:T(8,128)(2,1)S(1)}, bf16[1152,256]{1,0:T(8,128)(2,1)S(1)}, u32[]{:S(2)}, u32[]{:S(2)}) collective-permute-start(bf16[1152,256]{1,0:T(8,128)(2,1)S(1)} %constant_dynamic-slice_fusion.7), channel_id=1, source_target_pairs={{8,0},{12,4},{0,8},{4,12},{24,16},{28,20},{16,24},{20,28},{9,1},{1... | collective-permute-start | bytes 1769480 | tf_op jit(solution)/shard_map/ppermute | solution.py:77
  669.8 74.2 %reduce-scatter.12.cloned.1.call-start = ((), (), s32[]{:S(2)}) async-start(), calls=%async_computation.14 | async-start | bytes 737280 | tf_op jit(solution)/shard_map/reduce_scatter | solution.py:692
  692.1 34.5 %collective-permute-start.61 = (bf16[1152,256]{1,0:T(8,128)(2,1)S(1)}, bf16[1152,256]{1,0:T(8,128)(2,1)}, u32[]{:S(2)}, u32[]{:S(2)}) collective-permute-start(bf16[1152,256]{1,0:T(8,128)(2,1)S(1)} %copy-done.58), channel_id=1, source_target_pairs={{4,0},{0,4},{12,8},{8,12},{20,16},{16,20},{28,24},{24,28},{5,1},{1... | collective-permute-start | bytes 1769480 | tf_op jit(solution)/shard_map/ppermute | solution.py:77
  696.4 26.3 %collective-permute-start.69 = (f32[40,128]{1,0:T(8,128)S(1)}, f32[40,128]{1,0:T(8,128)S(1)}, u32[]{:S(2)}, u32[]{:S(2)}) collective-permute-start(f32[40,128]{1,0:T(8,128)S(1)} %fusion.112), channel_id=1, source_target_pairs={{8,0},{12,4},{0,8},{4,12},{24,16},{28,20},{16,24},{20,28},{9,1},{1... | collective-permute-start | bytes 61448 | tf_op jit(solution)/shard_map/ppermute | solution.py:77
  712.3 30.5 %all-to-all-start.1 = ((bf16[8,36,2688]{2,1,0:T(8,128)(2,1)}), bf16[8,36,2688]{2,1,0:T(8,128)(2,1)S(1)}, u32[]{:S(2)}, u32[]{:S(2)}) async-start(bf16[8,36,2688]{2,1,0:T(8,128)(2,1)} %reshape.527), calls=%async_computation.6 | async-start | bytes 3440640 | tf_op jit(solution)/shard_map/all_to_all | solution.py:695
  723.3 10.5 %collective-permute-start.70 = (f32[40,128]{1,0:T(8,128)S(1)}, f32[40,128]{1,0:T(8,128)S(1)}, u32[]{:S(2)}, u32[]{:S(2)}) collective-permute-start(f32[40,128]{1,0:T(8,128)S(1)} %add.602), channel_id=1, source_target_pairs={{1,0},{2,1},{3,2},{0,3},{5,4},{6,5},{7,6},{4,7},{9,8},{10,9},{11,1... | collective-permute-start | bytes 61448 | tf_op jit(solution)/shard_map/ppermute | solution.py:73
  728.6 13.5 %collective-permute-start.63 = (bf16[288,256]{1,0:T(8,128)(2,1)S(1)}, bf16[288,256]{1,0:T(8,128)(2,1)S(1)}, u32[]{:S(2)}, u32[]{:S(2)}) collective-permute-start(bf16[288,256]{1,0:T(8,128)(2,1)S(1)} %get-tuple-element.154), channel_id=1, source_target_pairs={{2,0},{3,1},{0,2},{1,3},{6,4},{7,5},{4,6},{5,7},{10,8},{11,9},{8,1... | collective-permute-start | bytes 442376 | tf_op jit(solution)/shard_map/ppermute | solution.py:73
  731.0 11.1 %collective-permute-start.62 = (bf16[288,256]{1,0:T(8,128)(2,1)S(1)}, bf16[288,256]{1,0:T(8,128)(2,1)S(1)}, u32[]{:S(2)}, u32[]{:S(2)}) collective-permute-start(bf16[288,256]{1,0:T(8,128)(2,1)S(1)} %get-tuple-element.152), channel_id=1, source_target_pairs={{1,0},{2,1},{3,2},{0,3},{5,4},{6,5},{7,6},{4,7},{9,8},{10,9},{11,1... | collective-permute-start | bytes 442376 | tf_op jit(solution)/shard_map/ppermute | solution.py:73
  756.4 10.8 %all-to-all-start.2 = ((bf16[8,36,384]{2,1,0:T(8,128)(2,1)}), bf16[8,36,384]{2,1,0:T(8,128)(2,1)S(1)}, u32[]{:S(2)}, u32[]{:S(2)}) async-start(bf16[8,36,384]{2,1,0:T(8,128)(2,1)} %reshape.528), calls=%async_computation.7 | async-start | bytes 491520 | tf_op jit(solution)/shard_map/all_to_all | solution.py:695
  (164 other events, 1226.8 us)
Sparse Core Ops, SparseCore 0:
  76.5 88.2 all-gather.3
  167.0 44.3 all-gather.5
  234.2 43.9 all-gather.7
  508.6 40.5 reduce-scatter.5
  565.2 40.6 reduce-scatter.7
  621.4 40.9 reduce-scatter.9
  669.9 39.8 reduce-scatter.13
  712.1 21.8 reduce-scatter.11

commit v5 on v4

--- a/solution.py
+++ b/solution.py
@@ -751,7 +751,7 @@
     back = to_rows(jnp.concatenate([summed_gate, summed_up, summed_down], axis=1))
     early = shard_sum(jnp.concatenate([query_share, out_share], axis=1))
     slices = scatter_parts(late_share.reshape(z_count, -1, late_share.shape[1]), "ctx")
-    late_rows = tie(tie(scatter_direct(slices, "ctx").astype(BF), back), early)
+    late_rows = tie(scatter_direct(slices, "ctx").astype(BF), early)
     late_rows = scatter_cols(late_rows, late_bits[1:])
     for bit in same_bits:
         late_rows = (late_rows.astype(F32) + flip(late_rows, bit).astype(F32)).astype(BF)

time: 797 us -> 814 us (1.021)
  waiting for transfers between devices: 237 us -> 251 us
    all_to_all x2, waiting for transfers between devices: 6.02 us -> 23.5 us  [to_rows(): lax.all_to_all(summed.reshape(dp_count, rows, summed.shape[1]), 'dp', 0,...]
    reduce_scatter x4, waiting for transfers between devices: 12.9 us -> 0.12 us  [shard_sum(): return lax.psum_scatter(grad, 'ctx', scatter_dimension=0, tiled=True)]
    ppermute x12, starting transfers between devices: 26.7 us -> 35.2 us  [shift(): lax.ppermute(values, axis, [((i + distance) % count, i) for i in range(co...]
    unnamed x317 -> x321, local copies, waits for them, and re-layouts: 43.9 us -> 45.5 us
  transfers between devices with their start and end apart: 84 -> 84, of which waited for: 38 -> 40; matrix products, arithmetic and copies ran while one was open for 23% -> 23% of each run, Pallas kernels for 18% -> 18%
where the time goes in v5:
time: 814 us; the launch traced here: 805 us
  waiting for transfers between devices  251 us (31%)
  Pallas kernels  189 us (23%)
  other arithmetic  113 us (14%)
  starting transfers between devices  105 us (13%)
  local copies, waits for them, and re-layouts  93.6 us (11%)
  matrix products  36.5 us (4%)
  between operations  17.9 us (2%)
    ppermute x61, waiting for transfers between devices, flip(): lax.ppermute(values, 'dp', [(i ^ bit, i) for i in range(lax.axis_size('dp...  124 us
    ppermute x61, starting transfers between devices, flip(): lax.ppermute(values, 'dp', [(i ^ bit, i) for i in range(lax.axis_size('dp...  56.9 us
    pallas_call x2, Pallas kernels, mlp_backward(): pl.pallas_call(mlp_back_kernel, grid=(rows // tile,), in_specs=[spec(widt...  54.1 us
    pallas_call x3, Pallas kernels, products(): pl.pallas_call(kernel, grid=(2,), in_specs=[left, left, right, right], ou...  53.1 us
    unnamed x321, local copies, waits for them, and re-layouts  45.5 us
    all_gather x1, waiting for transfers between devices, body(): key_value = lax.all_gather(key_value, 'ctx', axis=0, tiled=True)  45.3 us
    ppermute x12, starting transfers between devices, shift(): lax.ppermute(values, axis, [((i + distance) % count, i) for i in range(co...  35.2 us
    pallas_call x2, Pallas kernels, mlp_up(): pl.pallas_call(mlp_up_kernel, grid=(rows // tile,), in_specs=[spec(width)...  32.5 us
  transfers between devices with their start and end apart: 84, of which 40 were waited for; matrix products, arithmetic and copies ran while one was open for 23% of the time, Pallas kernels for 18%

profile of v5, /device:TPU:0, one launch (start us, length us, event | category | flops | bytes accessed | tf_op | source)
XLA Modules:
  0.0 805.2 jit_solution(8651166105402830188)
XLA Ops:
  11.7 5.3 all-to-all-start
  24.7 3.1 collective-permute-start.2
  31.7 6.0 collective-permute-done.2
  53.4 3.0 collective-permute-done.6
  56.6 7.5 collective-permute-done.5
  64.5 3.6 collective-permute-done.7
  71.3 3.3 multiply_reduce_fusion.8
  76.6 3.9 broadcast_select_fusion
  86.4 2.8 fusion.76
  96.7 6.1 collective-permute-start.11
  102.8 3.8 collective-permute-start.10
  107.3 4.8 collective-permute-done.11
  117.2 2.7 collective-permute-done.13
  124.5 3.0 collective-permute-done.16
  137.0 27.9 %all-gather.4.cloned.1.call-done.other_ref.own_ref = bf16[1152,1792]{1,0:T(8,128)(2,1)} async-done(((bf16[288,1792]{1,0:T(8,128)(2,1)}), bf16[1152,1792]{1,0:T(8,128)(2,1)}) %all-gather.4.cloned.1.call-update) | async-done | bytes 4128784 | tf_op jit(solution)/shard_map/all_gather | solution.py:601
  166.1 45.3 %all-gather.6.cloned.1.call-done.kv_ref.other_ref = bf16[2048,512]{1,0:T(8,128)(2,1)} async-done(((bf16[512,512]{1,0:T(8,128)(2,1)}), bf16[2048,512]{1,0:T(8,128)(2,1)}) %all-gather.6.cloned.1.call-update) | async-done | bytes 2097168 | tf_op jit(solution)/shard_map/all_gather | solution.py:639
  211.4 10.0 %shard_map.225 = (bf16[512,1024]{1,0:T(8,128)(2,1)}, f32[512,512]{1,0:T(8,128)}) custom-call(s32[2]{0:T(128)} %pad_add_fusion.2.info_ref, bf16[512,1024]{1,0:T(8,128)(2,1)} %bitcast.181, bf16[2048,512]{1,0:T(8,128)(2,1)} %all-gather.6.cloned.1.call-done.kv_ref.other_ref), custom_call_target="tpu_custom_call" | custom-call | tf_op jit(solution)/shard_map/pallas_call | solution.py:315
  221.5 3.1 multiply_reduce_fusion.7
  234.1 4.2 collective-permute-done.18
  240.9 2.5 collective-permute-done.22
  254.6 6.5 collective-permute-done.19
  261.2 10.8 %collective-permute-done.25 = bf16[256,1152]{1,0:T(8,128)(2,1)S(1)} collective-permute-done((bf16[256,1152]{1,0:T(8,128)(2,1)S(1)}, bf16[256,1152]{1,0:T(8,128)(2,1)S(1)}, u32[]{:S(2)}, u32[]{:S(2)}) %collective-permute-start.25) | collective-permute-done | bytes 589856 | tf_op jit(solution)/shard_map/ppermute | solution.py:77
  279.8 16.4 %shard_map.230 = (bf16[1024,3584]{1,0:T(8,128)(2,1)}, bf16[1024,1792]{1,0:T(8,128)(2,1)}) custom-call(bf16[1024,1152]{1,0:T(8,128)(2,1)} %shard_map.229.x_ref.refs_0_, bf16[1152,1792]{1,0:T(8,128)(2,1)} %all-gather.4.cloned.1.call-done.other_ref.own_ref, bf16[1152,1792]{1,0:T(8,128)(2,1)} %collective-permute-done.24.other_ref), custom_call_target="tpu_custom_call" | custom-call | tf_op jit(solution)/shard_map/pallas_call | solution.py:445
  296.2 16.2 %shard_map.232 = (bf16[1024,3584]{1,0:T(8,128)(2,1)}, bf16[1024,1792]{1,0:T(8,128)(2,1)}) custom-call(bf16[1024,1152]{1,0:T(8,128)(2,1)} %shard_map.231.x_ref.other_ref.refs_1_, bf16[1152,1792]{1,0:T(8,128)(2,1)} %all-gather.4.cloned.1.call-done.other_ref.own_ref, bf16[1152,1792]{1,0:T(8,128)(2,1)} %collective-permute-done.24.other_ref), custom_call_target="tpu_custom_call" | custom-call | tf_op jit(solution)/shard_map/pallas_call | solution.py:445
  313.7 9.5 %shard_map.235 = bf16[1024,1152]{1,0:T(8,128)(2,1)} custom-call(bf16[1024,1792]{1,0:T(8,128)(2,1)} %shard_map.233.hidden_ref.value_ref, bf16[1152,896]{1,0:T(8,128)(2,1)} %shard_map.234.own_ref.own_down_ref, bf16[1152,896]{1,0:T(8,128)(2,1)} %copy-done.11), custom_call_target="tpu_custom_call" | custom-call | tf_op jit(solution)/shard_map/pallas_call | solution.py:463
  329.7 10.3 %shard_map.238 = bf16[1024,1152]{1,0:T(8,128)(2,1)} custom-call(bf16[1024,1792]{1,0:T(8,128)(2,1)} %shard_map.237.hidden_ref.value_ref, bf16[1152,896]{1,0:T(8,128)(2,1)} %shard_map.234.own_ref.own_down_ref, bf16[1152,896]{1,0:T(8,128)(2,1)} %copy-done.11), custom_call_target="tpu_custom_call" | custom-call | tf_op jit(solution)/shard_map/pallas_call | solution.py:463
  348.0 5.6 collective-permute-done.31
  353.7 12.6 %collective-permute-done.29 = bf16[128,1152]{1,0:T(8,128)(2,1)S(1)} collective-permute-done((bf16[128,1152]{1,0:T(8,128)(2,1)S(1)}, bf16[128,1152]{1,0:T(8,128)(2,1)S(1)}, u32[]{:S(2)}, u32[]{:S(2)}) %collective-permute-start.29) | collective-permute-done | bytes 294944 | tf_op jit(solution)/shard_map/ppermute | solution.py:77
  372.7 2.7 collective-permute-done.33
  383.2 12.8 %collective-permute-done.36 = bf16[128,1152]{1,0:T(8,128)(2,1)} collective-permute-done((bf16[128,1152]{1,0:T(8,128)(2,1)}, bf16[128,1152]{1,0:T(8,128)(2,1)}, u32[]{:S(2)}, u32[]{:S(2)}) %collective-permute-start.36) | collective-permute-done | bytes 294944 | tf_op jit(solution)/shard_map/ppermute | solution.py:77
  403.6 3.6 collective-permute-done.41
  414.4 27.2 %shard_map.245 = (bf16[1024,1152]{1,0:T(8,128)(2,1)}, bf16[1024,3584]{1,0:T(8,128)(2,1)}) custom-call(bf16[1024,1152]{1,0:T(8,128)(2,1)} %shard_map.244.grad_ref.refs_0_, bf16[1024,3584]{1,0:T(8,128)(2,1)} %get-tuple-element.58.gate_up_ref, bf16[1152,1792]{1,0:T(8,128)(2,1)} %all-gather.4.cloned.1.call-done.other_ref.own_ref, ...), custom_call_target="tpu_custom_call" | custom-call | tf_op jit(solution)/shard_map/pallas_call | solution.py:511
  445.1 4.9 pad_maximum_fusion.2.refs_1_.grad_ref
  450.0 17.6 %shard_map.250 = (bf16[1152,896]{1,0:T(8,128)(2,1)}, bf16[1152,896]{1,0:T(8,128)(2,1)}) custom-call(bf16[1024,1152]{1,0:T(8,128)(2,1)} %shard_map.244.grad_ref.refs_0_, bf16[1024,1152]{1,0:T(8,128)(2,1)} %pad_maximum_fusion.2.refs_1_.grad_ref, bf16[1024,1792]{1,0:T(8,128)(2,1)} %shard_map.247.refs_2_, bf16[1024,1792]{1,0:T(8,128)(2,1)} %shard_map.249.refs_3_), custom_call_target="tpu_custom_call" | custom-call | tf_op jit(solution)/shard_map/pallas_call | solution.py:552
  469.9 27.0 %shard_map.252 = (bf16[1024,1152]{1,0:T(8,128)(2,1)}, bf16[1024,3584]{1,0:T(8,128)(2,1)}) custom-call(bf16[1024,1152]{1,0:T(8,128)(2,1)} %pad_maximum_fusion.2.refs_1_.grad_ref, bf16[1024,3584]{1,0:T(8,128)(2,1)} %shard_map.251.gate_up_ref, bf16[1152,1792]{1,0:T(8,128)(2,1)} %all-gather.4.cloned.1.call-done.other_ref.own_ref, ...), custom_call_target="tpu_custom_call" | custom-call | tf_op jit(solution)/shard_map/pallas_call | solution.py:511
  496.8 2.5 fusion.85
  504.4 4.1 add_convert_fusion.2
  511.6 10.4 %collective-permute-done.49 = bf16[128,1152]{1,0:T(8,128)(2,1)} collective-permute-done((bf16[128,1152]{1,0:T(8,128)(2,1)}, bf16[128,1152]{1,0:T(8,128)(2,1)}, u32[]{:S(2)}, u32[]{:S(2)}) %collective-permute-start.49) | collective-permute-done | bytes 294944 | tf_op jit(solution)/shard_map/ppermute | solution.py:77
  527.0 17.9 %shard_map.257 = (bf16[1152,896]{1,0:T(8,128)(2,1)}, bf16[1152,896]{1,0:T(8,128)(2,1)}) custom-call(bf16[1024,1152]{1,0:T(8,128)(2,1)} %shard_map.229.x_ref.refs_0_, bf16[1024,1152]{1,0:T(8,128)(2,1)} %shard_map.231.x_ref.other_ref.refs_1_, bf16[1024,3584]{1,0:T(8,128)(2,1)} %shard_map.254.refs_2_.value_ref, bf16[1024,3584]{1,0:T(8,128)(2,1)} %shard_map.256.refs_3_.value_ref), custom_call_target="tpu_custom_call" | custom-call | tf_op jit(solution)/shard_map/pallas_call | solution.py:552
  548.7 4.2 fusion.9.other_ref
  552.9 3.5 collective-permute-done.51
  561.6 3.4 add_convert_fusion.1
  566.8 3.1 multiply_reduce_fusion
  570.3 3.6 multiply_reduce_fusion.1
  576.4 2.5 convolution_convert_fusion.3.grad_ref
  578.9 19.1 %shard_map.264 = (f32[512,1024]{1,0:T(8,128)}, bf16[2048,512]{1,0:T(8,128)(2,1)}) custom-call(s32[2]{0:T(128)} %pad_add_fusion.2.info_ref, bf16[512,1024]{1,0:T(8,128)(2,1)} %bitcast.182, bf16[512,1024]{1,0:T(8,128)(2,1)} %convolution_convert_fusion.3.grad_ref, bf16[512,1024]{1,0:T(8,128)(2,1)} %get-tuple-element.54.mixed_ref, ...), custom_call_target="tpu_custom_call" | custom-call | tf_op jit(solution)/shard_map/pallas_call | solution.py:397
  601.0 3.2 mul.793
  606.6 2.8 multiply_reduce_fusion.9
  611.4 3.0 convolution_convert_fusion
  623.3 17.6 %shard_map.268 = (bf16[1152,896]{1,0:T(8,128)(2,1)}, bf16[1152,896]{1,0:T(8,128)(2,1)}) custom-call(bf16[1024,1152]{1,0:T(8,128)(2,1)} %shard_map.229.x_ref.refs_0_, bf16[1024,1152]{1,0:T(8,128)(2,1)} %shard_map.231.x_ref.other_ref.refs_1_, bf16[1024,3584]{1,0:T(8,128)(2,1)} %shard_map.266.refs_2_, bf16[1024,3584]{1,0:T(8,128)(2,1)} %shard_map.267.refs_3_), custom_call_target="tpu_custom_call" | custom-call | tf_op jit(solution)/shard_map/pallas_call | solution.py:552
  648.8 12.5 %collective-permute-done.59 = bf16[1152,256]{1,0:T(8,128)(2,1)S(1)} collective-permute-done((bf16[1152,256]{1,0:T(8,128)(2,1)S(1)}, bf16[1152,256]{1,0:T(8,128)(2,1)S(1)}, u32[]{:S(2)}, u32[]{:S(2)}) %collective-permute-start.59) | collective-permute-done | bytes 589856 | tf_op jit(solution)/shard_map/ppermute | solution.py:77
  665.7 4.7 collective-permute-done.60
  673.1 2.7 add_convert_fusion.other_ref
  677.1 6.2 reduce-scatter.10.cloned.1.call-done
  696.6 4.7 multiply_reduce_fusion.2
  706.2 2.6 collective-permute-start.62
  712.7 8.0 collective-permute-done.63
  729.2 5.8 fusion.10
  735.0 12.1 %collective-permute-start.72 = (f32[40,128]{1,0:T(8,128)S(1)}, f32[40,128]{1,0:T(8,128)S(1)}, u32[]{:S(2)}, u32[]{:S(2)}) collective-permute-start(f32[40,128]{1,0:T(8,128)S(1)} %add.602), channel_id=1, source_target_pairs={{3,0},{0,1},{1,2},{2,3},{7,4},{4,5},{5,6},{6,7},{11,8},{8,9},{9,10... | collective-permute-start | bytes 61448 | tf_op jit(solution)/shard_map/ppermute | solution.py:73
  749.4 3.4 all-to-all-start.1
  755.5 4.0 all-to-all-done.1
  759.5 3.6 all-to-all-start.2
  766.2 19.5 %all-to-all-done.2 = bf16[8,36,2688]{2,1,0:T(8,128)(2,1)S(1)} async-done(((bf16[8,36,2688]{2,1,0:T(8,128)(2,1)}), bf16[8,36,2688]{2,1,0:T(8,128)(2,1)S(1)}, u32[]{:S(2)}, u32[]{:S(2)}) %all-to-all-start.2) | async-done | bytes 1548320 | tf_op jit(solution)/shard_map/all_to_all | solution.py:695
  790.9 7.0 fusion.79
  (729 shorter events, 254.4 us)
Async XLA Ops:
  11.7 28.2 %all-to-all-start = ((bf16[8,36,2688]{2,1,0:T(8,128)(2,1)}), bf16[8,36,2688]{2,1,0:T(8,128)(2,1)}, u32[]{:S(2)}, u32[]{:S(2)}) async-start(bf16[8,36,2688]{2,1,0:T(8,128)(2,1)} %pad_maximum_fusion.5), calls=%async_computation | async-start | bytes 3440640 | tf_op jit(solution)/shard_map/all_to_all | solution.py:598
  17.1 147.8 %all-gather.4.cloned.1.call-start = ((), (), s32[]{:S(2)}) async-start(), calls=%async_computation.8 | async-start | bytes 5160960 | tf_op jit(solution)/shard_map/all_gather | solution.py:601
  24.7 12.9 %collective-permute-start.2 = (bf16[72,896]{1,0:T(8,128)(2,1)S(1)}, bf16[72,896]{1,0:T(8,128)(2,1)S(1)}, u32[]{:S(2)}, u32[]{:S(2)}) collective-permute-start(bf16[72,896]{1,0:T(8,128)(2,1)S(1)} %pad_maximum_fusion.33), channel_id=1, source_target_pairs={{2,0},{3,1},{0,2},{1,3},{6,4},{7,5},{4,6},{5,7},{10,8},{11,9},{8,1... | collective-permute-start | bytes 387080 | tf_op jit(solution)/shard_map/ppermute | solution.py:73
  27.8 9.8 %collective-permute-start.3 = (bf16[72,896]{1,0:T(8,128)(2,1)S(1)}, bf16[72,896]{1,0:T(8,128)(2,1)S(1)}, u32[]{:S(2)}, u32[]{:S(2)}) collective-permute-start(bf16[72,896]{1,0:T(8,128)(2,1)S(1)} %pad_maximum_fusion.33), channel_id=1, source_target_pairs={{3,0},{0,1},{1,2},{2,3},{7,4},{4,5},{5,6},{6,7},{11,8},{8,9},{9,10... | collective-permute-start | bytes 387080 | tf_op jit(solution)/shard_map/ppermute | solution.py:73
  46.8 9.6 %collective-permute-start.6 = (bf16[4,72,512]{2,1,0:T(8,128)(2,1)S(1)}, bf16[4,72,512]{2,1,0:T(8,128)(2,1)S(1)}, u32[]{:S(2)}, u32[]{:S(2)}) collective-permute-start(bf16[4,72,512]{2,1,0:T(8,128)(2,1)S(1)} %slice.357), channel_id=1, source_target_pairs={{16,0},{20,4},{24,8},{28,12},{0,16},{4,20},{8,24},{12,28},{17,1},{... | collective-permute-start | bytes 884744 | tf_op jit(solution)/shard_map/ppermute | solution.py:77
  51.8 12.3 %collective-permute-start.5 = (bf16[4,2,72,384]{3,2,0,1:T(8,128)(2,1)S(1)}, bf16[4,2,72,384]{3,2,0,1:T(8,128)(2,1)S(1)}, u32[]{:S(2)}, u32[]{:S(2)}) collective-permute-start(bf16[4,2,72,384]{3,2,0,1:T(8,128)(2,1)S(1)} %pad_maximum_fusion.28), channel_id=1, source_target_pairs={{16,0},{20,4},{24,8},{28,12},{0,16},{4,20},{8,24},{12,28},{17,1},{... | collective-permute-start | bytes 1327112 | tf_op jit(solution)/shard_map/ppermute | solution.py:77
  56.5 11.5 %collective-permute-start.7 = (bf16[4,2,72,512]{3,2,0,1:T(8,128)(2,1)S(1)}, bf16[4,2,72,512]{3,2,0,1:T(8,128)(2,1)S(1)}, u32[]{:S(2)}, u32[]{:S(2)}) collective-permute-start(bf16[4,2,72,512]{3,2,0,1:T(8,128)(2,1)S(1)} %pad_maximum_fusion.13), channel_id=1, source_target_pairs={{8,0},{12,4},{0,8},{4,12},{24,16},{28,20},{16,24},{20,28},{9,1},{1... | collective-permute-start | bytes 1769480 | tf_op jit(solution)/shard_map/ppermute | solution.py:77
  76.4 135.0 %all-gather.6.cloned.1.call-start = ((), (), s32[]{:S(2)}) async-start(), calls=%async_computation.9 | async-start | bytes 2621440 | tf_op jit(solution)/shard_map/all_gather | solution.py:639
  96.7 15.4 %collective-permute-start.11 = (bf16[72,512]{1,0:T(8,128)(2,1)S(1)}, bf16[72,512]{1,0:T(8,128)(2,1)S(1)}, u32[]{:S(2)}, u32[]{:S(2)}) collective-permute-start(bf16[72,512]{1,0:T(8,128)(2,1)S(1)} %pad_maximum_fusion.34), channel_id=1, source_target_pairs={{2,0},{3,1},{0,2},{1,3},{6,4},{7,5},{4,6},{5,7},{10,8},{11,9},{8,1... | collective-permute-start | bytes 221192 | tf_op jit(solution)/shard_map/ppermute | solution.py:73
  102.8 11.7 %collective-permute-start.10 = (bf16[72,512]{1,0:T(8,128)(2,1)S(1)}, bf16[72,512]{1,0:T(8,128)(2,1)S(1)}, u32[]{:S(2)}, u32[]{:S(2)}) collective-permute-start(bf16[72,512]{1,0:T(8,128)(2,1)S(1)} %pad_maximum_fusion.34), channel_id=1, source_target_pairs={{1,0},{2,1},{3,2},{0,3},{5,4},{6,5},{7,6},{4,7},{9,8},{10,9},{11,1... | collective-permute-start | bytes 221192 | tf_op jit(solution)/shard_map/ppermute | solution.py:73
  164.9 114.9 %all-gather.8.cloned.1.call-start = ((), (), s32[]{:S(2)}) async-start(), calls=%async_computation.10 | async-start | bytes 2580480 | tf_op jit(solution)/shard_map/all_gather | solution.py:640
  166.1 113.7 %collective-permute-start.24 = (bf16[1152,1792]{1,0:T(8,128)(2,1)}, bf16[1152,1792]{1,0:T(8,128)(2,1)}, u32[]{:S(2)}, u32[]{:S(2)}) collective-permute-start(bf16[1152,1792]{1,0:T(8,128)(2,1)} %all-gather.4.cloned.1.call-done.other_ref.own_ref), channel_id=1, source_target_pairs={{4,0},{0,4},{12,8},{8,12},{20,16},{16,20},{28,24},{24,28},{5,1},{1... | collective-permute-start | bytes 12386312 | tf_op jit(solution)/shard_map/ppermute | solution.py:77
  228.1 10.2 %collective-permute-start.18 = (bf16[128,1152]{1,0:T(8,128)(2,1)}, bf16[128,1152]{1,0:T(8,128)(2,1)}, u32[]{:S(2)}, u32[]{:S(2)}) collective-permute-start(bf16[128,1152]{1,0:T(8,128)(2,1)} %get-tuple-element.141), channel_id=1, source_target_pairs={{8,0},{12,4},{0,8},{4,12},{24,16},{28,20},{16,24},{20,28},{9,1},{1... | collective-permute-start | bytes 884744 | tf_op jit(solution)/shard_map/ppermute | solution.py:77
  229.5 13.9 %collective-permute-start.22 = (bf16[128,1152]{1,0:T(8,128)(2,1)}, bf16[128,1152]{1,0:T(8,128)(2,1)}, u32[]{:S(2)}, u32[]{:S(2)}) collective-permute-start(bf16[128,1152]{1,0:T(8,128)(2,1)} %get-tuple-element.140), channel_id=1, source_target_pairs={{8,0},{12,4},{0,8},{4,12},{24,16},{28,20},{16,24},{20,28},{9,1},{1... | collective-permute-start | bytes 884744 | tf_op jit(solution)/shard_map/ppermute | solution.py:77
  232.0 14.2 %collective-permute-start.20 = (bf16[128,1152]{1,0:T(8,128)(2,1)}, bf16[128,1152]{1,0:T(8,128)(2,1)}, u32[]{:S(2)}, u32[]{:S(2)}) collective-permute-start(bf16[128,1152]{1,0:T(8,128)(2,1)} %get-tuple-element.136), channel_id=1, source_target_pairs={{16,0},{20,4},{24,8},{28,12},{0,16},{4,20},{8,24},{12,28},{17,1},{... | collective-permute-start | bytes 884744 | tf_op jit(solution)/shard_map/ppermute | solution.py:77
  233.4 15.3 %collective-permute-start.23 = (bf16[128,1152]{1,0:T(8,128)(2,1)}, bf16[128,1152]{1,0:T(8,128)(2,1)}, u32[]{:S(2)}, u32[]{:S(2)}) collective-permute-start(bf16[128,1152]{1,0:T(8,128)(2,1)} %get-tuple-element.139), channel_id=1, source_target_pairs={{16,0},{20,4},{24,8},{28,12},{0,16},{4,20},{8,24},{12,28},{17,1},{... | collective-permute-start | bytes 884744 | tf_op jit(solution)/shard_map/ppermute | solution.py:77
  234.0 331.1 %reduce-scatter.6.cloned.1.call-start = ((), (), s32[]{:S(2)}) async-start(), calls=%async_computation.11 | async-start | bytes 2580480 | tf_op jit(solution)/shard_map/reduce_scatter | solution.py:692
  239.4 21.7 %collective-permute-start.19 = (bf16[256,1152]{1,0:T(8,128)(2,1)S(1)}, bf16[256,1152]{1,0:T(8,128)(2,1)S(1)}, u32[]{:S(2)}, u32[]{:S(2)}) collective-permute-start(bf16[256,1152]{1,0:T(8,128)(2,1)S(1)} %pad_maximum_fusion.16), channel_id=1, source_target_pairs={{16,0},{20,4},{24,8},{28,12},{0,16},{4,20},{8,24},{12,28},{17,1},{... | collective-permute-start | bytes 1769480 | tf_op jit(solution)/shard_map/ppermute | solution.py:77
  244.6 27.4 %collective-permute-start.25 = (bf16[256,1152]{1,0:T(8,128)(2,1)S(1)}, bf16[256,1152]{1,0:T(8,128)(2,1)S(1)}, u32[]{:S(2)}, u32[]{:S(2)}) collective-permute-start(bf16[256,1152]{1,0:T(8,128)(2,1)S(1)} %pad_maximum_fusion.18.other_ref), channel_id=1, source_target_pairs={{16,0},{20,4},{24,8},{28,12},{0,16},{4,20},{8,24},{12,28},{17,1},{... | collective-permute-start | bytes 1769480 | tf_op jit(solution)/shard_map/ppermute | solution.py:77
  247.2 27.4 %collective-permute-start.21 = (bf16[256,1152]{1,0:T(8,128)(2,1)S(1)}, bf16[256,1152]{1,0:T(8,128)(2,1)S(1)}, u32[]{:S(2)}, u32[]{:S(2)}) collective-permute-start(bf16[256,1152]{1,0:T(8,128)(2,1)S(1)} %pad_maximum_fusion.17), channel_id=1, source_target_pairs={{8,0},{12,4},{0,8},{4,12},{24,16},{28,20},{16,24},{20,28},{9,1},{1... | collective-permute-start | bytes 1769480 | tf_op jit(solution)/shard_map/ppermute | solution.py:77
  250.7 27.2 %collective-permute-start.26 = (bf16[256,1152]{1,0:T(8,128)(2,1)}, bf16[256,1152]{1,0:T(8,128)(2,1)}, u32[]{:S(2)}, u32[]{:S(2)}) collective-permute-start(bf16[256,1152]{1,0:T(8,128)(2,1)} %pad_maximum_fusion.19.other_ref), channel_id=1, source_target_pairs={{8,0},{12,4},{0,8},{4,12},{24,16},{28,20},{16,24},{20,28},{9,1},{1... | collective-permute-start | bytes 1769480 | tf_op jit(solution)/shard_map/ppermute | solution.py:77
  296.2 16.2 %collective-permute-start.27 = (bf16[1152,896]{1,0:T(8,128)(2,1)}, bf16[1152,896]{1,0:T(8,128)(2,1)S(1)}, u32[]{:S(2)}, u32[]{:S(2)}) collective-permute-start(bf16[1152,896]{1,0:T(8,128)(2,1)} %shard_map.234.own_ref.own_down_ref), channel_id=1, source_target_pairs={{4,0},{0,4},{12,8},{8,12},{20,16},{16,20},{28,24},{24,28},{5,1},{1... | collective-permute-start | bytes 6193160 | tf_op jit(solution)/shard_map/ppermute | solution.py:77
  324.7 15.9 %collective-permute-start.28 = (bf16[256,1152]{1,0:T(8,128)(2,1)S(1)}, bf16[256,1152]{1,0:T(8,128)(2,1)}, u32[]{:S(2)}, u32[]{:S(2)}) collective-permute-start(bf16[256,1152]{1,0:T(8,128)(2,1)S(1)} %get-tuple-element.126.other_ref), channel_id=1, source_target_pairs={{16,0},{20,4},{24,8},{28,12},{0,16},{4,20},{8,24},{12,28},{17,1},{... | collective-permute-start | bytes 1769480 | tf_op jit(solution)/shard_map/ppermute | solution.py:77
  326.2 15.5 %collective-permute-start.30 = (bf16[256,1152]{1,0:T(8,128)(2,1)S(1)}, bf16[256,1152]{1,0:T(8,128)(2,1)}, u32[]{:S(2)}, u32[]{:S(2)}) collective-permute-start(bf16[256,1152]{1,0:T(8,128)(2,1)S(1)} %get-tuple-element.125.other_ref), channel_id=1, source_target_pairs={{8,0},{12,4},{0,8},{4,12},{24,16},{28,20},{16,24},{20,28},{9,1},{1... | collective-permute-start | bytes 1769480 | tf_op jit(solution)/shard_map/ppermute | solution.py:77
  343.6 10.0 %collective-permute-start.31 = (bf16[128,1152]{1,0:T(8,128)(2,1)S(1)}, bf16[128,1152]{1,0:T(8,128)(2,1)S(1)}, u32[]{:S(2)}, u32[]{:S(2)}) collective-permute-start(bf16[128,1152]{1,0:T(8,128)(2,1)S(1)} %slice.626), channel_id=1, source_target_pairs={{16,0},{20,4},{24,8},{28,12},{0,16},{4,20},{8,24},{12,28},{17,1},{... | collective-permute-start | bytes 884744 | tf_op jit(solution)/shard_map/ppermute | solution.py:77
  344.4 26.3 %collective-permute-start.32 = (bf16[256,1152]{1,0:T(8,128)(2,1)S(1)}, bf16[256,1152]{1,0:T(8,128)(2,1)S(1)}, u32[]{:S(2)}, u32[]{:S(2)}) collective-permute-start(bf16[256,1152]{1,0:T(8,128)(2,1)S(1)} %get-tuple-element.121), channel_id=1, source_target_pairs={{16,0},{20,4},{24,8},{28,12},{0,16},{4,20},{8,24},{12,28},{17,1},{... | collective-permute-start | bytes 1769480 | tf_op jit(solution)/shard_map/ppermute | solution.py:77
  345.9 24.7 %collective-permute-start.35 = (bf16[256,1152]{1,0:T(8,128)(2,1)S(1)}, bf16[256,1152]{1,0:T(8,128)(2,1)S(1)}, u32[]{:S(2)}, u32[]{:S(2)}) collective-permute-start(bf16[256,1152]{1,0:T(8,128)(2,1)S(1)} %get-tuple-element.122), channel_id=1, source_target_pairs={{8,0},{12,4},{0,8},{4,12},{24,16},{28,20},{16,24},{20,28},{9,1},{1... | collective-permute-start | bytes 1769480 | tf_op jit(solution)/shard_map/ppermute | solution.py:77
  347.4 18.9 %collective-permute-start.29 = (bf16[128,1152]{1,0:T(8,128)(2,1)S(1)}, bf16[128,1152]{1,0:T(8,128)(2,1)S(1)}, u32[]{:S(2)}, u32[]{:S(2)}) collective-permute-start(bf16[128,1152]{1,0:T(8,128)(2,1)S(1)} %slice.627), channel_id=1, source_target_pairs={{8,0},{12,4},{0,8},{4,12},{24,16},{28,20},{16,24},{20,28},{9,1},{1... | collective-permute-start | bytes 884744 | tf_op jit(solution)/shard_map/ppermute | solution.py:77
  370.0 10.4 %collective-permute-start.38 = (bf16[128,1152]{1,0:T(8,128)(2,1)}, bf16[128,1152]{1,0:T(8,128)(2,1)}, u32[]{:S(2)}, u32[]{:S(2)}) collective-permute-start(bf16[128,1152]{1,0:T(8,128)(2,1)} %get-tuple-element.157), channel_id=1, source_target_pairs={{16,0},{20,4},{24,8},{28,12},{0,16},{4,20},{8,24},{12,28},{17,1},{... | collective-permute-start | bytes 884744 | tf_op jit(solution)/shard_map/ppermute | solution.py:77
  377.0 25.5 %collective-permute-start.37 = (bf16[256,1152]{1,0:T(8,128)(2,1)}, bf16[256,1152]{1,0:T(8,128)(2,1)}, u32[]{:S(2)}, u32[]{:S(2)}) collective-permute-start(bf16[256,1152]{1,0:T(8,128)(2,1)} %pad_maximum_fusion.20.other_ref), channel_id=1, source_target_pairs={{16,0},{20,4},{24,8},{28,12},{0,16},{4,20},{8,24},{12,28},{17,1},{... | collective-permute-start | bytes 1769480 | tf_op jit(solution)/shard_map/ppermute | solution.py:77
  377.6 18.4 %collective-permute-start.36 = (bf16[128,1152]{1,0:T(8,128)(2,1)}, bf16[128,1152]{1,0:T(8,128)(2,1)}, u32[]{:S(2)}, u32[]{:S(2)}) collective-permute-start(bf16[128,1152]{1,0:T(8,128)(2,1)} %shard_map.240), channel_id=1, source_target_pairs={{16,0},{20,4},{24,8},{28,12},{0,16},{4,20},{8,24},{12,28},{17,1},{... | collective-permute-start | bytes 884744 | tf_op jit(solution)/shard_map/ppermute | solution.py:77
  379.0 18.2 %collective-permute-start.34 = (bf16[128,1152]{1,0:T(8,128)(2,1)}, bf16[128,1152]{1,0:T(8,128)(2,1)S(1)}, u32[]{:S(2)}, u32[]{:S(2)}) collective-permute-start(bf16[128,1152]{1,0:T(8,128)(2,1)} %shard_map.239), channel_id=1, source_target_pairs={{8,0},{12,4},{0,8},{4,12},{24,16},{28,20},{16,24},{20,28},{9,1},{1... | collective-permute-start | bytes 884744 | tf_op jit(solution)/shard_map/ppermute | solution.py:77
  381.5 27.6 %collective-permute-start.39 = (bf16[256,1152]{1,0:T(8,128)(2,1)S(1)}, bf16[256,1152]{1,0:T(8,128)(2,1)S(1)}, u32[]{:S(2)}, u32[]{:S(2)}) collective-permute-start(bf16[256,1152]{1,0:T(8,128)(2,1)S(1)} %pad_maximum_fusion.21), channel_id=1, source_target_pairs={{8,0},{12,4},{0,8},{4,12},{24,16},{28,20},{16,24},{20,28},{9,1},{1... | collective-permute-start | bytes 1769480 | tf_op jit(solution)/shard_map/ppermute | solution.py:77
  412.5 31.5 %collective-permute-start.43 = (bf16[256,1152]{1,0:T(8,128)(2,1)}, bf16[256,1152]{1,0:T(8,128)(2,1)S(1)}, u32[]{:S(2)}, u32[]{:S(2)}) collective-permute-start(bf16[256,1152]{1,0:T(8,128)(2,1)} %shard_map.243.other_ref), channel_id=1, source_target_pairs={{8,0},{12,4},{0,8},{4,12},{24,16},{28,20},{16,24},{20,28},{9,1},{1... | collective-permute-start | bytes 1769480 | tf_op jit(solution)/shard_map/ppermute | solution.py:77
  413.8 30.2 %collective-permute-start.42 = (bf16[256,1152]{1,0:T(8,128)(2,1)}, bf16[256,1152]{1,0:T(8,128)(2,1)S(1)}, u32[]{:S(2)}, u32[]{:S(2)}) collective-permute-start(bf16[256,1152]{1,0:T(8,128)(2,1)} %shard_map.241.other_ref), channel_id=1, source_target_pairs={{16,0},{20,4},{24,8},{28,12},{0,16},{4,20},{8,24},{12,28},{17,1},{... | collective-permute-start | bytes 1769480 | tf_op jit(solution)/shard_map/ppermute | solution.py:77
  467.6 36.7 %collective-permute-start.52 = (bf16[1152,896]{1,0:T(8,128)(2,1)}, bf16[1152,896]{1,0:T(8,128)(2,1)}, u32[]{:S(2)}, u32[]{:S(2)}) collective-permute-start(bf16[1152,896]{1,0:T(8,128)(2,1)} %get-tuple-element.65), channel_id=1, source_target_pairs={{4,0},{0,4},{12,8},{8,12},{20,16},{16,20},{28,24},{24,28},{5,1},{1... | collective-permute-start | bytes 6193160 | tf_op jit(solution)/shard_map/ppermute | solution.py:77
  467.6 33.6 %collective-permute-start.46 = (bf16[256,1152]{1,0:T(8,128)(2,1)S(1)}, bf16[256,1152]{1,0:T(8,128)(2,1)S(1)}, u32[]{:S(2)}, u32[]{:S(2)}) collective-permute-start(bf16[256,1152]{1,0:T(8,128)(2,1)S(1)} %copy-done.41), channel_id=1, source_target_pairs={{16,0},{20,4},{24,8},{28,12},{0,16},{4,20},{8,24},{12,28},{17,1},{... | collective-permute-start | bytes 1769480 | tf_op jit(solution)/shard_map/ppermute | solution.py:77
  469.1 32.2 %collective-permute-start.48 = (bf16[256,1152]{1,0:T(8,128)(2,1)S(1)}, bf16[256,1152]{1,0:T(8,128)(2,1)S(1)}, u32[]{:S(2)}, u32[]{:S(2)}) collective-permute-start(bf16[256,1152]{1,0:T(8,128)(2,1)S(1)} %copy-done.40), channel_id=1, source_target_pairs={{8,0},{12,4},{0,8},{4,12},{24,16},{28,20},{16,24},{20,28},{9,1},{1... | collective-permute-start | bytes 1769480 | tf_op jit(solution)/shard_map/ppermute | solution.py:77
  499.3 24.5 %collective-permute-start.45 = (bf16[256,1152]{1,0:T(8,128)(2,1)}, bf16[256,1152]{1,0:T(8,128)(2,1)}, u32[]{:S(2)}, u32[]{:S(2)}) collective-permute-start(bf16[256,1152]{1,0:T(8,128)(2,1)} %get-tuple-element.115), channel_id=1, source_target_pairs={{8,0},{12,4},{0,8},{4,12},{24,16},{28,20},{16,24},{20,28},{9,1},{1... | collective-permute-start | bytes 1769480 | tf_op jit(solution)/shard_map/ppermute | solution.py:77
  500.5 23.3 %collective-permute-start.44 = (bf16[256,1152]{1,0:T(8,128)(2,1)}, bf16[256,1152]{1,0:T(8,128)(2,1)}, u32[]{:S(2)}, u32[]{:S(2)}) collective-permute-start(bf16[256,1152]{1,0:T(8,128)(2,1)} %get-tuple-element.116), channel_id=1, source_target_pairs={{16,0},{20,4},{24,8},{28,12},{0,16},{4,20},{8,24},{12,28},{17,1},{... | collective-permute-start | bytes 1769480 | tf_op jit(solution)/shard_map/ppermute | solution.py:77
  502.3 19.7 %collective-permute-start.49 = (bf16[128,1152]{1,0:T(8,128)(2,1)}, bf16[128,1152]{1,0:T(8,128)(2,1)}, u32[]{:S(2)}, u32[]{:S(2)}) collective-permute-start(bf16[128,1152]{1,0:T(8,128)(2,1)} %slice.620.other_ref), channel_id=1, source_target_pairs={{16,0},{20,4},{24,8},{28,12},{0,16},{4,20},{8,24},{12,28},{17,1},{... | collective-permute-start | bytes 884744 | tf_op jit(solution)/shard_map/ppermute | solution.py:77
  508.5 133.6 %reduce-scatter.8.cloned.1.call-start = ((), (), s32[]{:S(2)}) async-start(), calls=%async_computation.12 | async-start | bytes 2580480 | tf_op jit(solution)/shard_map/reduce_scatter | solution.py:692
  510.8 34.1 %collective-permute-start.47 = (bf16[128,1152]{1,0:T(8,128)(2,1)}, bf16[128,1152]{1,0:T(8,128)(2,1)}, u32[]{:S(2)}, u32[]{:S(2)}) collective-permute-start(bf16[128,1152]{1,0:T(8,128)(2,1)} %slice.621.other_ref), channel_id=1, source_target_pairs={{8,0},{12,4},{0,8},{4,12},{24,16},{28,20},{16,24},{20,28},{9,1},{1... | collective-permute-start | bytes 884744 | tf_op jit(solution)/shard_map/ppermute | solution.py:77
  544.8 15.2 %collective-permute-start.53 = (bf16[1152,896]{1,0:T(8,128)(2,1)}, bf16[1152,896]{1,0:T(8,128)(2,1)}, u32[]{:S(2)}, u32[]{:S(2)}) collective-permute-start(bf16[1152,896]{1,0:T(8,128)(2,1)} %get-tuple-element.69), channel_id=1, source_target_pairs={{4,0},{0,4},{12,8},{8,12},{20,16},{16,20},{28,24},{24,28},{5,1},{1... | collective-permute-start | bytes 6193160 | tf_op jit(solution)/shard_map/ppermute | solution.py:77
  546.7 9.7 %collective-permute-start.51 = (bf16[128,1152]{1,0:T(8,128)(2,1)}, bf16[128,1152]{1,0:T(8,128)(2,1)}, u32[]{:S(2)}, u32[]{:S(2)}) collective-permute-start(bf16[128,1152]{1,0:T(8,128)(2,1)} %slice.622.other_ref), channel_id=1, source_target_pairs={{16,0},{20,4},{24,8},{28,12},{0,16},{4,20},{8,24},{12,28},{17,1},{... | collective-permute-start | bytes 884744 | tf_op jit(solution)/shard_map/ppermute | solution.py:77
  547.3 10.1 %collective-permute-start.50 = (bf16[128,1152]{1,0:T(8,128)(2,1)}, bf16[128,1152]{1,0:T(8,128)(2,1)}, u32[]{:S(2)}, u32[]{:S(2)}) collective-permute-start(bf16[128,1152]{1,0:T(8,128)(2,1)} %slice.623.other_ref), channel_id=1, source_target_pairs={{8,0},{12,4},{0,8},{4,12},{24,16},{28,20},{16,24},{20,28},{9,1},{1... | collective-permute-start | bytes 884744 | tf_op jit(solution)/shard_map/ppermute | solution.py:77
  565.0 118.3 %reduce-scatter.10.cloned.1.call-start = ((), (), s32[]{:S(2)}) async-start(), calls=%async_computation.13 | async-start | bytes 2621440 | tf_op jit(solution)/shard_map/reduce_scatter | solution.py:726
  615.6 26.6 %collective-permute-start.58 = (bf16[1152,512]{1,0:T(8,128)(2,1)}, bf16[1152,512]{1,0:T(8,128)(2,1)}, u32[]{:S(2)}, u32[]{:S(2)}) collective-permute-start(bf16[1152,512]{1,0:T(8,128)(2,1)} %constant_dynamic-slice_fusion.5), channel_id=1, source_target_pairs={{4,0},{0,4},{12,8},{8,12},{20,16},{16,20},{28,24},{24,28},{5,1},{1... | collective-permute-start | bytes 3538952 | tf_op jit(solution)/shard_map/ppermute | solution.py:77
  622.6 23.3 %collective-permute-start.55 = (bf16[1152,512]{1,0:T(8,128)(2,1)S(1)}, bf16[1152,512]{1,0:T(8,128)(2,1)}, u32[]{:S(2)}, u32[]{:S(2)}) collective-permute-start(bf16[1152,512]{1,0:T(8,128)(2,1)S(1)} %constant_dynamic-slice_fusion.8), channel_id=1, source_target_pairs={{4,0},{0,4},{12,8},{8,12},{20,16},{16,20},{28,24},{24,28},{5,1},{1... | collective-permute-start | bytes 3538952 | tf_op jit(solution)/shard_map/ppermute | solution.py:77
  640.9 32.2 %collective-permute-start.54 = (bf16[1152,896]{1,0:T(8,128)(2,1)}, bf16[1152,896]{1,0:T(8,128)(2,1)}, u32[]{:S(2)}, u32[]{:S(2)}) collective-permute-start(bf16[1152,896]{1,0:T(8,128)(2,1)} %get-tuple-element.71), channel_id=1, source_target_pairs={{4,0},{0,4},{12,8},{8,12},{20,16},{16,20},{28,24},{24,28},{5,1},{1... | collective-permute-start | bytes 6193160 | tf_op jit(solution)/shard_map/ppermute | solution.py:77
  642.1 79.3 %reduce-scatter.12.cloned.1.call-start = ((), (), s32[]{:S(2)}) async-start(), calls=%async_computation.14 | async-start | bytes 737280 | tf_op jit(solution)/shard_map/reduce_scatter | solution.py:692
  645.5 15.8 %collective-permute-start.59 = (bf16[1152,256]{1,0:T(8,128)(2,1)S(1)}, bf16[1152,256]{1,0:T(8,128)(2,1)S(1)}, u32[]{:S(2)}, u32[]{:S(2)}) collective-permute-start(bf16[1152,256]{1,0:T(8,128)(2,1)S(1)} %constant_dynamic-slice_fusion.4), channel_id=1, source_target_pairs={{16,0},{20,4},{24,8},{28,12},{0,16},{4,20},{8,24},{12,28},{17,1},{... | collective-permute-start | bytes 1769480 | tf_op jit(solution)/shard_map/ppermute | solution.py:77
  647.7 15.5 %collective-permute-start.56 = (bf16[1152,256]{1,0:T(8,128)(2,1)S(1)}, bf16[1152,256]{1,0:T(8,128)(2,1)S(1)}, u32[]{:S(2)}, u32[]{:S(2)}) collective-permute-start(bf16[1152,256]{1,0:T(8,128)(2,1)S(1)} %constant_dynamic-slice_fusion.7), channel_id=1, source_target_pairs={{8,0},{12,4},{0,8},{4,12},{24,16},{28,20},{16,24},{20,28},{9,1},{1... | collective-permute-start | bytes 1769480 | tf_op jit(solution)/shard_map/ppermute | solution.py:77
  673.0 79.9 %reduce-scatter.14.cloned.1.call-start = ((), (), s32[]{:S(2)}) async-start(), calls=%async_computation.15 | async-start | bytes 2580480 | tf_op jit(solution)/shard_map/reduce_scatter | solution.py:692
  704.1 16.5 %collective-permute-start.63 = (bf16[288,256]{1,0:T(8,128)(2,1)S(1)}, bf16[288,256]{1,0:T(8,128)(2,1)S(1)}, u32[]{:S(2)}, u32[]{:S(2)}) collective-permute-start(bf16[288,256]{1,0:T(8,128)(2,1)S(1)} %get-tuple-element.154), channel_id=1, source_target_pairs={{2,0},{3,1},{0,2},{1,3},{6,4},{7,5},{4,6},{5,7},{10,8},{11,9},{8,1... | collective-permute-start | bytes 442376 | tf_op jit(solution)/shard_map/ppermute | solution.py:73
  706.2 14.5 %collective-permute-start.62 = (bf16[288,256]{1,0:T(8,128)(2,1)S(1)}, bf16[288,256]{1,0:T(8,128)(2,1)S(1)}, u32[]{:S(2)}, u32[]{:S(2)}) collective-permute-start(bf16[288,256]{1,0:T(8,128)(2,1)S(1)} %get-tuple-element.152), channel_id=1, source_target_pairs={{1,0},{2,1},{3,2},{0,3},{5,4},{6,5},{7,6},{4,7},{9,8},{10,9},{11,1... | collective-permute-start | bytes 442376 | tf_op jit(solution)/shard_map/ppermute | solution.py:73
  709.5 14.3 %collective-permute-start.68 = (f32[40,128]{1,0:T(8,128)S(1)}, f32[40,128]{1,0:T(8,128)S(1)}, u32[]{:S(2)}, u32[]{:S(2)}) collective-permute-start(f32[40,128]{1,0:T(8,128)S(1)} %fusion.111), channel_id=1, source_target_pairs={{16,0},{20,4},{24,8},{28,12},{0,16},{4,20},{8,24},{12,28},{17,1},{... | collective-permute-start | bytes 61448 | tf_op jit(solution)/shard_map/ppermute | solution.py:77
  724.6 10.4 %collective-permute-start.69 = (f32[40,128]{1,0:T(8,128)S(1)}, f32[40,128]{1,0:T(8,128)S(1)}, u32[]{:S(2)}, u32[]{:S(2)}) collective-permute-start(f32[40,128]{1,0:T(8,128)S(1)} %fusion.112), channel_id=1, source_target_pairs={{8,0},{12,4},{0,8},{4,12},{24,16},{28,20},{16,24},{20,28},{9,1},{1... | collective-permute-start | bytes 61448 | tf_op jit(solution)/shard_map/ppermute | solution.py:77
  727.6 21.0 %collective-permute-start.66 = (bf16[288,128]{1,0:T(8,128)(2,1)S(1)}, bf16[288,128]{1,0:T(8,128)(2,1)S(1)}, u32[]{:S(2)}, u32[]{:S(2)}) collective-permute-start(bf16[288,128]{1,0:T(8,128)(2,1)S(1)} %add_convert_fusion.11), channel_id=1, source_target_pairs={{8,0},{12,4},{0,8},{4,12},{24,16},{28,20},{16,24},{20,28},{9,1},{1... | collective-permute-start | bytes 221192 | tf_op jit(solution)/shard_map/ppermute | solution.py:77
  735.0 28.1 %collective-permute-start.72 = (f32[40,128]{1,0:T(8,128)S(1)}, f32[40,128]{1,0:T(8,128)S(1)}, u32[]{:S(2)}, u32[]{:S(2)}) collective-permute-start(f32[40,128]{1,0:T(8,128)S(1)} %add.602), channel_id=1, source_target_pairs={{3,0},{0,1},{1,2},{2,3},{7,4},{4,5},{5,6},{6,7},{11,8},{8,9},{9,10... | collective-permute-start | bytes 61448 | tf_op jit(solution)/shard_map/ppermute | solution.py:73
  747.1 16.1 %collective-permute-start.70 = (f32[40,128]{1,0:T(8,128)S(1)}, f32[40,128]{1,0:T(8,128)S(1)}, u32[]{:S(2)}, u32[]{:S(2)}) collective-permute-start(f32[40,128]{1,0:T(8,128)S(1)} %add.602), channel_id=1, source_target_pairs={{1,0},{2,1},{3,2},{0,3},{5,4},{6,5},{7,6},{4,7},{9,8},{10,9},{11,1... | collective-permute-start | bytes 61448 | tf_op jit(solution)/shard_map/ppermute | solution.py:73
  747.7 15.5 %collective-permute-start.71 = (f32[40,128]{1,0:T(8,128)S(1)}, f32[40,128]{1,0:T(8,128)S(1)}, u32[]{:S(2)}, u32[]{:S(2)}) collective-permute-start(f32[40,128]{1,0:T(8,128)S(1)} %add.602), channel_id=1, source_target_pairs={{2,0},{3,1},{0,2},{1,3},{6,4},{7,5},{4,6},{5,7},{10,8},{11,9},{8,1... | collective-permute-start | bytes 61448 | tf_op jit(solution)/shard_map/ppermute | solution.py:73
  749.4 10.1 %all-to-all-start.1 = ((bf16[8,36,384]{2,1,0:T(8,128)(2,1)}), bf16[8,36,384]{2,1,0:T(8,128)(2,1)S(1)}, u32[]{:S(2)}, u32[]{:S(2)}) async-start(bf16[8,36,384]{2,1,0:T(8,128)(2,1)} %reshape.527), calls=%async_computation.5 | async-start | bytes 491520 | tf_op jit(solution)/shard_map/all_to_all | solution.py:695
  759.5 26.1 %all-to-all-start.2 = ((bf16[8,36,2688]{2,1,0:T(8,128)(2,1)}), bf16[8,36,2688]{2,1,0:T(8,128)(2,1)S(1)}, u32[]{:S(2)}, u32[]{:S(2)}) async-start(bf16[8,36,2688]{2,1,0:T(8,128)(2,1)} %reshape.529), calls=%async_computation.7 | async-start | bytes 3440640 | tf_op jit(solution)/shard_map/all_to_all | solution.py:695
  (166 other events, 1212.3 us)
Sparse Core Ops, SparseCore 0:
  76.5 88.2 all-gather.3
  167.0 44.3 all-gather.5
  234.1 43.9 all-gather.7
  508.6 40.5 reduce-scatter.5
  565.1 40.6 reduce-scatter.7
  642.2 41.0 reduce-scatter.9
  685.7 21.2 reduce-scatter.11
  709.5 43.3 reduce-scatter.13
